TPU v7x, 128 devices: a whole 4x4x4 slice. The times are simulated.
128 devices in a mesh: experts: 16 (over x, z), context: 4 (over y), dp: 2 (over core).
Axes of the slice: x: 4, y: 4, z: 4, core: 2. Of those that a mesh axis runs over, the one named last changes fastest.
Arguments:
- tokens: bfloat16 [2, 32, 256, 2048], P(None, ('experts', 'dp'), 'context'), may hold values from -6 to 6
- lengths: int32 [2, 32], P(None, ('experts', 'dp')), may hold values from 64 to 256, as said below
- routes: int32 [2, 32, 256, 8], P(None, ('experts', 'dp'), 'context'), may hold values from 0 to 15, all different within a row; in each aligned block of 64 rows (0 to 63, 64 to 127, ..., all dimensions but the last counted through in order) at most 33 rows name the same one
- mix_weights: float32 [2, 32, 256, 8], P(None, ('experts', 'dp'), 'context'), may hold values from 0.06 to 0.25
- cotangent: bfloat16 [2, 32, 256, 2048], P(None, ('experts', 'dp'), 'context'), may hold values from -6 to 6
- w_query: bfloat16 [2048, 4096], P('experts'), may hold values from -0.125 to 0.125
- key_weight: bfloat16 [2048, 512], P('experts'), may hold values from -0.125 to 0.125
- value_weight: bfloat16 [2048, 512], P('experts'), may hold values from -0.125 to 0.125
- w_out: bfloat16 [4096, 2048], P('experts'), may hold values from -0.375 to 0.375
- norm_attn: bfloat16 [2048], P('experts'), may hold values from 0.5 to 1.5
- norm_moe: bfloat16 [2048], P('experts'), may hold values from 0.5 to 1.5
- norm_query: bfloat16 [128], P('experts'), may hold values from 0.5 to 1.5
- norm_key: bfloat16 [128], P('experts'), may hold values from 0.5 to 1.5
- w_gate: bfloat16 [16, 2048, 768], P('experts'), may hold values from -0.125 to 0.125
- w_up: bfloat16 [16, 2048, 768], P('experts'), may hold values from -0.125 to 0.125
- w_down: bfloat16 [16, 768, 2048], P('experts'), may hold values from -0.4375 to 0.4375
Outputs:
- output: bfloat16 [2, 32, 256, 2048], P(None, ('experts', 'dp'), 'context')
- input_grad: float32 [2, 32, 256, 2048], P(None, ('experts', 'dp'), 'context')
- grad_w_query: float32 [2048, 4096], P('experts')
- grad_w_key: float32 [2048, 512], P('experts')
- grad_w_value: float32 [2048, 512], P('experts')
- grad_w_out: float32 [4096, 2048], P('experts')
- grad_norm_attn: float32 [2048], P('experts')
- grad_norm_moe: float32 [2048], P('experts')
- grad_norm_query: float32 [128], P('experts')
- grad_norm_key: float32 [128], P('experts')
- grad_w_gate: float32 [16, 2048, 768], P('experts')
- grad_w_up: float32 [16, 2048, 768], P('experts')
- grad_w_down: float32 [16, 768, 2048], P('experts')
Inputs may be any that keep to these rules, and one draw needn't show every extreme that they name: `routes`: each row names 8 distinct experts; in each aligned block of 64 rows (leading dimensions taken together in order) no expert is named by more than 33 rows. `lengths`: for every slot index, one of its 2 micro-batches, drawn from the seed, is full.
All inputs are finite; a program needn't handle non-finite values.
Results may differ from a plain program's by a relative error of at most 0.035.
Values may be sent and summed in bfloat16 or wider, within the bound.
No kernel may reach another device: no remote copies, remote signals or barrier semaphores. Data moves between devices by JAX's collectives and lax.ppermute only.
A program may use at most 320 MiB of HBM per device.

v0:
```python
import jax
import jax.numpy as jnp
from jax import lax
from jax.sharding import PartitionSpec as P

EPS = 1e-06
ROPE_BASE = 1000000.0


def angles(positions, head_size):
    half_size = head_size // 2
    frequency = ROPE_BASE ** (-jnp.arange(half_size, dtype=jnp.float32) * 2.0 / head_size)
    phase_angle = positions.astype(jnp.float32)[:, None] * frequency[None, :]
    return (jnp.cos(phase_angle), jnp.sin(phase_angle))


def apply_rotation(value_matrix, cosine_table, sine_values):
    half_size = value_matrix.shape[-1] // 2
    first_half = value_matrix[..., :half_size]
    second = value_matrix[..., half_size:]
    cos_rows = cosine_table[:, None, :]
    sin_rows = sine_values[:, None, :]
    return jnp.concatenate(
        [first_half * cos_rows - second * sin_rows, second * cos_rows + first_half * sin_rows],
        axis=-1,
    )


def inverse_rms(value_matrix):
    return lax.rsqrt(jnp.mean(value_matrix * value_matrix, axis=-1, keepdims=True) + EPS)


def norm_back(grad_in, value_matrix, inverse, gain):
    scaled = grad_in * gain
    return inverse * scaled - value_matrix * inverse**3 * jnp.mean(
        scaled * value_matrix, axis=-1, keepdims=True
    )


def outer(left, right):
    return lax.dot_general(
        left, right, (((0,), (0,)), ((), ())), preferred_element_type=jnp.float32
    )


def against(left, right):
    return lax.dot_general(
        left, right, (((1,), (1,)), ((), ())), preferred_element_type=jnp.float32
    )


def masked_logits(grouped_queries, key_matrix, allowed, score_scale):
    logits = (
        jnp.einsum(
            "qhgd,khd->hgqk", grouped_queries, key_matrix, preferred_element_type=jnp.float32
        )
        * score_scale
    )
    return jnp.where(allowed[None, None], logits, -1e30)


def local(
    tokens,
    lengths,
    routes,
    mix_weights,
    cotangent,
    w_query,
    key_weight,
    value_weight,
    w_out,
    norm_attn,
    norm_moe,
    norm_query,
    norm_key,
    w_gate,
    w_up,
    w_down,
):
    gathered = (
        lax.all_gather(w_query, "experts", axis=0, tiled=True),
        lax.all_gather(key_weight, "experts", axis=0, tiled=True),
        lax.all_gather(value_weight, "experts", axis=0, tiled=True),
        lax.all_gather(w_out, "experts", axis=0, tiled=True),
        lax.all_gather(norm_attn, "experts", axis=0, tiled=True),
        lax.all_gather(norm_moe, "experts", axis=0, tiled=True),
        lax.all_gather(norm_query, "experts", axis=0, tiled=True),
        lax.all_gather(norm_key, "experts", axis=0, tiled=True),
    )
    query_w, key_w, value_w, out_w = (gathered[0], gathered[1], gathered[2], gathered[3])
    gain_attn = gathered[4].astype(jnp.float32)
    gain_moe = gathered[5].astype(jnp.float32)
    gain_query = gathered[6].astype(jnp.float32)
    key_gain = gathered[7].astype(jnp.float32)
    micro_count = tokens.shape[0]
    row_count = tokens.shape[2]
    model_width = tokens.shape[3]
    top_count = routes.shape[3]
    head_size = gain_query.shape[0]
    query_heads = query_w.shape[1] // head_size
    key_heads = key_w.shape[1] // head_size
    group_size = query_heads // key_heads
    local_experts = w_gate.shape[0]
    owner_count = lax.axis_size("experts")
    expert_total = owner_count * local_experts
    room_size = min(row_count, (row_count * top_count + expert_total - 1) // expert_total + 1)
    seq_total = lax.axis_size("context") * row_count
    query_pos = lax.axis_index("context") * row_count + jnp.arange(row_count, dtype=jnp.int32)
    key_pos = jnp.arange(seq_total, dtype=jnp.int32)
    cosine_table, sine_values = angles(query_pos, head_size)
    score_scale = head_size ** (-0.5)
    expert_ids = jnp.arange(expert_total, dtype=jnp.int32)
    buffer_shape = (expert_total * room_size, model_width)
    send_shape = (owner_count, local_experts * room_size, model_width)
    arrive_shape = (owner_count, local_experts, room_size, model_width)
    saved = []
    outputs = []
    for micro_step in range(micro_count):
        resid_in = tokens[micro_step, 0].astype(jnp.float32)
        inverse_in = inverse_rms(resid_in)
        normed_in = (resid_in * inverse_in * gain_attn).astype(jnp.bfloat16)
        query_pre = jnp.dot(normed_in, query_w, preferred_element_type=jnp.float32).reshape(
            row_count, query_heads, head_size
        )
        key_unrotated = jnp.dot(normed_in, key_w, preferred_element_type=jnp.float32).reshape(
            row_count, key_heads, head_size
        )
        value_projected = jnp.dot(normed_in, value_w, preferred_element_type=jnp.float32)
        inverse_query = inverse_rms(query_pre)
        inverse_key = inverse_rms(key_unrotated)
        query_rows = apply_rotation(
            query_pre * inverse_query * gain_query, cosine_table, sine_values
        ).astype(jnp.bfloat16)
        key_local = apply_rotation(
            key_unrotated * inverse_key * key_gain, cosine_table, sine_values
        ).astype(jnp.bfloat16)
        value_local = value_projected.reshape(row_count, key_heads, head_size).astype(jnp.bfloat16)
        key_matrix, value_rows = (
            lax.all_gather(key_local, "context", axis=0, tiled=True),
            lax.all_gather(value_local, "context", axis=0, tiled=True),
        )
        allowed = (key_pos[None, :] <= query_pos[:, None]) & (
            key_pos[None, :] < lengths[micro_step, 0]
        )
        grouped_queries = query_rows.reshape(row_count, key_heads, group_size, head_size)
        logits = masked_logits(grouped_queries, key_matrix, allowed, score_scale)
        largest = jnp.max(logits, axis=-1, keepdims=True)
        scaled_exp = jnp.exp(logits - largest)
        denominator = jnp.sum(scaled_exp, axis=-1, keepdims=True)
        soft = (scaled_exp / denominator).astype(jnp.bfloat16)
        log_total = largest + jnp.log(denominator)
        heads_out = (
            jnp.einsum("hgqk,khd->qhgd", soft, value_rows, preferred_element_type=jnp.float32)
            .reshape(row_count, query_heads * head_size)
            .astype(jnp.bfloat16)
        )
        resid_mid = resid_in + jnp.dot(heads_out, out_w, preferred_element_type=jnp.float32)
        inverse_mid = inverse_rms(resid_mid)
        normed_mid = (resid_mid * inverse_mid * gain_moe).astype(jnp.bfloat16)
        picks = routes[micro_step, 0].reshape(row_count * top_count)
        hits = (picks[:, None] == expert_ids[None, :]).astype(jnp.int32)
        earlier = jnp.cumsum(hits, axis=0) - hits
        places = picks * room_size + jnp.sum(earlier * hits, axis=1)
        outgoing = (
            jnp.zeros(buffer_shape, jnp.bfloat16)
            .at[places]
            .set(jnp.repeat(normed_mid, top_count, axis=0))
        )
        arrived = lax.all_to_all(
            outgoing.reshape(send_shape), "experts", split_axis=0, concat_axis=0, tiled=True
        ).reshape(arrive_shape)
        gate_act = jnp.einsum("iecd,edf->iecf", arrived, w_gate, preferred_element_type=jnp.float32)
        up_act = jnp.einsum("iecd,edf->iecf", arrived, w_up, preferred_element_type=jnp.float32)
        hidden = (jax.nn.silu(gate_act) * up_act).astype(jnp.bfloat16)
        produced = jnp.einsum(
            "iecf,efd->iecd", hidden, w_down, preferred_element_type=jnp.float32
        ).astype(jnp.bfloat16)
        returned = lax.all_to_all(
            produced.reshape(send_shape), "experts", split_axis=0, concat_axis=0, tiled=True
        ).reshape(buffer_shape)
        mixing = mix_weights[micro_step, 0]
        combined = jnp.sum(
            returned[places].reshape(row_count, top_count, model_width) * mixing[:, :, None], axis=1
        )
        outputs.append((resid_mid + combined).astype(jnp.bfloat16))
        saved.append(
            (
                resid_in,
                inverse_in,
                normed_in,
                query_pre,
                key_unrotated,
                inverse_query,
                inverse_key,
                key_local,
                value_local,
                key_matrix,
                value_rows,
                allowed,
                grouped_queries,
                soft,
                log_total,
                heads_out,
                resid_mid,
                inverse_mid,
                places,
                arrived,
                gate_act,
                up_act,
                hidden,
            )
        )
    grad_query_w = jnp.zeros(query_w.shape, jnp.float32)
    grad_key_w = jnp.zeros(key_w.shape, jnp.float32)
    grad_value_w = jnp.zeros(value_w.shape, jnp.float32)
    grad_out_w = jnp.zeros(out_w.shape, jnp.float32)
    grad_attn_gain = jnp.zeros(gain_attn.shape, jnp.float32)
    grad_moe_gain = jnp.zeros(gain_moe.shape, jnp.float32)
    grad_query_gain = jnp.zeros(gain_query.shape, jnp.float32)
    grad_key_gain = jnp.zeros(key_gain.shape, jnp.float32)
    grad_gate = jnp.zeros(w_gate.shape, jnp.float32)
    grad_up = jnp.zeros(w_up.shape, jnp.float32)
    grad_down = jnp.zeros(w_down.shape, jnp.float32)
    input_grads = []
    for micro_step in range(micro_count):
        (
            resid_in,
            inverse_in,
            normed_in,
            query_pre,
            key_unrotated,
            inverse_query,
            inverse_key,
            key_local,
            value_local,
            key_matrix,
            value_rows,
            allowed,
            grouped_queries,
            soft,
            log_total,
            heads_out,
            resid_mid,
            inverse_mid,
            places,
            arrived,
            gate_act,
            up_act,
            hidden,
        ) = saved[micro_step]
        valid = (query_pos < lengths[micro_step, 0]).astype(jnp.float32)
        grad_top = cotangent[micro_step, 0].astype(jnp.float32) * valid[:, None]
        mixing = mix_weights[micro_step, 0]
        sent_grad = (
            jnp.repeat(grad_top, top_count, axis=0) * mixing.reshape(row_count * top_count, 1)
        ).astype(jnp.bfloat16)
        grad_outgoing = jnp.zeros(buffer_shape, jnp.bfloat16).at[places].set(sent_grad)
        grad_arrived = lax.all_to_all(
            grad_outgoing.reshape(send_shape), "experts", split_axis=0, concat_axis=0, tiled=True
        ).reshape(arrive_shape)
        grad_hidden = jnp.einsum(
            "iecd,efd->iecf", grad_arrived, w_down, preferred_element_type=jnp.float32
        )
        grad_down = grad_down + jnp.einsum(
            "iecf,iecd->efd", hidden, grad_arrived, preferred_element_type=jnp.float32
        )
        sigma = jax.nn.sigmoid(gate_act)
        grad_gate_act = (grad_hidden * up_act * sigma * (1.0 + gate_act * (1.0 - sigma))).astype(
            jnp.bfloat16
        )
        grad_up_act = (grad_hidden * gate_act * sigma).astype(jnp.bfloat16)
        grad_gate = grad_gate + jnp.einsum(
            "iecd,iecf->edf", arrived, grad_gate_act, preferred_element_type=jnp.float32
        )
        grad_up = grad_up + jnp.einsum(
            "iecd,iecf->edf", arrived, grad_up_act, preferred_element_type=jnp.float32
        )
        grad_arrival = jnp.einsum(
            "iecf,edf->iecd", grad_gate_act, w_gate, preferred_element_type=jnp.float32
        )
        grad_arrival = (
            grad_arrival
            + jnp.einsum("iecf,edf->iecd", grad_up_act, w_up, preferred_element_type=jnp.float32)
        ).astype(jnp.bfloat16)
        grad_back = lax.all_to_all(
            grad_arrival.reshape(send_shape), "experts", split_axis=0, concat_axis=0, tiled=True
        ).reshape(buffer_shape)
        grad_normed_mid = jnp.sum(
            grad_back[places].reshape(row_count, top_count, model_width), axis=1, dtype=jnp.float32
        )
        grad_moe_gain = grad_moe_gain + jnp.sum(grad_normed_mid * resid_mid * inverse_mid, axis=0)
        grad_mid = grad_top + norm_back(grad_normed_mid, resid_mid, inverse_mid, gain_moe)
        grad_attn_out = grad_mid.astype(jnp.bfloat16)
        grad_heads = (
            against(grad_attn_out, out_w)
            .astype(jnp.bfloat16)
            .reshape(row_count, key_heads, group_size, head_size)
        )
        use_keys, use_values = (key_matrix, value_rows)
        logits = masked_logits(grouped_queries, use_keys, allowed, score_scale)
        probs = jnp.exp(logits - log_total)
        grad_soft = jnp.einsum(
            "qhgd,khd->hgqk", grad_heads, use_values, preferred_element_type=jnp.float32
        )
        grad_logits = (
            probs * (grad_soft - jnp.sum(probs * grad_soft, axis=-1, keepdims=True))
        ).astype(jnp.bfloat16)
        grad_queries = (
            jnp.einsum(
                "hgqk,khd->qhgd", grad_logits, use_keys, preferred_element_type=jnp.float32
            ).reshape(row_count, query_heads, head_size)
            * score_scale
        )
        grad_key_rows = (
            jnp.einsum(
                "hgqk,qhgd->khd", grad_logits, grouped_queries, preferred_element_type=jnp.float32
            )
            * score_scale
        )
        grad_value_rows = jnp.einsum(
            "hgqk,qhgd->khd", soft, grad_heads, preferred_element_type=jnp.float32
        )
        grad_key_local, grad_value_local = (
            lax.psum_scatter(
                grad_key_rows.astype(jnp.bfloat16), "context", scatter_dimension=0, tiled=True
            ).astype(jnp.float32),
            lax.psum_scatter(
                grad_value_rows.astype(jnp.bfloat16), "context", scatter_dimension=0, tiled=True
            ).astype(jnp.float32),
        )
        grad_value_pre = grad_value_local.reshape(row_count, key_heads * head_size).astype(
            jnp.bfloat16
        )
        grad_key_normed = apply_rotation(grad_key_local, cosine_table, -sine_values)
        grad_key_gain = grad_key_gain + jnp.sum(
            grad_key_normed * key_unrotated * inverse_key, axis=(0, 1)
        )
        grad_key_pre = (
            norm_back(grad_key_normed, key_unrotated, inverse_key, key_gain)
            .reshape(row_count, key_heads * head_size)
            .astype(jnp.bfloat16)
        )
        grad_query_normed = apply_rotation(grad_queries, cosine_table, -sine_values)
        grad_query_gain = grad_query_gain + jnp.sum(
            grad_query_normed * query_pre * inverse_query, axis=(0, 1)
        )
        grad_query_pre = (
            norm_back(grad_query_normed, query_pre, inverse_query, gain_query)
            .reshape(row_count, query_heads * head_size)
            .astype(jnp.bfloat16)
        )
        grad_out_w = grad_out_w + outer(heads_out, grad_attn_out)
        grad_query_w = grad_query_w + outer(normed_in, grad_query_pre)
        grad_key_w = grad_key_w + outer(normed_in, grad_key_pre)
        grad_value_w = grad_value_w + outer(normed_in, grad_value_pre)
        grad_normed_in = (
            against(grad_query_pre, query_w)
            + against(grad_key_pre, key_w)
            + against(grad_value_pre, value_w)
        )
        grad_attn_gain = grad_attn_gain + jnp.sum(grad_normed_in * resid_in * inverse_in, axis=0)
        input_grads.append(grad_mid + norm_back(grad_normed_in, resid_in, inverse_in, gain_attn))
    shards = (
        lax.psum_scatter(
            grad_query_w.astype(jnp.bfloat16), "experts", scatter_dimension=0, tiled=True
        ).astype(jnp.float32),
        lax.psum_scatter(
            grad_key_w.astype(jnp.bfloat16), "experts", scatter_dimension=0, tiled=True
        ).astype(jnp.float32),
        lax.psum_scatter(
            grad_value_w.astype(jnp.bfloat16), "experts", scatter_dimension=0, tiled=True
        ).astype(jnp.float32),
        lax.psum_scatter(
            grad_out_w.astype(jnp.bfloat16), "experts", scatter_dimension=0, tiled=True
        ).astype(jnp.float32),
        lax.psum_scatter(
            grad_attn_gain.astype(jnp.bfloat16), "experts", scatter_dimension=0, tiled=True
        ).astype(jnp.float32),
        lax.psum_scatter(
            grad_moe_gain.astype(jnp.bfloat16), "experts", scatter_dimension=0, tiled=True
        ).astype(jnp.float32),
        lax.psum_scatter(
            grad_query_gain.astype(jnp.bfloat16), "experts", scatter_dimension=0, tiled=True
        ).astype(jnp.float32),
        lax.psum_scatter(
            grad_key_gain.astype(jnp.bfloat16), "experts", scatter_dimension=0, tiled=True
        ).astype(jnp.float32),
    )
    results = (
        lax.psum(shards[0].astype(jnp.bfloat16), ("context", "dp")).astype(jnp.float32),
        lax.psum(shards[1].astype(jnp.bfloat16), ("context", "dp")).astype(jnp.float32),
        lax.psum(shards[2].astype(jnp.bfloat16), ("context", "dp")).astype(jnp.float32),
        lax.psum(shards[3].astype(jnp.bfloat16), ("context", "dp")).astype(jnp.float32),
        lax.psum(shards[4].astype(jnp.bfloat16), ("context", "dp")).astype(jnp.float32),
        lax.psum(shards[5].astype(jnp.bfloat16), ("context", "dp")).astype(jnp.float32),
        lax.psum(shards[6].astype(jnp.bfloat16), ("context", "dp")).astype(jnp.float32),
        lax.psum(shards[7].astype(jnp.bfloat16), ("context", "dp")).astype(jnp.float32),
        lax.psum(grad_gate.astype(jnp.bfloat16), ("context", "dp")).astype(jnp.float32),
        lax.psum(grad_up.astype(jnp.bfloat16), ("context", "dp")).astype(jnp.float32),
        lax.psum(grad_down.astype(jnp.bfloat16), ("context", "dp")).astype(jnp.float32),
    )
    output = jnp.stack(outputs)[:, None]
    input_grad = jnp.stack(input_grads)[:, None]
    return (
        output,
        input_grad,
        results[0],
        results[1],
        results[2],
        results[3],
        results[4],
        results[5],
        results[6],
        results[7],
        results[8],
        results[9],
        results[10],
    )


def solution(mesh):
    in_specs = (
        P(None, ("experts", "dp"), "context", None),
        P(None, ("experts", "dp")),
        P(None, ("experts", "dp"), "context", None),
        P(None, ("experts", "dp"), "context", None),
        P(None, ("experts", "dp"), "context", None),
        P("experts", None),
        P("experts", None),
        P("experts", None),
        P("experts", None),
        P("experts"),
        P("experts"),
        P("experts"),
        P("experts"),
        P("experts", None, None),
        P("experts", None, None),
        P("experts", None, None),
    )
    out_specs = (
        P(None, ("experts", "dp"), "context", None),
        P(None, ("experts", "dp"), "context", None),
        P("experts", None),
        P("experts", None),
        P("experts", None),
        P("experts", None),
        P("experts"),
        P("experts"),
        P("experts"),
        P("experts"),
        P("experts", None, None),
        P("experts", None, None),
        P("experts", None, None),
    )
    return jax.shard_map(local, mesh=mesh, in_specs=in_specs, out_specs=out_specs, check_vma=False)
```

profile of v0, /device:TPU:49, one launch (start us, length us, event | category | flops | bytes accessed | tf_op | source)
XLA Modules:
  0.0 1388.4 jit_solution(7807262874247576225)
XLA Ops:
  12.7 29.9 %all-reduce.9 = (bf16[128]{0:T(256)(128)(2,1)S(1)}, bf16[128]{0:T(256)(128)(2,1)S(1)}) all-reduce(bf16[128]{0:T(256)(128)(2,1)S(1)} %dynamic-update-slice, bf16[128]{0:T(256)(128)(2,1)S(1)} %dynamic-update-slice.1), channel_id=1, replica_groups=mesh['experts'=16,'context'=4,'dp'=2] {'experts'}, use_global_device_ids=true, to_apply=%add | all-reduce | flops 256 | bytes 1024
  43.2 19.1 %all-gather = bf16[16,1,128]{2,1,0:T(2,128)(2,1)S(1)} all-gather(bf16[1,1,128]{2,1,0:T(2,128)(2,1)S(1)} %bitcast.704), channel_id=1, replica_groups=mesh['experts'=16,'context'=4,'dp'=2] {'experts'}, dimensions={0}, use_global_device_ids=true | all-gather | bytes 4352 | tf_op jit(solution)/shard_map/all_gather | solution.py:85
  62.3 14.1 %all-gather.1 = bf16[16,1,128]{2,1,0:T(2,128)(2,1)S(1)} all-gather(bf16[1,1,128]{2,1,0:T(2,128)(2,1)S(1)} %bitcast.705), channel_id=1, replica_groups=mesh['experts'=16,'context'=4,'dp'=2] {'experts'}, dimensions={0}, use_global_device_ids=true | all-gather | bytes 4352 | tf_op jit(solution)/shard_map/all_gather | solution.py:86
  87.3 15.5 %all-gather.9.cloned.1.call-done = bf16[2048,512]{1,0:T(8,128)(2,1)} async-done(((bf16[128,512]{1,0:T(8,128)(2,1)}), bf16[2048,512]{1,0:T(8,128)(2,1)}) %all-gather.9.cloned.1.call-update) | async-done | bytes 2097168 | tf_op jit(solution)/shard_map/all_gather | solution.py:82
  132.7 84.1 %all-gather.11.cloned.1.call-done = bf16[2048,4096]{1,0:T(8,128)(2,1)} async-done(((bf16[128,4096]{1,0:T(8,128)(2,1)}), bf16[2048,4096]{1,0:T(8,128)(2,1)}) %all-gather.11.cloned.1.call-update) | async-done | bytes 16777232 | tf_op jit(solution)/shard_map/all_gather | solution.py:81
  216.8 22.7 %copy.73 = bf16[4096,2048]{1,0:T(8,128)(2,1)} copy(bf16[4096,2048]{0,1:T(8,128)(2,1)} %bitcast.647) | data formatting | bytes 33554432 | tf_op jit(solution)/shard_map/dot_general | solution.py:122
  239.5 12.3 multiply_reduce_fusion.4
  252.5 12.1 multiply_reduce_fusion.5
  273.8 56.1 %all-gather.13.cloned.1.call-done = bf16[4096,2048]{1,0:T(8,128)(2,1)} async-done(((bf16[256,2048]{1,0:T(8,128)(2,1)}), bf16[4096,2048]{1,0:T(8,128)(2,1)}) %all-gather.13.cloned.1.call-update) | async-done | bytes 16777232 | tf_op jit(solution)/shard_map/all_gather | solution.py:84
  373.3 15.2 %all-to-all-done = bf16[16,33,2048]{2,1,0:T(8,128)(2,1)} async-done(((bf16[16,33,2048]{2,1,0:T(8,128)(2,1)}), bf16[16,33,2048]{2,1,0:T(8,128)(2,1)}, u32[]{:S(2)}, u32[]{:S(2)}) %all-to-all-start) | async-done | bytes 2162720 | tf_op jit(solution)/shard_map/all_to_all | solution.py:169
  520.8 19.6 %all-to-all-done.2 = bf16[16,33,2048]{2,1,0:T(8,128)(2,1)} async-done(((bf16[16,33,2048]{2,1,0:T(8,128)(2,1)}), bf16[16,33,2048]{2,1,0:T(8,128)(2,1)}, u32[]{:S(2)}, u32[]{:S(2)}) %all-to-all-start.2) | async-done | bytes 2162720 | tf_op jit(solution)/shard_map/all_to_all | solution.py:169
  558.8 15.9 %all-to-all-done.6 = bf16[16,33,2048]{2,1,0:T(8,128)(2,1)} async-done(((bf16[16,33,2048]{2,1,0:T(8,128)(2,1)}), bf16[16,33,2048]{2,1,0:T(8,128)(2,1)}, u32[]{:S(2)}, u32[]{:S(2)}) %all-to-all-start.6) | async-done | bytes 2162720 | tf_op jit(solution)/shard_map/all_to_all | solution.py:258
  574.7 11.7 all-to-all-start.1
  602.1 13.3 all-to-all-done.1
  633.2 21.2 %all-to-all-done.3 = bf16[16,33,2048]{2,1,0:T(8,128)(2,1)S(1)} async-done(((bf16[16,33,2048]{2,1,0:T(8,128)(2,1)}), bf16[16,33,2048]{2,1,0:T(8,128)(2,1)S(1)}, u32[]{:S(2)}, u32[]{:S(2)}) %all-to-all-start.3) | async-done | bytes 2162720 | tf_op jit(solution)/shard_map/all_to_all | solution.py:178
  681.4 13.0 all-to-all-done.7
  707.0 11.4 fusion.73
  720.2 11.8 fusion.72
  752.3 38.7 %all-reduce.18.cloned.1.call-done = (bf16[256,4,128]{2,1,0:T(4,128)(2,1)}, bf16[256,4,128]{2,1,0:T(4,128)(2,1)}) async-done(((bf16[256,4,128]{2,1,0:T(4,128)(2,1)}, bf16[256,4,128]{2,1,0:T(4,128)(2,1)}), (bf16[256,4,128]{2,1,0:T(4,128)(2,1)}, bf16[256,4,128]{2,1,0:T(4,128)(2,1)})) %all-reduce.18.cloned.1.call-update) | async-done | bytes 524304
  796.5 16.9 %reduce-scatter.7.cloned.1.call-done = bf16[64,4,128]{2,0,1:T(8,128)(2,1)} async-done(((bf16[256,4,128]{2,0,1:T(8,128)(2,1)}), bf16[64,4,128]{2,0,1:T(8,128)(2,1)}) %reduce-scatter.7.cloned.1.call-update) | async-done | bytes 65552 | tf_op jit(solution)/shard_map/reduce_scatter | solution.py:324
  814.3 22.5 %reduce-scatter.9.cloned.1.call-done = bf16[64,4,128]{2,0,1:T(8,128)(2,1)} async-done(((bf16[256,4,128]{2,0,1:T(8,128)(2,1)}), bf16[64,4,128]{2,0,1:T(8,128)(2,1)}) %reduce-scatter.9.cloned.1.call-update) | async-done | bytes 65552 | tf_op jit(solution)/shard_map/reduce_scatter | solution.py:324
  843.0 14.6 %fusion.139 = f32[4096,2048]{1,0:T(8,128)} fusion(bf16[8,8,32,128]{3,2,1,0:T(8,128)(2,1)} %bitcast.661, f32[64,2048]{1,0:T(8,128)S(1)} %copy-done.19), kind=kOutput, calls=%fused_computation.229 | convolution fusion | flops 1073872896 | bytes 34603008 | tf_op jit(solution)/shard_map/dot_general | solution.py:41
  857.6 18.7 %add_convert_fusion = bf16[4096,2048]{1,0:T(8,128)(2,1)} fusion(f32[4096,2048]{1,0:T(8,128)} %fusion.139, bf16[8,8,32,128]{3,2,1,0:T(8,128)(2,1)S(1)} %bitcast.659, f32[64,2048]{1,0:T(8,128)S(1)} %copy-done.22), kind=kOutput, calls=%fused_computation.8 | convolution fusion | flops 1090650112 | bytes 51380224 | tf_op jit(solution)/shard_map/dot_general | solution.py:41
  884.2 13.4 fusion.145
  897.5 17.1 %add_convert_fusion.1 = bf16[2048,4096]{1,0:T(8,128)(2,1)} fusion(f32[2048,4096]{1,0:T(8,128)} %fusion.145, bf16[32,8,8,128]{3,2,1,0:T(8,128)(2,1)S(1)} %get-tuple-element.160, f32[64]{0:T(128)S(1)} %copy-done.92, f32[2048]{0:T(1024)S(1)} %bitcast.681, bf16[2,1,64,2048]{3,2,1,0:T(8,128)(2,1)S(1)} %copy-done.8), kind=kOutput, calls=%fused_computation.9 | convolution fusion | flops 1091043328 | bytes 51126784 | tf_op jit(solution)/shard_map/dot_general | solution.py:41
  948.5 45.8 %reduce-scatter.13.cloned.1.call-done = bf16[128,512]{1,0:T(8,128)(2,1)} async-done(((bf16[2048,512]{1,0:T(8,128)(2,1)}), bf16[128,512]{1,0:T(8,128)(2,1)}) %reduce-scatter.13.cloned.1.call-update) | async-done | bytes 131088 | tf_op jit(solution)/shard_map/reduce_scatter | solution.py:367
  994.2 115.2 %reduce-scatter.17.cloned.1.call-done = bf16[256,2048]{1,0:T(8,128)(2,1)} async-done(((bf16[4096,2048]{1,0:T(8,128)(2,1)}), bf16[256,2048]{1,0:T(8,128)(2,1)}) %reduce-scatter.17.cloned.1.call-update) | async-done | bytes 1048592 | tf_op jit(solution)/shard_map/reduce_scatter | solution.py:373
  1109.4 113.6 %reduce-scatter.11.cloned.1.call-done = bf16[128,4096]{1,0:T(8,128)(2,1)} async-done(((bf16[2048,4096]{1,0:T(8,128)(2,1)}), bf16[128,4096]{1,0:T(8,128)(2,1)}) %reduce-scatter.11.cloned.1.call-update) | async-done | bytes 1048592 | tf_op jit(solution)/shard_map/reduce_scatter | solution.py:364
  1236.3 11.4 fusion.143
  1253.7 30.0 %all-reduce.8 = (bf16[2048]{0:T(1024)(128)(2,1)S(1)}, bf16[2048]{0:T(1024)(128)(2,1)S(1)}, bf16[128]{0:T(256)(128)(2,1)S(1)}, bf16[128]{0:T(256)(128)(2,1)S(1)}) all-reduce(bf16[2048]{0:T(1024)(128)(2,1)S(1)} %add_convert_fusion.13, ...), channel_id=10, replica_groups=mesh['experts'=16,'context'=4,'dp'=2] {'experts'}, use_global_device_ids=true, to_apply=%region_50.51.clone | all-reduce | flops 4352 | bytes 17408
  1284.0 17.5 %all-reduce.10 = (bf16[128]{0:T(256)(128)(2,1)S(1)}, bf16[128]{0:T(256)(128)(2,1)S(1)}, bf16[8]{0:T(256)(128)(2,1)S(1)}, bf16[8]{0:T(256)(128)(2,1)S(1)}) all-reduce(bf16[128]{0:T(256)(128)(2,1)S(1)} %dynamic-slice.7, bf16[128]{0:T(256)(128)(2,1)S(1)} %dynamic-slice.9, ...), channel_id=1, replica_groups=mesh['experts'=16,'context'=4,'dp'=2] {'context','dp'}, use_global_device_ids=true, to_apply=%region_51.52 | all-reduce | flops 272 | bytes 1088 | tf_op jit(solution)/shard_map/psum | solution.py:394
  1306.7 55.9 %all-reduce.16.cloned.1.call-done = (bf16[128,4096]{1,0:T(8,128)(2,1)}, bf16[128,512]{1,0:T(8,128)(2,1)}, bf16[128,512]{1,0:T(8,128)(2,1)}, bf16[256,2048]{1,0:T...) async-done(((bf16[128,4096]{1,0:T(8,128)(2,1)}, bf16[128,512]{1,0:T(8,128)(2,1)}, ...) | async-done | bytes 11796496 | tf_op jit(solution)/shard_map/psum | solution.py:390
  (532 shorter events, 439.0 us)
Async XLA Ops:
  7.2 424.1 %copy-start = (bf16[1,768,2048]{2,1,0:T(8,128)(2,1)S(1)}, bf16[1,768,2048]{2,1,0:T(8,128)(2,1)}, u32[]{:S(2)}) copy-start(bf16[1,768,2048]{2,1,0:T(8,128)(2,1)} %param.31) | copy-start | bytes 9437188
  7.2 55.1 %copy-start.129 = (bf16[128]{0:T(256)(128)(2,1)S(1)}, bf16[128]{0:T(256)(128)(2,1)}, u32[]{:S(2)}) copy-start(bf16[128]{0:T(256)(128)(2,1)} %param.26) | copy-start | bytes 772
  7.3 70.9 %copy-start.124 = (s32[2,1]{0,1:T(1,128)S(1)}, s32[2,1]{0,1:T(1,128)}, u32[]{:S(2)}) copy-start(s32[2,1]{0,1:T(1,128)} %param.17) | copy-start | bytes 28
  7.3 76.1 %all-gather.7.cloned.1.call-start = ((), (), s32[]{:S(2)}) async-start(), calls=%async_computation.14 | async-start | bytes 2228224 | tf_op jit(solution)/shard_map/all_gather | solution.py:83
  8.0 94.7 %all-gather.9.cloned.1.call-start = ((), (), s32[]{:S(2)}) async-start(), calls=%async_computation.15 | async-start | bytes 2228224 | tf_op jit(solution)/shard_map/all_gather | solution.py:82
  8.8 208.1 %all-gather.11.cloned.1.call-start = ((), (), s32[]{:S(2)}) async-start(), calls=%async_computation.16 | async-start | bytes 17825792 | tf_op jit(solution)/shard_map/all_gather | solution.py:81
  9.5 320.4 %all-gather.13.cloned.1.call-start = ((), (), s32[]{:S(2)}) async-start(), calls=%async_computation.17 | async-start | bytes 17825792 | tf_op jit(solution)/shard_map/all_gather | solution.py:84
  42.7 77.7 %copy-start.118 = (f32[128]{0:T(128)}, f32[128]{0:T(128)S(1)}, u32[]{:S(2)}) copy-start(f32[128]{0:T(128)S(1)} %convert_element_type.415) | copy-start | bytes 1540
  81.9 157.7 %copy-start.90 = (f32[64]{0:T(128)}, f32[64]{0:T(128)S(1)}, u32[]{:S(2)}) copy-start(f32[64]{0:T(128)S(1)} %get-tuple-element.154) | copy-start | bytes 772
  83.3 183.8 %copy-start.69 = (f32[64,64]{1,0:T(8,128)}, f32[64,64]{1,0:T(8,128)S(1)}, u32[]{:S(2)}) copy-start(f32[64,64]{1,0:T(8,128)S(1)} %get-tuple-element.148) | copy-start | bytes 49156
  120.4 119.2 %copy-start.95 = (f32[64,4]{0,1:T(4,128)}, f32[64,4]{0,1:T(4,128)S(1)}, u32[]{:S(2)}) copy-start(f32[64,4]{0,1:T(4,128)S(1)} %get-tuple-element.143) | copy-start | bytes 3076
  349.1 39.4 %all-to-all-start = ((bf16[16,33,2048]{2,1,0:T(8,128)(2,1)}), bf16[16,33,2048]{2,1,0:T(8,128)(2,1)}, u32[]{:S(2)}, u32[]{:S(2)}) async-start(bf16[16,33,2048]{2,1,0:T(8,128)(2,1)} %reshape.832), calls=%async_computation | async-start | bytes 5242880 | tf_op jit(solution)/shard_map/all_to_all | solution.py:169
  373.2 106.5 %copy-start.99 = (s32[1024]{0:T(1024)}, s32[1024]{0:T(1024)S(1)}, u32[]{:S(2)}) copy-start(s32[1024]{0:T(1024)S(1)} %pad_clamp_fusion.1) | copy-start | bytes 12292
  373.3 118.1 %copy-start.109 = (s32[512,1]{0,1:T(1,128)}, s32[512,1]{0,1:T(1,128)S(1)}, u32[]{:S(2)}) copy-start(s32[512,1]{0,1:T(1,128)S(1)} %compare_select_fusion) | copy-start | bytes 6148
  388.5 42.8 %all-to-all-start.4 = ((bf16[16,33,2048]{2,1,0:T(8,128)(2,1)}), bf16[16,33,2048]{2,1,0:T(8,128)(2,1)}, u32[]{:S(2)}, u32[]{:S(2)}) async-start(bf16[16,33,2048]{2,1,0:T(8,128)(2,1)} %reshape.844), calls=%async_computation.4 | async-start | bytes 5242880 | tf_op jit(solution)/shard_map/all_to_all | solution.py:258
  444.6 32.1 %all-to-all-start.5 = ((bf16[16,33,2048]{2,1,0:T(8,128)(2,1)}), bf16[16,33,2048]{2,1,0:T(8,128)(2,1)}, u32[]{:S(2)}, u32[]{:S(2)}) async-start(bf16[16,33,2048]{2,1,0:T(8,128)(2,1)} %add_convert_fusion.3), calls=%async_computation.5 | async-start | bytes 5242880 | tf_op jit(solution)/shard_map/all_to_all | solution.py:285
  500.5 39.8 %all-to-all-start.2 = ((bf16[16,33,2048]{2,1,0:T(8,128)(2,1)}), bf16[16,33,2048]{2,1,0:T(8,128)(2,1)}, u32[]{:S(2)}, u32[]{:S(2)}) async-start(bf16[16,33,2048]{2,1,0:T(8,128)(2,1)} %reshape.840), calls=%async_computation.2 | async-start | bytes 5242880 | tf_op jit(solution)/shard_map/all_to_all | solution.py:169
  540.4 34.4 %all-to-all-start.6 = ((bf16[16,33,2048]{2,1,0:T(8,128)(2,1)}), bf16[16,33,2048]{2,1,0:T(8,128)(2,1)}, u32[]{:S(2)}, u32[]{:S(2)}) async-start(bf16[16,33,2048]{2,1,0:T(8,128)(2,1)} %reshape.850), calls=%async_computation.7 | async-start | bytes 5242880 | tf_op jit(solution)/shard_map/all_to_all | solution.py:258
  574.7 40.8 %all-to-all-start.1 = ((bf16[16,33,2048]{2,1,0:T(8,128)(2,1)}), bf16[16,33,2048]{2,1,0:T(8,128)(2,1)}, u32[]{:S(2)}, u32[]{:S(2)}) async-start(bf16[16,33,2048]{2,1,0:T(8,128)(2,1)} %convolution_convert_fusion.3), calls=%async_computation.1 | async-start | bytes 5242880 | tf_op jit(solution)/shard_map/all_to_all | solution.py:178
  615.5 38.9 %all-to-all-start.3 = ((bf16[16,33,2048]{2,1,0:T(8,128)(2,1)}), bf16[16,33,2048]{2,1,0:T(8,128)(2,1)S(1)}, u32[]{:S(2)}, u32[]{:S(2)}) async-start(bf16[16,33,2048]{2,1,0:T(8,128)(2,1)} %convolution_convert_fusion.2), calls=%async_computation.3 | async-start | bytes 5242880 | tf_op jit(solution)/shard_map/all_to_all | solution.py:178
  655.8 38.6 %all-to-all-start.7 = ((bf16[16,33,2048]{2,1,0:T(8,128)(2,1)}), bf16[16,33,2048]{2,1,0:T(8,128)(2,1)}, u32[]{:S(2)}, u32[]{:S(2)}) async-start(bf16[16,33,2048]{2,1,0:T(8,128)(2,1)} %add_convert_fusion.2), calls=%async_computation.8 | async-start | bytes 5242880 | tf_op jit(solution)/shard_map/all_to_all | solution.py:285
  664.9 126.1 %all-reduce.18.cloned.1.call-start = ((), (), s32[]{:S(2)}) async-start(), calls=%async_computation.25 | async-start | bytes 1048576
  740.8 72.6 %reduce-scatter.7.cloned.1.call-start = ((), (), s32[]{:S(2)}) async-start(), calls=%async_computation.18 | async-start | bytes 327680 | tf_op jit(solution)/shard_map/reduce_scatter | solution.py:324
  747.6 89.2 %reduce-scatter.9.cloned.1.call-start = ((), (), s32[]{:S(2)}) async-start(), calls=%async_computation.19 | async-start | bytes 327680 | tf_op jit(solution)/shard_map/reduce_scatter | solution.py:324
  752.2 196.3 %reduce-scatter.15.cloned.1.call-start = ((), (), s32[]{:S(2)}) async-start(), calls=%async_computation.22 | async-start | bytes 2228224 | tf_op jit(solution)/shard_map/reduce_scatter | solution.py:370
  796.5 197.7 %reduce-scatter.13.cloned.1.call-start = ((), (), s32[]{:S(2)}) async-start(), calls=%async_computation.21 | async-start | bytes 2228224 | tf_op jit(solution)/shard_map/reduce_scatter | solution.py:367
  842.0 267.4 %reduce-scatter.17.cloned.1.call-start = ((), (), s32[]{:S(2)}) async-start(), calls=%async_computation.23 | async-start | bytes 17825792 | tf_op jit(solution)/shard_map/reduce_scatter | solution.py:373
  876.4 346.6 %reduce-scatter.11.cloned.1.call-start = ((), (), s32[]{:S(2)}) async-start(), calls=%async_computation.20 | async-start | bytes 17825792 | tf_op jit(solution)/shard_map/reduce_scatter | solution.py:364
  914.6 448.0 %all-reduce.16.cloned.1.call-start = ((), (), s32[]{:S(2)}) async-start(), calls=%async_computation.24 | async-start | bytes 23592960 | tf_op jit(solution)/shard_map/psum | solution.py:390
  1251.9 51.6 %copy-start.20 = (f32[64,2048]{1,0:T(8,128)S(1)}, f32[64,2048]{1,0:T(8,128)}, u32[]{:S(2)}) copy-start(f32[64,2048]{1,0:T(8,128)} %copy-done.18) | copy-start | bytes 1572868
  1251.9 51.6 %copy-start.125 = (f32[64]{0:T(128)S(1)}, f32[64]{0:T(128)}, u32[]{:S(2)}) copy-start(f32[64]{0:T(128)} %get-tuple-element.153) | copy-start | bytes 772
  1251.9 51.6 %copy-start.126 = (f32[64]{0:T(128)S(1)}, f32[64]{0:T(128)}, u32[]{:S(2)}) copy-start(f32[64]{0:T(128)} %get-tuple-element.197) | copy-start | bytes 772
  (139 other events, 1181.5 us)
Sparse Core Ops, SparseCore 0:
  10.2 45.6 all-gather.6
  58.1 44.5 all-gather.8
  104.9 111.8 all-gather.10
  218.8 111.0 all-gather.12
  741.0 49.9 all-reduce.17
  793.2 20.1 reduce-scatter.6
  816.5 20.2 reduce-scatter.8
  840.6 75.6 reduce-scatter.14
  920.5 73.6 reduce-scatter.12
  997.5 111.8 reduce-scatter.16
  1112.8 110.0 reduce-scatter.10
  1226.3 136.3 all-reduce.15
where the time goes:
time: 1400 us; the launch traced here: 1390 us
  waiting for transfers between devices  676 us (48%)
  matrix products  275 us (20%)
  blocking collectives  151 us (11%)
  local copies, waits for them, and re-layouts  111 us (8%)
  other arithmetic  88.9 us (6%)
  starting transfers between devices  67.9 us (5%)
  between operations  19 us (1%)
    reduce_scatter x1, waiting for transfers between devices, local(): lax.psum_scatter(grad_out_w.astype(jnp.bfloat16), 'experts', scatter_dime...  115 us
    reduce_scatter x1, waiting for transfers between devices, local(): lax.psum_scatter(grad_query_w.astype(jnp.bfloat16), 'experts', scatter_di...  114 us
    all_gather x1, waiting for transfers between devices, local(): lax.all_gather(w_query, 'experts', axis=0, tiled=True)  84.1 us
    dot_general x8, matrix products, outer(): lax.dot_general(left, right, (((0,), (0,)), ((), ())), preferred_element_...  69.6 us
    unnamed x2, blocking collectives  60 us
    all_gather x1, waiting for transfers between devices, local(): lax.all_gather(w_out, 'experts', axis=0, tiled=True)  56.1 us
    psum x1, waiting for transfers between devices, local(): lax.psum(shards[0].astype(jnp.bfloat16), ('context', 'dp'))  55.9 us
    dot_general x8, matrix products, against(): lax.dot_general(left, right, (((1,), (1,)), ((), ())), preferred_element_...  49.6 us
  transfers between devices with their start and end apart: 20, of which 17 were waited for; matrix products, arithmetic and copies ran while one was open for 25% of the time, Pallas kernels for 0%

commit v1 on v0

v1 whole, which is shorter than its diff:
```python
import functools

import jax
import jax.numpy as jnp
from jax import lax
from jax.experimental import pallas as pl
from jax.experimental.pallas import tpu as pltpu
from jax.sharding import PartitionSpec as P

EPS = 1e-06
ROPE_BASE = 1000000.0
F32 = jnp.float32
BF16 = jnp.bfloat16
GROUP = ("context", "dp")
EVERY = ("experts", "context", "dp")
VMEM = 60 * 1024 * 1024
SIDE = 4
TINY = pl.CostEstimate(flops=0, bytes_accessed=1000, transcendentals=0)


def inverse_rms(v):
    return lax.rsqrt(jnp.mean(v * v, axis=-1, keepdims=True) + EPS)


def norm_back(grad_in, v, inverse, gain):
    scaled = grad_in * gain
    return inverse * scaled - v * inverse**3 * jnp.mean(scaled * v, axis=-1, keepdims=True)


def matmul(left, right):
    return jnp.dot(left, right, preferred_element_type=F32)


def against(left, right):
    return lax.dot_general(left, right, (((1,), (1,)), ((), ())), preferred_element_type=F32)


def outer(left, right):
    return lax.dot_general(left, right, (((0,), (0,)), ((), ())), preferred_element_type=F32)


def swap(v):
    return lax.ppermute(v, "dp", [(0, 1), (1, 0)])


def gather_rows(own, ring):
    pieces = [own]
    for k in range(1, ring):
        pieces.append(lax.ppermute(own, "context", [((i + k) % ring, i) for i in range(ring)]))
    mine = jnp.stack(pieces)
    return jnp.stack([mine, swap(mine)])


def ring_sum(pieces):
    ring = len(pieces)
    total = pieces[0].astype(F32)
    for k in range(1, ring):
        got = lax.ppermute(pieces[k], "context", [(i, (i + k) % ring) for i in range(ring)])
        total = total + got.astype(F32)
    return total


def add_cores(theirs, mine):
    other = swap(theirs)
    return [
        (mine[k].astype(F32) + other[k].astype(F32)).astype(BF16) for k in range(mine.shape[0])
    ]


def scatter_rows(theirs, mine):
    return ring_sum(add_cores(theirs, mine))


def gather_members(v):
    ring = lax.axis_size("context")
    pieces = [v]
    for k in range(1, ring):
        pieces.append(lax.ppermute(v, "context", [((i + k) % ring, i) for i in range(ring)]))
    mine = jnp.stack(pieces)
    return mine, swap(mine)


def plane(v, dx, dz):
    moves = [
        (((i // SIDE + dx) % SIDE) * SIDE + (i % SIDE + dz) % SIDE, i) for i in range(SIDE * SIDE)
    ]
    return lax.ppermute(v, "experts", moves)


def after_kernel(v_ref, token_ref, out_ref):
    pass


def after_call(v, token):
    anywhere = pl.BlockSpec(memory_space=pl.ANY)
    return pl.pallas_call(
        after_kernel,
        in_specs=[anywhere, anywhere],
        out_specs=anywhere,
        out_shape=jax.ShapeDtypeStruct(v.shape, v.dtype),
        input_output_aliases={0: 0},
        cost_estimate=TINY,
        name="after",
    )(v, token)


def rope(v, cosines, sines):
    return v * cosines + pltpu.roll(v, v.shape[-1] // 2, 1) * sines


def rope_back(v, cosines, sines):
    return v * cosines + pltpu.roll(v * sines, v.shape[-1] // 2, 1)


def flat(ref):
    v = ref[...]
    return v.reshape(v.shape[1] * v.shape[3], v.shape[4])


def chunks(ref, columns):
    v = ref[:, :-16, :columns]
    return v.reshape(v.shape[0] * v.shape[1], columns)


def out_blocks(ref, first):
    last = ref.shape[2] - first
    rows = last // ref.shape[0]
    for k in range((ref.shape[1] - 16) // rows):
        yield k * last, (k + 1) * last, ref[:, k * rows : (k + 1) * rows, first:].reshape(last, last)


def put(ref, v):
    ref[...] = v.reshape(ref.shape).astype(ref.dtype)


def attend_kernel(
    heads,
    scale,
    x_ref,
    gain_ref,
    w_ref,
    cos_ref,
    sin_ref,
    bias_ref,
    gain_q_ref,
    gain_k_ref,
    token_ref,
    h1_ref,
    qkv_ref,
    heads_ref,
    theirs_ref,
    mine_ref,
    heads_out,
    total,
):
    size = cos_ref.shape[1]
    x = flat(x_ref).astype(F32)
    h1 = (x * inverse_rms(x) * gain_ref[...]).astype(BF16)
    put(h1_ref, h1)
    width = (heads + 2) * size
    qkv = matmul(h1, chunks(w_ref, width))
    put(qkv_ref, qkv)
    cosines, sines, bias = cos_ref[...], sin_ref[...], bias_ref[0]
    k_pre = qkv[:, heads * size : (heads + 1) * size]
    key = rope(k_pre * inverse_rms(k_pre) * gain_k_ref[...], cosines, sines).astype(BF16)
    value = qkv[:, (heads + 1) * size :].astype(BF16)
    for g in range(heads):
        q_pre = qkv[:, g * size : (g + 1) * size]
        query = rope(q_pre * inverse_rms(q_pre) * gain_q_ref[...], cosines, sines).astype(BF16)
        logits = against(query, key) * scale + bias
        scaled = jnp.exp(logits - jnp.max(logits, axis=-1, keepdims=True))
        soft = (scaled / jnp.sum(scaled, axis=-1, keepdims=True)).astype(BF16)
        heads_out[:, g * size : (g + 1) * size] = matmul(soft, value).astype(BF16)
    out = heads_out[...]
    put(heads_ref, out)
    for first, last, block in out_blocks(w_ref, width):
        total[:, first:last] = matmul(out, block).astype(BF16)

    @pl.when(pl.program_id(0) < 2)
    def _():
        put(theirs_ref, total[...])

    @pl.when(pl.program_id(0) >= 2)
    def _():
        put(mine_ref, total[...])


def attend_back_kernel(
    heads,
    scale,
    da_ref,
    x_ref,
    gain_ref,
    w_ref,
    cos_ref,
    sin_ref,
    bias_ref,
    gain_q_ref,
    gain_k_ref,
    qkv_ref,
    token_ref,
    other_token_ref,
    d_qkv_ref,
    theirs_ref,
    mine_ref,
    sum_q_ref,
    sum_k_ref,
    sum_x_ref,
    d_qkv,
):
    size = cos_ref.shape[1]
    step = pl.program_id(0)

    @pl.when(step == 0)
    def _():
        sum_q_ref[...] = jnp.zeros_like(sum_q_ref)
        sum_k_ref[...] = jnp.zeros_like(sum_k_ref)
        sum_x_ref[...] = jnp.zeros_like(sum_x_ref)

    width = (heads + 2) * size
    da = flat(da_ref)
    d_heads = None
    for first, last, block in out_blocks(w_ref, width):
        piece = against(da[:, first:last], block)
        d_heads = piece if d_heads is None else d_heads + piece
    d_heads = d_heads.astype(BF16)
    qkv = flat(qkv_ref)
    cosines, sines, bias = cos_ref[...], sin_ref[...], bias_ref[0]
    gain_q, gain_k = gain_q_ref[...], gain_k_ref[...]
    k_pre = qkv[:, heads * size : (heads + 1) * size]
    inverse_k = inverse_rms(k_pre)
    key = rope(k_pre * inverse_k * gain_k, cosines, sines).astype(BF16)
    value = qkv[:, (heads + 1) * size :].astype(BF16)
    d_key = jnp.zeros(k_pre.shape, F32)
    d_value = jnp.zeros(k_pre.shape, F32)
    sum_q = jnp.zeros((1, size), F32)
    for g in range(heads):
        q_pre = qkv[:, g * size : (g + 1) * size]
        inverse_q = inverse_rms(q_pre)
        query = rope(q_pre * inverse_q * gain_q, cosines, sines).astype(BF16)
        logits = against(query, key) * scale + bias
        scaled = jnp.exp(logits - jnp.max(logits, axis=-1, keepdims=True))
        probs = scaled / jnp.sum(scaled, axis=-1, keepdims=True)
        d_head = d_heads[:, g * size : (g + 1) * size]
        d_probs = against(d_head, value)
        d_scores = probs * (d_probs - jnp.sum(probs * d_probs, axis=-1, keepdims=True))
        d_scores = d_scores.astype(BF16)
        d_query = rope_back(matmul(d_scores, key) * scale, cosines, sines)
        d_key = d_key + outer(d_scores, query)
        d_value = d_value + outer(probs.astype(BF16), d_head)
        sum_q = sum_q + jnp.sum(d_query * q_pre * inverse_q, axis=0, keepdims=True)
        d_qkv[:, g * size : (g + 1) * size] = norm_back(d_query, q_pre, inverse_q, gain_q).astype(
            BF16
        )
    d_key = rope_back(d_key * scale, cosines, sines)
    sum_k = jnp.sum(d_key * k_pre * inverse_k, axis=0, keepdims=True)
    d_qkv[:, heads * size : (heads + 1) * size] = norm_back(d_key, k_pre, inverse_k, gain_k).astype(
        BF16
    )
    d_qkv[:, (heads + 1) * size :] = d_value.astype(BF16)
    grads = d_qkv[...]
    put(d_qkv_ref, grads)
    part = against(grads, chunks(w_ref, width))
    x = flat(x_ref).astype(F32)
    sum_x_ref[0:1, :] += jnp.sum(part * (x * inverse_rms(x)), axis=0, keepdims=True)
    sum_q_ref[0:1, :] += sum_q
    sum_k_ref[0:1, :] += sum_k

    @pl.when(step < 2)
    def _():
        put(theirs_ref, part)

    @pl.when(step >= 2)
    def _():
        put(mine_ref, part)


def attend_call(kernel, operands, extra, outputs, scratch, shape, name, flops):
    ring, micro, row_count, width = shape

    def rows_spec(last):
        return pl.BlockSpec(
            (1, ring, 1, row_count, last), lambda b: (1 - b // 2, 0, b % 2, 0, 0)
        )

    def whole(v):
        return pl.BlockSpec(v.shape, lambda b: (0,) * v.ndim)

    in_specs = [
        rows_spec(v.shape[-1])
        if kind == "rows"
        else pl.BlockSpec((1,) + v.shape[1:], lambda b: ((1 - b // 2) * micro + b % 2, 0, 0))
        if kind == "bias"
        else pl.BlockSpec(memory_space=pl.ANY)
        if kind == "token"
        else whole(v)
        for v, kind in zip(operands, extra)
    ]
    out_shape, out_specs = [], []
    for kind, last, dtype in outputs:
        if kind == "rows":
            out_shape.append(jax.ShapeDtypeStruct((2, ring, micro, row_count, last), dtype))
            out_specs.append(rows_spec(last))
        elif kind == "parts":
            one = jax.ShapeDtypeStruct((1, ring, micro, row_count, last), dtype)
            out_shape += [one, one]
            block = (1, ring, 1, row_count, last)
            out_specs.append(pl.BlockSpec(block, lambda b: (0, 0, jnp.minimum(b, 1), 0, 0)))
            out_specs.append(pl.BlockSpec(block, lambda b: (0, 0, jnp.maximum(b - 2, 0), 0, 0)))
        else:
            out_shape.append(jax.ShapeDtypeStruct((8, last), dtype))
            out_specs.append(pl.BlockSpec((8, last), lambda b: (0, 0)))
    return pl.pallas_call(
        kernel,
        grid=(2 * micro,),
        in_specs=in_specs,
        out_specs=out_specs,
        out_shape=out_shape,
        scratch_shapes=scratch,
        compiler_params=pltpu.CompilerParams(vmem_limit_bytes=VMEM),
        cost_estimate=TINY,
        name=name,
    )(*operands)


def experts_kernel(
    part, h2_ref, dy_ref, w_ref, spread_ref, dg_ref, du_ref, hid_ref, theirs_ref, mine_ref, acc
):
    chunk, block = pl.program_id(0), pl.program_id(1)
    width = h2_ref.shape[1]
    count = w_ref.shape[0] * part
    gate_w = w_ref[:, :part].reshape(count, width)
    up_w = w_ref[:, part : 2 * part].reshape(count, width)
    down_w = w_ref[:, 2 * part :].reshape(count, width)
    h2 = h2_ref[...]
    mix = matmul(dy_ref[:, width:], spread_ref[...])
    gate = against(h2, gate_w)
    up = against(h2, up_w)
    d_hidden = against(dy_ref[:, :width], down_w) * mix
    sigma = jax.nn.sigmoid(gate)
    silu = gate * sigma
    hid_ref[...] = (silu * up * mix).astype(BF16)
    d_gate = (d_hidden * up * sigma * (1.0 + gate * (1.0 - sigma))).astype(BF16)
    d_up = (d_hidden * silu).astype(BF16)
    dg_ref[...] = d_gate
    du_ref[...] = d_up
    total = matmul(d_gate, gate_w) + matmul(d_up, up_w)

    @pl.when(chunk == 0)
    def _():
        acc[block] = total

    @pl.when((chunk == 1) & (block < 2))
    def _():
        theirs_ref[...] = (acc[block] + total).astype(BF16)

    @pl.when((chunk == 1) & (block >= 2))
    def _():
        mine_ref[...] = (acc[block] + total).astype(BF16)


def experts_call(h2, dy, weights, spread, part):
    rows, width = h2.shape
    owners, depth, _ = weights.shape
    hidden = owners * part
    n, blocks = 2, 4
    step, wide = rows // blocks, hidden // n
    half = jax.ShapeDtypeStruct((rows // 2, width), BF16)
    wide_shape = jax.ShapeDtypeStruct((rows, hidden), BF16)

    def row(c, b):
        return (b + blocks // 2) % blocks

    wide_spec = pl.BlockSpec((step, wide), lambda c, b: (row(c, b), c))
    return pl.pallas_call(
        functools.partial(experts_kernel, part),
        grid=(n, blocks),
        in_specs=[
            pl.BlockSpec((step, width), lambda c, b: (row(c, b), 0)),
            pl.BlockSpec((step, dy.shape[1]), lambda c, b: (row(c, b), 0)),
            pl.BlockSpec((owners // n, depth, width), lambda c, b: (c, 0, 0)),
            pl.BlockSpec((spread.shape[0], wide), lambda c, b: (0, c)),
        ],
        out_specs=[
            wide_spec,
            wide_spec,
            wide_spec,
            pl.BlockSpec((step, width), lambda c, b: (c * jnp.minimum(b, 1), 0)),
            pl.BlockSpec((step, width), lambda c, b: (c * jnp.maximum(b - 2, 0), 0)),
        ],
        out_shape=[wide_shape, wide_shape, wide_shape, half, half],
        scratch_shapes=[pltpu.VMEM((blocks, step, width), F32)],
        compiler_params=pltpu.CompilerParams(vmem_limit_bytes=VMEM),
        cost_estimate=TINY,
        name="experts_rows",
    )(h2, dy, weights, spread)


def expert_grads_kernel(
    part, dg_ref, du_ref, hid_ref, h2_ref, dy_ref, after_ref, out_ref, token_ref
):
    width = h2_ref.shape[1]
    group = out_ref.shape[0]
    h2 = h2_ref[...]
    out_ref[:, :part] = outer(dg_ref[...], h2).astype(BF16).reshape(group, part, width)
    out_ref[:, part : 2 * part] = outer(du_ref[...], h2).astype(BF16).reshape(group, part, width)
    out_ref[:, 2 * part :] = (
        outer(hid_ref[...], dy_ref[:, :width]).astype(BF16).reshape(group, part, width)
    )
    token_ref[...] = jnp.zeros_like(token_ref)


def expert_grads_call(d_gate, d_up, hidden, h2, dy, after, owners, part):
    rows, width = h2.shape
    n = 4
    wide = d_gate.shape[1] // n
    wide_spec = pl.BlockSpec((rows, wide), lambda c: (0, c))
    return pl.pallas_call(
        functools.partial(expert_grads_kernel, part),
        grid=(n,),
        in_specs=[
            wide_spec,
            wide_spec,
            wide_spec,
            pl.BlockSpec((rows, width), lambda c: (0, 0)),
            pl.BlockSpec((rows, dy.shape[1]), lambda c: (0, 0)),
            pl.BlockSpec(memory_space=pl.ANY),
        ],
        out_specs=[
            pl.BlockSpec((owners // n, 3 * part, width), lambda c: (c, 0, 0)),
            pl.BlockSpec((8, 128), lambda c: (0, 0)),
        ],
        out_shape=[
            jax.ShapeDtypeStruct((owners, 3 * part, width), BF16),
            jax.ShapeDtypeStruct((8, 128), F32),
        ],
        compiler_params=pltpu.CompilerParams(vmem_limit_bytes=VMEM),
        cost_estimate=TINY,
        name="experts_weights",
    )(d_gate, d_up, hidden, h2, dy, after)


def add_kernel(theirs_ref, mine_ref, token_ref, *out_refs):
    for k, out_ref in enumerate(out_refs):
        out_ref[...] = (theirs_ref[k].astype(F32) + mine_ref[k].astype(F32)).astype(BF16)


def add_call(theirs, mine, token):
    shape = theirs.shape
    one = jax.ShapeDtypeStruct(shape[1:], BF16)
    vmem = pl.BlockSpec(memory_space=pltpu.VMEM)
    return pl.pallas_call(
        add_kernel,
        in_specs=[vmem, vmem, pl.BlockSpec(memory_space=pl.ANY)],
        out_specs=[vmem] * shape[0],
        out_shape=[one] * shape[0],
        compiler_params=pltpu.CompilerParams(vmem_limit_bytes=VMEM),
        cost_estimate=TINY,
        name="add_cores",
    )(theirs, mine, token)


def gate_up_down_kernel(part, in_ref, gate_ref, up_ref, down_ref):
    last = in_ref.shape[2]
    count = in_ref.shape[0] * part
    gate_ref[...] = in_ref[:, :part].reshape(count, last).astype(F32).T
    up_ref[...] = in_ref[:, part : 2 * part].reshape(count, last).astype(F32).T
    down_ref[...] = in_ref[:, 2 * part :].reshape(count, last).astype(F32)


def gate_up_down_call(gathered, part):
    members, depth, width = gathered.shape
    ff = members * part
    n = 8
    step = width // n
    return pl.pallas_call(
        functools.partial(gate_up_down_kernel, part),
        grid=(n,),
        in_specs=[pl.BlockSpec((members, depth, step), lambda c: (0, 0, c))],
        out_specs=[
            pl.BlockSpec((step, ff), lambda c: (c, 0)),
            pl.BlockSpec((step, ff), lambda c: (c, 0)),
            pl.BlockSpec((ff, step), lambda c: (0, c)),
        ],
        out_shape=[
            jax.ShapeDtypeStruct((width, ff), F32),
            jax.ShapeDtypeStruct((width, ff), F32),
            jax.ShapeDtypeStruct((ff, width), F32),
        ],
        compiler_params=pltpu.CompilerParams(vmem_limit_bytes=VMEM),
        cost_estimate=TINY,
        name="experts_results",
    )(gathered)


def attend_grads_kernel(
    cut, place_ref, h1_ref, d_qkv_ref, out_ref, gains_ref, token_ref, *refs
):
    firsts, seconds, share = refs[:SIDE], refs[SIDE : 2 * SIDE], refs[-1]
    step = pl.program_id(0)
    last = d_qkv_ref.shape[1]
    depth = share.shape[1] - 16
    grad = outer(h1_ref[...], d_qkv_ref[...]).astype(BF16)
    share[:, :depth, :last] = grad.reshape(SIDE, depth, last)
    rows, columns = out_ref.shape[1], share.shape[2] - last
    for k in range(depth // rows):
        share[:, k * rows : (k + 1) * rows, last:] = out_ref[:, :, k * columns : (k + 1) * columns]
    share[:, depth:] = gains_ref[...]
    for k in range(SIDE):

        @pl.when(step == k)
        def _():
            firsts[k][...] = share[:, :cut]

        seconds[k][0] = share[lax.rem(place_ref[1] + k, SIDE), cut:]


def attend_grads_call(place, h1, d_qkv, grad_out, gains, token, cut):
    rows, width = h1.shape
    owners, extra, columns = gains.shape
    depth = width // owners
    last = d_qkv.shape[1]

    def at(i, place):
        return lax.rem(place[0] + i, SIDE)

    first = jax.ShapeDtypeStruct((SIDE, cut, columns), BF16)
    second = jax.ShapeDtypeStruct((SIDE, depth + extra - cut, columns), BF16)
    outs = pl.pallas_call(
        functools.partial(attend_grads_kernel, cut),
        grid_spec=pltpu.PrefetchScalarGridSpec(
            num_scalar_prefetch=1,
            grid=(SIDE,),
            in_specs=[
                pl.BlockSpec((rows, width // SIDE), lambda i, place: (0, at(i, place))),
                pl.BlockSpec((rows, last), lambda i, place: (0, 0)),
                pl.BlockSpec((SIDE,) + grad_out.shape[1:], lambda i, place: (at(i, place), 0, 0)),
                pl.BlockSpec((SIDE, extra, columns), lambda i, place: (at(i, place), 0, 0)),
                pl.BlockSpec(memory_space=pl.ANY),
            ],
            out_specs=[pl.BlockSpec(first.shape, lambda i, place: (0, 0, 0))] * SIDE
            + [pl.BlockSpec((1,) + second.shape[1:], lambda i, place: (i, 0, 0))] * SIDE,
            scratch_shapes=[pltpu.VMEM((SIDE, depth + extra, columns), BF16)],
        ),
        out_shape=[first] * SIDE + [second] * SIDE,
        compiler_params=pltpu.CompilerParams(vmem_limit_bytes=VMEM),
        cost_estimate=TINY,
        name="attention_weights",
    )(place, h1, d_qkv, grad_out, gains, token)
    return outs[:SIDE], outs[SIDE:]


def total_of(refs):
    total = refs[0][...].astype(F32)
    for ref in refs[1:]:
        total = total + ref[...].astype(F32)
    return total.astype(BF16)


def half_sum_kernel(place_ref, *refs):
    firsts, seconds, total = refs[2 * SIDE : 3 * SIDE], refs[3 * SIDE : 4 * SIDE], refs[-1]
    total[...] = total_of(refs[:SIDE])
    other = total_of(refs[SIDE : 2 * SIDE])
    for k in range(SIDE):
        firsts[k][...] = total[lax.rem(place_ref[1] + k, SIDE)]
        seconds[k][...] = other[k]


def half_sum_call(place, firsts, seconds):
    vmem = pl.BlockSpec(memory_space=pltpu.VMEM)
    outs = pl.pallas_call(
        half_sum_kernel,
        grid_spec=pltpu.PrefetchScalarGridSpec(
            num_scalar_prefetch=1,
            grid=(),
            in_specs=[vmem] * (2 * SIDE),
            out_specs=[vmem] * (2 * SIDE),
            scratch_shapes=[pltpu.VMEM(firsts[0].shape, BF16)],
        ),
        out_shape=[jax.ShapeDtypeStruct(v.shape[1:], BF16) for v in (*firsts, *seconds)],
        compiler_params=pltpu.CompilerParams(vmem_limit_bytes=VMEM),
        cost_estimate=TINY,
        name="half_sum",
    )(place, *firsts, *seconds)
    return outs[:SIDE], outs[SIDE:]


def last_sum_kernel(*refs):
    out = refs[-1]
    cut = refs[0].shape[0]
    out[:cut] = total_of(refs[:SIDE])
    out[cut:] = total_of(refs[SIDE : 2 * SIDE])


def last_sum_call(firsts, seconds):
    rows, columns = firsts[0].shape[0] + seconds[0].shape[0], firsts[0].shape[1]
    vmem = pl.BlockSpec(memory_space=pltpu.VMEM)
    return pl.pallas_call(
        last_sum_kernel,
        in_specs=[vmem] * (2 * SIDE),
        out_specs=vmem,
        out_shape=jax.ShapeDtypeStruct((rows, columns), BF16),
        compiler_params=pltpu.CompilerParams(vmem_limit_bytes=VMEM),
        cost_estimate=TINY,
        name="last_sum",
    )(*firsts, *seconds)


def plane_send(pieces, dx, dz):
    return [pieces[0]] + [plane(pieces[k], -k * dx, -k * dz) for k in range(1, SIDE)]


def columns_kernel(
    heads_width, size, where_ref, mine_ref, theirs_ref, q_ref, k_ref, v_ref, out_ref, sum_ref
):
    depth = q_ref.shape[0]
    last = heads_width + 2 * size
    mine, theirs = mine_ref[0].astype(F32), theirs_ref[0].astype(F32)
    first = where_ref[1] == 0
    low, high = jnp.where(first, mine, theirs), jnp.where(first, theirs, mine)
    q_ref[:, :heads_width] = low[:depth, :heads_width]
    q_ref[:, heads_width:] = high[:depth, :heads_width]
    both = mine + theirs
    k_ref[...] = both[:depth, heads_width : heads_width + size]
    v_ref[...] = both[:depth, heads_width + size : last]
    columns = mine.shape[1] - last
    rows = out_ref.shape[0] // 2
    for k in range(depth // rows):
        out_ref[:rows, k * columns : (k + 1) * columns] = low[k * rows : (k + 1) * rows, last:]
        out_ref[rows:, k * columns : (k + 1) * columns] = high[k * rows : (k + 1) * rows, last:]

    @pl.when(pl.program_id(0) == 0)
    def _():
        sum_ref[...] = jnp.zeros_like(sum_ref)

    sum_ref[...] += both[depth:]


def columns_call(where, mine, theirs, depth, heads_width, size, out_rows, width):
    ring, rows, last = mine.shape
    cores = 2

    def at(k, where):
        return (0, lax.rem(where[0] + k, ring))

    def row_at(k, where):
        return (lax.rem(where[0] + k, ring), 0)

    return pl.pallas_call(
        functools.partial(columns_kernel, heads_width, size),
        grid_spec=pltpu.PrefetchScalarGridSpec(
            num_scalar_prefetch=1,
            grid=(ring,),
            in_specs=[pl.BlockSpec((1, rows, last), lambda k, where: (k, 0, 0))] * 2,
            out_specs=[
                pl.BlockSpec((depth, cores * heads_width), at),
                pl.BlockSpec((depth, size), at),
                pl.BlockSpec((depth, size), at),
                pl.BlockSpec((out_rows // ring, width), row_at),
                pl.BlockSpec((rows - depth, last), lambda k, where: (0, 0)),
            ],
        ),
        out_shape=[
            jax.ShapeDtypeStruct((depth, ring * cores * heads_width), F32),
            jax.ShapeDtypeStruct((depth, ring * size), F32),
            jax.ShapeDtypeStruct((depth, ring * size), F32),
            jax.ShapeDtypeStruct((out_rows, width), F32),
            jax.ShapeDtypeStruct((rows - depth, last), F32),
        ],
        compiler_params=pltpu.CompilerParams(vmem_limit_bytes=VMEM),
        cost_estimate=TINY,
        name="attention_results",
    )(where, mine, theirs)


def expert_out_kernel(part, hid_ref, w_ref, token_ref, theirs_ref, mine_ref):
    width = w_ref.shape[2]
    block = pl.program_id(0)
    total = matmul(hid_ref[...], w_ref[...].reshape(w_ref.shape[0] * part, width)).astype(BF16)

    @pl.when(block < 2)
    def _():
        theirs_ref[...] = total

    @pl.when(block >= 2)
    def _():
        mine_ref[...] = total


def expert_out_call(hidden, weights, token, part):
    rows, wide = hidden.shape
    owners, _, width = weights.shape
    blocks = 4
    step = rows // blocks
    half = jax.ShapeDtypeStruct((rows // 2, width), BF16)
    return pl.pallas_call(
        functools.partial(expert_out_kernel, part),
        grid=(blocks,),
        in_specs=[
            pl.BlockSpec((step, wide), lambda b: ((b + blocks // 2) % blocks, 0)),
            pl.BlockSpec((owners, part, width), lambda b: (0, 2, 0)),
            pl.BlockSpec(memory_space=pl.ANY),
        ],
        out_specs=[
            pl.BlockSpec((step, width), lambda b: (jnp.minimum(b, 1), 0)),
            pl.BlockSpec((step, width), lambda b: (jnp.maximum(b - 2, 0), 0)),
        ],
        out_shape=[half, half],
        compiler_params=pltpu.CompilerParams(vmem_limit_bytes=VMEM),
        cost_estimate=TINY,
        name="experts_out",
    )(hidden, weights, token)


def local(
    tokens,
    lengths,
    routes,
    mix_weights,
    cotangent,
    w_query,
    key_weight,
    value_weight,
    w_out,
    norm_attn,
    norm_moe,
    norm_query,
    norm_key,
    w_gate,
    w_up,
    w_down,
):
    owners = lax.axis_size("experts")
    ring = lax.axis_size("context")
    cores = lax.axis_size("dp")
    members = ring * cores
    y = lax.axis_index("context")
    d = lax.axis_index("dp")
    j = y * cores + d
    micro, _, row_count, width = tokens.shape
    head = norm_query.shape[0] * owners
    q_width = w_query.shape[1] // members
    q_heads = q_width // head
    depth = w_query.shape[0]
    ff = w_gate.shape[2]
    ff_part = ff // members
    out_rows = w_out.shape[0]
    out_part = out_rows // members
    seqs = cores * micro
    span = ring * row_count
    rows = seqs * span
    scale = head ** (-0.5)

    forth = [
        (es * members + k, ((es % cores) * members + k) * members + es // cores)
        for es in range(owners)
        for k in range(members)
    ]
    back = [(b, a) for a, b in forth]
    out_chunk = lax.ppermute(
        lax.dynamic_slice_in_dim(w_out, j * out_part, out_part, axis=0), EVERY, forth
    )
    expert_pack = jnp.concatenate(
        [
            lax.dynamic_slice_in_dim(w_gate[0], j * ff_part, ff_part, axis=1).T,
            lax.dynamic_slice_in_dim(w_up[0], j * ff_part, ff_part, axis=1).T,
            lax.dynamic_slice_in_dim(w_down[0], j * ff_part, ff_part, axis=0),
        ],
        axis=0,
    )
    gains = jnp.concatenate([norm_attn, norm_moe, norm_query, norm_key])
    packed = jnp.concatenate(
        [
            lax.dynamic_slice_in_dim(w_query, j * q_width, q_width, axis=1),
            lax.dynamic_slice_in_dim(key_weight, y * head, head, axis=1),
            lax.dynamic_slice_in_dim(value_weight, y * head, head, axis=1),
            jnp.concatenate(jnp.split(out_chunk, depth // out_part, axis=1), axis=0),
        ],
        axis=1,
    )
    qkv_width = q_width + 2 * head
    gain_rows = jnp.pad(gains[None], ((0, 15), (0, packed.shape[1] - gains.shape[0])))
    shared = lax.all_gather(
        jnp.concatenate([packed, gain_rows]), "experts", axis=0, tiled=False
    )
    expert_all = lax.all_gather(expert_pack, "experts", axis=0, tiled=False)
    gain_row = shared[:, depth]
    gain_row = gain_row.astype(F32)
    gain_attn = gain_row[:, :depth].reshape(-1)
    gain_moe = gain_row[:, depth : 2 * depth].reshape(-1)
    eighth = norm_query.shape[0]
    gain_query = gain_row[:, 2 * depth : 2 * depth + eighth].reshape(-1)
    gain_key = gain_row[:, 2 * depth + eighth : 2 * depth + 2 * eighth].reshape(-1)
    hidden_width = owners * ff_part

    x_own = tokens[:, 0]
    x_rows = gather_rows(x_own, ring)
    len_all = jnp.stack([lengths[:, 0], swap(lengths[:, 0])]).reshape(seqs)
    own_pos = y * row_count + jnp.arange(row_count, dtype=jnp.int32)
    valid = (own_pos[None, :] < lengths[:, 0][:, None]).astype(F32)
    dy_own = (cotangent[:, 0].astype(F32) * valid[:, :, None]).astype(BF16)
    ids = jnp.arange(owners, dtype=jnp.int32)
    mix_own = jnp.sum(
        jnp.where(routes[:, 0][..., None] == ids, mix_weights[:, 0][..., None], 0.0), axis=2
    )
    mix_high = mix_own.astype(BF16)
    mix_low = (mix_own - mix_high.astype(F32)).astype(BF16)
    lanes = 128
    mix_pad = jnp.zeros((micro, row_count, lanes - 2 * owners), BF16)
    dy_mix = gather_rows(jnp.concatenate([dy_own, mix_high, mix_low, mix_pad], axis=-1), ring)
    dy_mix = dy_mix.reshape(rows, width + lanes)
    lane = jnp.arange(lanes, dtype=jnp.int32)
    spread = (
        (jnp.arange(hidden_width, dtype=jnp.int32)[None, :] // ff_part == (lane % owners)[:, None])
        & (lane < 2 * owners)[:, None]
    ).astype(BF16)

    k_index = jnp.arange(span, dtype=jnp.int32)
    pos = ((y + k_index // row_count) % ring) * row_count + k_index % row_count
    frequency = ROPE_BASE ** (-jnp.arange(head // 2, dtype=F32) * 2.0 / head)
    phase = pos.astype(F32)[:, None] * frequency[None, :]
    cosines, sines = jnp.cos(phase), jnp.sin(phase)
    cosines = jnp.concatenate([cosines, cosines], axis=1)
    sines = jnp.concatenate([-sines, sines], axis=1)
    allowed = (pos[None, None, :] <= pos[None, :, None]) & (
        pos[None, None, :] < len_all[:, None, None]
    )
    bias = jnp.where(allowed, 0.0, -1e30).astype(F32)

    shape = (ring, micro, row_count, width)
    head_gains = (gain_query[None], gain_key[None])
    h1, qkv, heads_out, theirs, mine = attend_call(
        functools.partial(attend_kernel, q_heads, scale),
        (x_rows, gain_attn[None], shared, cosines, sines, bias, *head_gains, dy_mix),
        ("rows", "", "", "", "", "bias", "", "", "token"),
        (
            ("rows", width, BF16),
            ("rows", qkv_width, F32),
            ("rows", q_width, BF16),
            ("parts", width, BF16),
        ),
        [pltpu.VMEM((span, q_width), BF16), pltpu.VMEM((span, width), BF16)],
        shape,
        "attention",
        6_000_000_000,
    )
    attn_own = scatter_rows(theirs[0], mine[0])
    x1 = x_own.astype(F32) + attn_own
    inverse_mid = inverse_rms(x1)
    h2 = gather_rows((x1 * inverse_mid * gain_moe).astype(BF16), ring).reshape(rows, width)

    d_gate, d_up, hidden, theirs, mine = experts_call(h2, dy_mix, expert_all, spread, ff_part)
    pieces = add_call(swap(theirs.reshape(shape)), mine.reshape(shape), d_gate)
    d_h2 = ring_sum(pieces)
    grad_experts, token = expert_grads_call(
        d_gate, d_up, hidden, h2, dy_mix, pieces[1], owners, ff_part
    )
    moe_theirs, moe_mine = expert_out_call(hidden, expert_all, token, ff_part)

    grad_gain_moe = jnp.sum(d_h2 * x1 * inverse_mid, axis=(0, 1))
    d_x1 = dy_own.astype(F32) + norm_back(d_h2, x1, inverse_mid, gain_moe)
    grad_experts = lax.psum_scatter(
        after_call(grad_experts, d_x1), "experts", scatter_dimension=0, tiled=False
    )
    d_attn = gather_rows(d_x1.astype(BF16), ring)
    moe_pieces = add_call(swap(moe_theirs.reshape(shape)), moe_mine.reshape(shape), d_attn)
    output = (x1 + ring_sum(moe_pieces)).astype(BF16)[:, None]
    grad_out = outer(heads_out.reshape(rows, q_width), d_attn.reshape(rows, width)).astype(BF16)
    grad_out = grad_out.reshape(owners, out_part, width)
    d_qkv, theirs, mine, sum_q, sum_k, sum_x = attend_call(
        functools.partial(attend_back_kernel, q_heads, scale),
        (
            d_attn,
            x_rows,
            gain_attn[None],
            shared,
            cosines,
            sines,
            bias,
            *head_gains,
            qkv,
            moe_pieces[0],
            grad_out,
        ),
        ("rows", "rows", "", "", "", "", "bias", "", "", "rows", "token", "token"),
        (
            ("rows", qkv_width, BF16),
            ("parts", width, BF16),
            ("sum", head, F32),
            ("sum", head, F32),
            ("sum", width, F32),
        ),
        [pltpu.VMEM((span, qkv_width), BF16)],
        shape,
        "attention_back",
        9_000_000_000,
    )
    grad_gain_query, grad_gain_key, grad_gain_attn = sum_q[0], sum_k[0], sum_x[0]
    d_h1 = scatter_rows(theirs[0], mine[0])
    x_f32 = x_own.astype(F32)
    input_grad = (d_x1 + norm_back(d_h1, x_f32, inverse_rms(x_f32), gain_attn))[:, None]
    h1, d_qkv = h1.reshape(rows, width), d_qkv.reshape(rows, qkv_width)

    where = jnp.stack([y, d]).astype(jnp.int32)
    grad_gains = jnp.concatenate(
        [
            grad_gain_attn.reshape(owners, depth),
            grad_gain_moe.reshape(owners, depth),
            grad_gain_query.reshape(owners, eighth),
            grad_gain_key.reshape(owners, eighth),
        ],
        axis=1,
    ).astype(BF16)
    grad_gains = jnp.pad(
        grad_gains[:, None], ((0, 0), (0, 15), (0, shared.shape[2] - grad_gains.shape[1]))
    )
    index = lax.axis_index("experts")
    place = jnp.stack([index // SIDE, index % SIDE]).astype(jnp.int32)
    firsts, seconds = attend_grads_call(
        place, h1, d_qkv, grad_out, grad_gains, output, depth // 2 + 16
    )
    firsts, seconds = half_sum_call(
        place, plane_send(firsts, 1, 0), plane_send(seconds, 0, 1)
    )
    grads = last_sum_call(plane_send(firsts, 0, 1), plane_send(seconds, 1, 0))
    out_back = lax.ppermute(grads[:depth, qkv_width:], EVERY, back)
    grads = jnp.concatenate(
        [grads[:, :qkv_width], jnp.pad(out_back, ((0, 16), (0, 0)))], axis=1
    )
    result_q, result_k, result_v, result_out, gain_sum = columns_call(
        where, *gather_members(grads), depth, q_width, head, w_out.shape[0], width
    )
    gain_sum = gain_sum[0]
    grad_experts = after_call(grad_experts, seconds[1])
    all_experts = lax.all_gather(grad_experts, GROUP, axis=0, tiled=False)
    result_gate, result_up, result_down = gate_up_down_call(all_experts, ff_part)
    return (
        output,
        input_grad,
        result_q,
        result_k,
        result_v,
        result_out,
        gain_sum[:depth],
        gain_sum[depth : 2 * depth],
        gain_sum[2 * depth : 2 * depth + eighth],
        gain_sum[2 * depth + eighth : 2 * depth + 2 * eighth],
        result_gate[None],
        result_up[None],
        result_down[None],
    )


def solution(mesh):
    rows = P(None, ("experts", "dp"), "context", None)
    in_specs = (
        rows,
        P(None, ("experts", "dp")),
        rows,
        rows,
        rows,
        P("experts", None),
        P("experts", None),
        P("experts", None),
        P("experts", None),
        P("experts"),
        P("experts"),
        P("experts"),
        P("experts"),
        P("experts", None, None),
        P("experts", None, None),
        P("experts", None, None),
    )
    out_specs = (
        rows,
        rows,
        P("experts", None),
        P("experts", None),
        P("experts", None),
        P("experts", None),
        P("experts"),
        P("experts"),
        P("experts"),
        P("experts"),
        P("experts", None, None),
        P("experts", None, None),
        P("experts", None, None),
    )
    return jax.shard_map(local, mesh=mesh, in_specs=in_specs, out_specs=out_specs, check_vma=False)
```

time: 1400 us -> 601 us (0.43)
  the two profiles are of different devices: /device:TPU:49 before, /device:TPU:4 now
where the time goes in v1:
time: 601 us; the launch traced here: 591 us
  waiting for transfers between devices  239 us (40%)
  Pallas kernels  179 us (30%)
  starting transfers between devices  77.5 us (13%)
  other arithmetic  53.5 us (9%)
  local copies, waits for them, and re-layouts  21.5 us (4%)
  between operations  14.8 us (2%)
    ppermute x12, waiting for transfers between devices, gather_rows(): lax.ppermute(own, 'context', [((i + k) % ring, i) for i in range(ring)])  82.7 us
    ppermute x12, waiting for transfers between devices, ring_sum(): lax.ppermute(pieces[k], 'context', [(i, (i + k) % ring) for i in range(ri...  49.2 us
    pallas_call x1, Pallas kernels, experts_call(): pl.pallas_call(functools.partial(experts_kernel, part), grid=(n, blocks),...  48.9 us
    pallas_call x2, Pallas kernels, attend_call(): pl.pallas_call(kernel, grid=(2 * micro,), in_specs=in_specs, out_specs=ou...  48 us
    ppermute x12, waiting for transfers between devices, plane(): return lax.ppermute(v, 'experts', moves)  45.7 us
    pallas_call x1, Pallas kernels, expert_grads_call(): pl.pallas_call(functools.partial(expert_grads_kernel, part), grid=(n,), i...  27 us
    ppermute x3, waiting for transfers between devices, gather_members(): lax.ppermute(v, 'context', [((i + k) % ring, i) for i in range(ring)])  25.6 us
    another operation x8, other arithmetic, gather_rows(): return jnp.stack([mine, swap(mine)])  24.4 us
  transfers between devices with their start and end apart: 55, of which 29 were waited for; matrix products, arithmetic and copies ran while one was open for 12% of the time, Pallas kernels for 19%

profile of v1, /device:TPU:4, one launch (start us, length us, event | category | flops | bytes accessed | tf_op | source)
XLA Modules:
  0.0 590.9 jit_solution(3104948744771208731)
XLA Ops:
  8.3 5.0 collective-permute-start.4
  38.9 8.6 %collective-permute-done.2 = bf16[2,64,2048]{2,1,0:T(8,128)(2,1)S(1)} collective-permute-done((bf16[2,64,2048]{2,1,0:T(8,128)(2,1)S(1)}, bf16[2,64,2048]{2,1,0:T(8,128)(2,1)S(1)}, u32[]{:S(2)}, u32[]{:S(2)}) %collective-permute-start.2) | collective-permute-done | bytes 524320 | tf_op jit(solution)/shard_map/ppermute | solution.py:49
  47.9 10.7 %collective-permute-done.1 = bf16[2,64,2048]{2,1,0:T(8,128)(2,1)S(1)} collective-permute-done((bf16[2,64,2048]{2,1,0:T(8,128)(2,1)S(1)}, bf16[2,64,2048]{2,1,0:T(8,128)(2,1)S(1)}, u32[]{:S(2)}, u32[]{:S(2)}) %collective-permute-start.1) | collective-permute-done | bytes 524320 | tf_op jit(solution)/shard_map/ppermute | solution.py:49
  62.0 6.1 %collective-permute-done.8 = bf16[2,64,2176]{2,1,0:T(8,128)(2,1)S(1)} collective-permute-done((bf16[2,64,2176]{2,1,0:T(8,128)(2,1)S(1)}, bf16[2,64,2176]{2,1,0:T(8,128)(2,1)S(1)}, u32[]{:S(2)}, u32[]{:S(2)}) %collective-permute-start.8) | collective-permute-done | bytes 557088 | tf_op jit(solution)/shard_map/ppermute | solution.py:49
  68.1 12.8 %collective-permute-done.7 = bf16[2,64,2176]{2,1,0:T(8,128)(2,1)S(1)} collective-permute-done((bf16[2,64,2176]{2,1,0:T(8,128)(2,1)S(1)}, bf16[2,64,2176]{2,1,0:T(8,128)(2,1)S(1)}, u32[]{:S(2)}, u32[]{:S(2)}) %collective-permute-start.7) | collective-permute-done | bytes 557088 | tf_op jit(solution)/shard_map/ppermute | solution.py:49
  89.0 4.6 pad_maximum_fusion.1.x_ref
  93.6 4.2 pad_maximum_fusion
  100.7 21.9 %attention.1 = (bf16[2,4,2,64,2048]{4,3,2,1,0:T(8,128)(2,1)}, f32[2,4,2,64,768]{4,3,2,1,0:T(8,128)}, bf16[2,4,2,64,512]{4,3,2,1,0:T(8,128)(2,1)}, bf16[1,4,2,64,...) custom-call(bf16[2,4,2,64,2048]{4,3,2,1,0:T(8,128)(2,1)} %pad_maximum_fusion.1.x_ref, f32[1,2048]{1,0:T(1,128)} %bitcast.235, ...), custom_call_target="tpu_custom_call" | custom-call | bytes 1000 | tf_op jit(solution)/shard_map/attention/pallas_call | solution.py:313
  133.4 21.2 %collective-permute-done.13 = bf16[2,64,2048]{2,1,0:T(8,128)(2,1)S(1)} collective-permute-done((bf16[2,64,2048]{2,1,0:T(8,128)(2,1)S(1)}, bf16[2,64,2048]{2,1,0:T(8,128)(2,1)S(1)}, u32[]{:S(2)}, u32[]{:S(2)}) %collective-permute-start.13) | collective-permute-done | bytes 524320 | tf_op jit(solution)/shard_map/ppermute | solution.py:58
  164.2 22.3 %collective-permute-done.16 = bf16[2,64,2048]{2,1,0:T(8,128)(2,1)S(1)} collective-permute-done((bf16[2,64,2048]{2,1,0:T(8,128)(2,1)S(1)}, bf16[2,64,2048]{2,1,0:T(8,128)(2,1)S(1)}, u32[]{:S(2)}, u32[]{:S(2)}) %collective-permute-start.16) | collective-permute-done | bytes 524320 | tf_op jit(solution)/shard_map/ppermute | solution.py:49
  194.1 15.5 %all-gather.9.cloned.1.call-done = bf16[4608,2048]{1,0:T(8,128)(2,1)} async-done(((bf16[288,2048]{1,0:T(8,128)(2,1)}), bf16[4608,2048]{1,0:T(8,128)(2,1)}) %all-gather.9.cloned.1.call-update) | async-done | bytes 18874384 | tf_op jit(solution)/shard_map/all_gather | solution.py:786
  209.6 48.9 %experts_rows.1 = (bf16[1024,1536]{1,0:T(8,128)(2,1)}, bf16[1024,1536]{1,0:T(8,128)(2,1)}, bf16[1024,1536]{1,0:T(8,128)(2,1)}, bf16[512,2048]{1,0:T(8,128)(2,1)}, bf16[512,2048]{1,0:T(8,128)(2,1)}) custom-call(bf16[1024,2048]{1,0:T(8,128)(2,1)} %bitcast.197, bf16[1024,2176]{1,0:T(8,128)(2,1)} %bitcast.195, bf16[16,288,2048]{2,1,0:T(8,128)(2,1)} %bitcast.192, ...), custom_call_target="tpu_custom_call" | custom-call | bytes 1000 | tf_op jit(solution)/shard_map/experts_rows/pallas_call | solution.py:375
  258.5 4.4 collective-permute-done.18.theirs_ref
  272.4 27.0 %experts_weights.1 = (bf16[16,288,2048]{2,1,0:T(8,128)(2,1)}, f32[8,128]{1,0:T(8,128)}) custom-call(bf16[1024,1536]{1,0:T(8,128)(2,1)} %get-tuple-element.68.token_ref.dg_ref, bf16[1024,1536]{1,0:T(8,128)(2,1)} %get-tuple-element.69.du_ref, bf16[1024,1536]{1,0:T(8,128)(2,1)} %get-tuple-element.67.hid_ref, bf16[1024,2048]{1,0:T(8,128)(2,1)} %bitcast.198, ...), custom_call_target="tpu_custom_call" | custom-call | bytes 1000 | tf_op jit(solution)/shard_map/experts_weights/pallas_call | solution.py:418
  308.1 10.9 %collective-permute-done.25 = bf16[2,64,2048]{2,1,0:T(8,128)(2,1)S(1)} collective-permute-done((bf16[2,64,2048]{2,1,0:T(8,128)(2,1)S(1)}, bf16[2,64,2048]{2,1,0:T(8,128)(2,1)S(1)}, u32[]{:S(2)}, u32[]{:S(2)}) %collective-permute-start.25) | collective-permute-done | bytes 524320 | tf_op jit(solution)/shard_map/ppermute | solution.py:49
  319.0 10.7 %collective-permute-done.24 = bf16[2,64,2048]{2,1,0:T(8,128)(2,1)S(1)} collective-permute-done((bf16[2,64,2048]{2,1,0:T(8,128)(2,1)S(1)}, bf16[2,64,2048]{2,1,0:T(8,128)(2,1)S(1)}, u32[]{:S(2)}, u32[]{:S(2)}) %collective-permute-start.24) | collective-permute-done | bytes 524320 | tf_op jit(solution)/shard_map/ppermute | solution.py:49
  332.4 12.5 %experts_out.1 = (bf16[512,2048]{1,0:T(8,128)(2,1)}, bf16[512,2048]{1,0:T(8,128)(2,1)}) custom-call(bf16[1024,1536]{1,0:T(8,128)(2,1)} %get-tuple-element.67.hid_ref, bf16[16,288,2048]{2,1,0:T(8,128)(2,1)} %bitcast.193, f32[8,128]{1,0:T(8,128)} %get-tuple-element.73.token_ref), custom_call_target="tpu_custom_call" | custom-call | bytes 1000 | tf_op jit(solution)/shard_map/experts_out/pallas_call | solution.py:696
  358.2 5.7 bitcast_convert_fusion
  363.8 26.0 %attention_back.1 = (bf16[2,4,2,64,768]{4,3,2,1,0:T(8,128)(2,1)}, bf16[1,4,2,64,2048]{4,3,2,1,0:T(8,128)(2,1)}, bf16[1,4,2,64,2048]{4,3,2,1,0:T(8,128)(2,1)}, f3...) custom-call(bf16[2,4,2,64,2048]{4,3,2,1,0:T(8,128)(2,1)} %pad_maximum_fusion.3.token_ref.da_ref, ...), custom_call_target="tpu_custom_call" | custom-call | bytes 1000 | tf_op jit(solution)/shard_map/attention_back/pallas_call | solution.py:313
  395.8 10.2 %attention_weights.1 = (bf16[4,80,1280]{2,1,0:T(8,128)(2,1)}, bf16[4,80,1280]{2,1,0:T(8,128)(2,1)}, bf16[4,80,1280]{2,1,0:T(8,128)(2,1)}, bf16[4,80,1280]{2,1,0:...) custom-call(s32[2]{0:T(128)} %pad_add_fusion.2.place_ref, ...), custom_call_target="tpu_custom_call" | custom-call | bytes 1000 | tf_op jit(solution)/shard_map/attention_weights/pallas_call | solution.py:529
  413.6 23.1 %collective-permute-done.37.refs_5_ = bf16[4,64,1280]{2,1,0:T(8,128)(2,1)S(1)} collective-permute-done((bf16[4,64,1280]{2,1,0:T(8,128)(2,1)}, bf16[4,64,1280]{2,1,0:T(8,128)(2,1)S(1)}, u32[]{:S(2)}, u32[]{:S(2)}) %collective-permute-start.37) | collective-permute-done | bytes 655392 | tf_op jit(solution)/shard_map/ppermute | solution.py:87
  438.0 12.6 %collective-permute-done.38.refs_6_ = bf16[4,64,1280]{2,1,0:T(8,128)(2,1)S(1)} collective-permute-done((bf16[4,64,1280]{2,1,0:T(8,128)(2,1)}, bf16[4,64,1280]{2,1,0:T(8,128)(2,1)S(1)}, u32[]{:S(2)}, u32[]{:S(2)}) %collective-permute-start.38) | collective-permute-done | bytes 655392 | tf_op jit(solution)/shard_map/ppermute | solution.py:87
  456.5 5.6 half_sum.1
  476.2 4.4 collective-permute-done.45.refs_7_
  484.9 6.6 %collective-permute-start.46 = (bf16[128,512]{1,0:T(8,128)(2,1)S(1)}, bf16[128,512]{1,0:T(8,128)(2,1)S(1)}, u32[]{:S(2)}, u32[]{:S(2)}) collective-permute-start(bf16[128,512]{1,0:T(8,128)(2,1)S(1)} %slice.167), channel_id=1, source_target_pairs={{0,0},{8,1},{16,2},{24,3},{32,4},{40,5},{48,6},{56,7},{64,8},{72,9... | collective-permute-start | bytes 393224 | tf_op jit(solution)/shard_map/ppermute | solution.py:926
  507.6 9.3 %collective-permute-done.49 = bf16[144,1280]{1,0:T(8,128)(2,1)S(1)} collective-permute-done((bf16[144,1280]{1,0:T(8,128)(2,1)S(1)}, bf16[144,1280]{1,0:T(8,128)(2,1)S(1)}, u32[]{:S(2)}, u32[]{:S(2)}) %collective-permute-start.49) | collective-permute-done | bytes 368672 | tf_op jit(solution)/shard_map/ppermute | solution.py:78
  518.2 16.3 %collective-permute-done.48 = bf16[144,1280]{1,0:T(8,128)(2,1)S(1)} collective-permute-done((bf16[144,1280]{1,0:T(8,128)(2,1)S(1)}, bf16[144,1280]{1,0:T(8,128)(2,1)S(1)}, u32[]{:S(2)}, u32[]{:S(2)}) %collective-permute-start.48) | collective-permute-done | bytes 368672 | tf_op jit(solution)/shard_map/ppermute | solution.py:78
  535.4 7.1 %collective-permute-done.33 = bf16[2,64,2048]{2,1,0:T(8,128)(2,1)S(1)} collective-permute-done((bf16[2,64,2048]{2,1,0:T(8,128)(2,1)S(1)}, bf16[2,64,2048]{2,1,0:T(8,128)(2,1)S(1)}, u32[]{:S(2)}, u32[]{:S(2)}) %collective-permute-start.33) | collective-permute-done | bytes 524320 | tf_op jit(solution)/shard_map/ppermute | solution.py:58
  542.5 6.5 %collective-permute-done.32 = bf16[2,64,2048]{2,1,0:T(8,128)(2,1)S(1)} collective-permute-done((bf16[2,64,2048]{2,1,0:T(8,128)(2,1)S(1)}, bf16[2,64,2048]{2,1,0:T(8,128)(2,1)S(1)}, u32[]{:S(2)}, u32[]{:S(2)}) %collective-permute-start.32) | collective-permute-done | bytes 524320 | tf_op jit(solution)/shard_map/ppermute | solution.py:58
  549.0 10.7 %collective-permute-done.31 = bf16[2,64,2048]{2,1,0:T(8,128)(2,1)S(1)} collective-permute-done((bf16[2,64,2048]{2,1,0:T(8,128)(2,1)S(1)}, bf16[2,64,2048]{2,1,0:T(8,128)(2,1)S(1)}, u32[]{:S(2)}, u32[]{:S(2)}) %collective-permute-start.31) | collective-permute-done | bytes 524320 | tf_op jit(solution)/shard_map/ppermute | solution.py:58
  564.2 5.3 attention_results.1
  572.1 11.8 %experts_results.1 = (f32[2048,768]{1,0:T(8,128)}, f32[2048,768]{1,0:T(8,128)}, f32[768,2048]{1,0:T(8,128)}) custom-call(bf16[8,288,2048]{2,1,0:T(8,128)(2,1)} %bitcast.202), custom_call_target="tpu_custom_call" | custom-call | bytes 1000 | tf_op jit(solution)/shard_map/experts_results/pallas_call | solution.py:476
  (244 shorter events, 167.5 us)
Async XLA Ops:
  7.2 90.6 %all-gather.7.cloned.1.call-start = ((), (), s32[]{:S(2)}) async-start(), calls=%async_computation.1 | async-start | bytes 6266880 | tf_op jit(solution)/shard_map/all_gather | solution.py:783
  19.8 189.8 %all-gather.9.cloned.1.call-start = ((), (), s32[]{:S(2)}) async-start(), calls=%async_computation.2 | async-start | bytes 20054016 | tf_op jit(solution)/shard_map/all_gather | solution.py:786
  28.3 433.8 %reduce-scatter.4.cloned.1.call-start = ((), (), s32[]{:S(2)}) async-start(), calls=%async_computation.4 | async-start | bytes 20054016
  32.3 26.4 %collective-permute-start.1 = (bf16[2,64,2048]{2,1,0:T(8,128)(2,1)S(1)}, bf16[2,64,2048]{2,1,0:T(8,128)(2,1)S(1)}, u32[]{:S(2)}, u32[]{:S(2)}) collective-permute-start(bf16[2,64,2048]{2,1,0:T(8,128)(2,1)S(1)} %bitcast.206), channel_id=1, source_target_pairs={{4,0},{6,2},{0,4},{2,6},{5,1},{7,3},{1,5},{3,7},{12,8},{14,10},{8,... | collective-permute-start | bytes 1572872 | tf_op jit(solution)/shard_map/ppermute | solution.py:49
  37.3 30.8 %collective-permute-start.8 = (bf16[2,64,2176]{2,1,0:T(8,128)(2,1)S(1)}, bf16[2,64,2176]{2,1,0:T(8,128)(2,1)S(1)}, u32[]{:S(2)}, u32[]{:S(2)}) collective-permute-start(bf16[2,64,2176]{2,1,0:T(8,128)(2,1)S(1)} %concatenate.52), channel_id=1, source_target_pairs={{6,0},{0,2},{2,4},{4,6},{7,1},{1,3},{3,5},{5,7},{14,8},{8,10},{10,... | collective-permute-start | bytes 1671176 | tf_op jit(solution)/shard_map/ppermute | solution.py:49
  37.4 43.5 %collective-permute-start.7 = (bf16[2,64,2176]{2,1,0:T(8,128)(2,1)S(1)}, bf16[2,64,2176]{2,1,0:T(8,128)(2,1)S(1)}, u32[]{:S(2)}, u32[]{:S(2)}) collective-permute-start(bf16[2,64,2176]{2,1,0:T(8,128)(2,1)S(1)} %concatenate.52), channel_id=1, source_target_pairs={{4,0},{6,2},{0,4},{2,6},{5,1},{7,3},{1,5},{3,7},{12,8},{14,10},{8,... | collective-permute-start | bytes 1671176 | tf_op jit(solution)/shard_map/ppermute | solution.py:49
  47.5 33.5 %collective-permute-start.6 = (bf16[2,64,2176]{2,1,0:T(8,128)(2,1)S(1)}, bf16[2,64,2176]{2,1,0:T(8,128)(2,1)S(1)}, u32[]{:S(2)}, u32[]{:S(2)}) collective-permute-start(bf16[2,64,2176]{2,1,0:T(8,128)(2,1)S(1)} %concatenate.52), channel_id=1, source_target_pairs={{2,0},{4,2},{6,4},{0,6},{3,1},{5,3},{7,5},{1,7},{10,8},{12,10},{14... | collective-permute-start | bytes 1671176 | tf_op jit(solution)/shard_map/ppermute | solution.py:49
  62.0 26.9 %collective-permute-start.3 = (bf16[4,2,64,2048]{3,2,1,0:T(8,128)(2,1)}, bf16[4,2,64,2048]{3,2,1,0:T(8,128)(2,1)}, u32[]{:S(2)}, u32[]{:S(2)}) collective-permute-start(bf16[4,2,64,2048]{3,2,1,0:T(8,128)(2,1)} %get-tuple-element.203), channel_id=1, source_target_pairs={{0,1},{1,0},{2,3},{3,2},{4,5},{5,4},{6,7},{7,6},{8,9},{9,8},{10,11... | collective-permute-start | bytes 6291464 | tf_op jit(solution)/shard_map/ppermute | solution.py:43
  128.9 25.7 %collective-permute-start.13 = (bf16[2,64,2048]{2,1,0:T(8,128)(2,1)S(1)}, bf16[2,64,2048]{2,1,0:T(8,128)(2,1)S(1)}, u32[]{:S(2)}, u32[]{:S(2)}) collective-permute-start(bf16[2,64,2048]{2,1,0:T(8,128)(2,1)S(1)} %get-tuple-element.194), channel_id=1, source_target_pairs={{0,6},{2,0},{4,2},{6,4},{1,7},{3,1},{5,3},{7,5},{8,14},{10,8},{12,... | collective-permute-start | bytes 1572872 | tf_op jit(solution)/shard_map/ppermute | solution.py:58
  133.0 25.3 %collective-permute-start.11 = (bf16[2,64,2048]{2,1,0:T(8,128)(2,1)S(1)}, bf16[2,64,2048]{2,1,0:T(8,128)(2,1)S(1)}, u32[]{:S(2)}, u32[]{:S(2)}) collective-permute-start(bf16[2,64,2048]{2,1,0:T(8,128)(2,1)S(1)} %get-tuple-element.193), channel_id=1, source_target_pairs={{0,2},{2,4},{4,6},{6,0},{1,3},{3,5},{5,7},{7,1},{8,10},{10,12},{12... | collective-permute-start | bytes 1572872 | tf_op jit(solution)/shard_map/ppermute | solution.py:58
  160.1 26.5 %collective-permute-start.16 = (bf16[2,64,2048]{2,1,0:T(8,128)(2,1)S(1)}, bf16[2,64,2048]{2,1,0:T(8,128)(2,1)S(1)}, u32[]{:S(2)}, u32[]{:S(2)}) collective-permute-start(bf16[2,64,2048]{2,1,0:T(8,128)(2,1)S(1)} %multiply_convert_fusion), channel_id=1, source_target_pairs={{6,0},{0,2},{2,4},{4,6},{7,1},{1,3},{3,5},{5,7},{14,8},{8,10},{10,... | collective-permute-start | bytes 1572872 | tf_op jit(solution)/shard_map/ppermute | solution.py:49
  160.1 26.4 %collective-permute-start.15 = (bf16[2,64,2048]{2,1,0:T(8,128)(2,1)S(1)}, bf16[2,64,2048]{2,1,0:T(8,128)(2,1)S(1)}, u32[]{:S(2)}, u32[]{:S(2)}) collective-permute-start(bf16[2,64,2048]{2,1,0:T(8,128)(2,1)S(1)} %multiply_convert_fusion), channel_id=1, source_target_pairs={{4,0},{6,2},{0,4},{2,6},{5,1},{7,3},{1,5},{3,7},{12,8},{14,10},{8,... | collective-permute-start | bytes 1572872 | tf_op jit(solution)/shard_map/ppermute | solution.py:49
  162.2 24.9 %collective-permute-start.14 = (bf16[2,64,2048]{2,1,0:T(8,128)(2,1)S(1)}, bf16[2,64,2048]{2,1,0:T(8,128)(2,1)S(1)}, u32[]{:S(2)}, u32[]{:S(2)}) collective-permute-start(bf16[2,64,2048]{2,1,0:T(8,128)(2,1)S(1)} %multiply_convert_fusion), channel_id=1, source_target_pairs={{2,0},{4,2},{6,4},{0,6},{3,1},{5,3},{7,5},{1,7},{10,8},{12,10},{14... | collective-permute-start | bytes 1572872 | tf_op jit(solution)/shard_map/ppermute | solution.py:49
  267.9 31.6 %collective-permute-start.22 = (bf16[2,64,2048]{2,1,0:T(8,128)(2,1)}, bf16[2,64,2048]{2,1,0:T(8,128)(2,1)S(1)}, u32[]{:S(2)}, u32[]{:S(2)}) collective-permute-start(bf16[2,64,2048]{2,1,0:T(8,128)(2,1)} %get-tuple-element.78), channel_id=1, source_target_pairs={{0,6},{2,0},{4,2},{6,4},{1,7},{3,1},{5,3},{7,5},{8,14},{10,8},{12,... | collective-permute-start | bytes 1572872 | tf_op jit(solution)/shard_map/ppermute | solution.py:58
  270.6 28.9 %collective-permute-start.21 = (bf16[2,64,2048]{2,1,0:T(8,128)(2,1)}, bf16[2,64,2048]{2,1,0:T(8,128)(2,1)S(1)}, u32[]{:S(2)}, u32[]{:S(2)}) collective-permute-start(bf16[2,64,2048]{2,1,0:T(8,128)(2,1)} %get-tuple-element.77), channel_id=1, source_target_pairs={{0,4},{2,6},{4,0},{6,2},{1,5},{3,7},{5,1},{7,3},{8,12},{10,14},{12... | collective-permute-start | bytes 1572872 | tf_op jit(solution)/shard_map/ppermute | solution.py:58
  271.4 28.1 %collective-permute-start.20 = (bf16[2,64,2048]{2,1,0:T(8,128)(2,1)}, bf16[2,64,2048]{2,1,0:T(8,128)(2,1)S(1)}, u32[]{:S(2)}, u32[]{:S(2)}) collective-permute-start(bf16[2,64,2048]{2,1,0:T(8,128)(2,1)} %get-tuple-element.72.after_ref), channel_id=1, source_target_pairs={{0,2},{2,4},{4,6},{6,0},{1,3},{3,5},{5,7},{7,1},{8,10},{10,12},{12... | collective-permute-start | bytes 1572872 | tf_op jit(solution)/shard_map/ppermute | solution.py:58
  303.4 268.7 %all-gather.11.cloned.1.call-start = ((), (), s32[]{:S(2)}) async-start(), calls=%async_computation.3 | async-start | bytes 10616832 | tf_op jit(solution)/shard_map/all_gather | solution.py:935
  354.3 39.0 %collective-permute-start.29 = (bf16[2,64,2048]{2,1,0:T(8,128)(2,1)}, bf16[2,64,2048]{2,1,0:T(8,128)(2,1)}, u32[]{:S(2)}, u32[]{:S(2)}) collective-permute-start(bf16[2,64,2048]{2,1,0:T(8,128)(2,1)} %get-tuple-element.82), channel_id=1, source_target_pairs={{0,6},{2,0},{4,2},{6,4},{1,7},{3,1},{5,3},{7,5},{8,14},{10,8},{12,... | collective-permute-start | bytes 1572872 | tf_op jit(solution)/shard_map/ppermute | solution.py:58
  357.0 36.3 %collective-permute-start.28 = (bf16[2,64,2048]{2,1,0:T(8,128)(2,1)}, bf16[2,64,2048]{2,1,0:T(8,128)(2,1)}, u32[]{:S(2)}, u32[]{:S(2)}) collective-permute-start(bf16[2,64,2048]{2,1,0:T(8,128)(2,1)} %get-tuple-element.81), channel_id=1, source_target_pairs={{0,4},{2,6},{4,0},{6,2},{1,5},{3,7},{5,1},{7,3},{8,12},{10,14},{12... | collective-permute-start | bytes 1572872 | tf_op jit(solution)/shard_map/ppermute | solution.py:58
  357.9 35.4 %collective-permute-start.27 = (bf16[2,64,2048]{2,1,0:T(8,128)(2,1)}, bf16[2,64,2048]{2,1,0:T(8,128)(2,1)}, u32[]{:S(2)}, u32[]{:S(2)}) collective-permute-start(bf16[2,64,2048]{2,1,0:T(8,128)(2,1)} %get-tuple-element.80), channel_id=1, source_target_pairs={{0,2},{2,4},{4,6},{6,0},{1,3},{3,5},{5,7},{7,1},{8,10},{10,12},{12... | collective-permute-start | bytes 1572872 | tf_op jit(solution)/shard_map/ppermute | solution.py:58
  406.1 30.7 %collective-permute-start.37 = (bf16[4,64,1280]{2,1,0:T(8,128)(2,1)}, bf16[4,64,1280]{2,1,0:T(8,128)(2,1)S(1)}, u32[]{:S(2)}, u32[]{:S(2)}) collective-permute-start(bf16[4,64,1280]{2,1,0:T(8,128)(2,1)} %get-tuple-element.97), channel_id=1, source_target_pairs={{24,0},{0,8},{8,16},{16,24},{56,32},{32,40},{40,48},{48,56},{88,64... | collective-permute-start | bytes 1966088 | tf_op jit(solution)/shard_map/ppermute | solution.py:87
  406.5 48.5 %collective-permute-start.34 = (bf16[4,80,1280]{2,1,0:T(8,128)(2,1)}, bf16[4,80,1280]{2,1,0:T(8,128)(2,1)S(1)}, u32[]{:S(2)}, u32[]{:S(2)}) collective-permute-start(bf16[4,80,1280]{2,1,0:T(8,128)(2,1)} %get-tuple-element.93), channel_id=1, source_target_pairs={{96,0},{104,8},{112,16},{120,24},{0,32},{8,40},{16,48},{24,56},{32... | collective-permute-start | bytes 2457608 | tf_op jit(solution)/shard_map/ppermute | solution.py:87
  407.6 47.4 %collective-permute-start.35 = (bf16[4,80,1280]{2,1,0:T(8,128)(2,1)}, bf16[4,80,1280]{2,1,0:T(8,128)(2,1)S(1)}, u32[]{:S(2)}, u32[]{:S(2)}) collective-permute-start(bf16[4,80,1280]{2,1,0:T(8,128)(2,1)} %get-tuple-element.94), channel_id=1, source_target_pairs={{64,0},{72,8},{80,16},{88,24},{96,32},{104,40},{112,48},{120,56},{... | collective-permute-start | bytes 2457608 | tf_op jit(solution)/shard_map/ppermute | solution.py:87
  408.5 47.1 %collective-permute-start.36 = (bf16[4,80,1280]{2,1,0:T(8,128)(2,1)}, bf16[4,80,1280]{2,1,0:T(8,128)(2,1)S(1)}, u32[]{:S(2)}, u32[]{:S(2)}) collective-permute-start(bf16[4,80,1280]{2,1,0:T(8,128)(2,1)} %get-tuple-element.95), channel_id=1, source_target_pairs={{32,0},{40,8},{48,16},{56,24},{64,32},{72,40},{80,48},{88,56},{96,... | collective-permute-start | bytes 2457608 | tf_op jit(solution)/shard_map/ppermute | solution.py:87
  410.8 39.8 %collective-permute-start.38 = (bf16[4,64,1280]{2,1,0:T(8,128)(2,1)}, bf16[4,64,1280]{2,1,0:T(8,128)(2,1)S(1)}, u32[]{:S(2)}, u32[]{:S(2)}) collective-permute-start(bf16[4,64,1280]{2,1,0:T(8,128)(2,1)} %get-tuple-element.98), channel_id=1, source_target_pairs={{16,0},{24,8},{0,16},{8,24},{48,32},{56,40},{32,48},{40,56},{80,64... | collective-permute-start | bytes 1966088 | tf_op jit(solution)/shard_map/ppermute | solution.py:87
  462.2 40.9 %collective-permute-start.30 = (bf16[4,2,64,2048]{3,2,1,0:T(8,128)(2,1)}, bf16[4,2,64,2048]{3,2,1,0:T(8,128)(2,1)}, u32[]{:S(2)}, u32[]{:S(2)}) collective-permute-start(bf16[4,2,64,2048]{3,2,1,0:T(8,128)(2,1)} %bitcast.247), channel_id=1, source_target_pairs={{0,1},{1,0},{2,3},{3,2},{4,5},{5,4},{6,7},{7,6},{8,9},{9,8},{10,11... | collective-permute-start | bytes 6291464 | tf_op jit(solution)/shard_map/ppermute | solution.py:43
  498.9 35.6 %collective-permute-start.48 = (bf16[144,1280]{1,0:T(8,128)(2,1)S(1)}, bf16[144,1280]{1,0:T(8,128)(2,1)S(1)}, u32[]{:S(2)}, u32[]{:S(2)}) collective-permute-start(bf16[144,1280]{1,0:T(8,128)(2,1)S(1)} %get-tuple-element.205), channel_id=1, source_target_pairs={{4,0},{6,2},{0,4},{2,6},{5,1},{7,3},{1,5},{3,7},{12,8},{14,10},{8,... | collective-permute-start | bytes 1105928 | tf_op jit(solution)/shard_map/ppermute | solution.py:78
  501.4 33.1 %collective-permute-start.47 = (bf16[144,1280]{1,0:T(8,128)(2,1)S(1)}, bf16[144,1280]{1,0:T(8,128)(2,1)S(1)}, u32[]{:S(2)}, u32[]{:S(2)}) collective-permute-start(bf16[144,1280]{1,0:T(8,128)(2,1)S(1)} %get-tuple-element.205), channel_id=1, source_target_pairs={{2,0},{4,2},{6,4},{0,6},{3,1},{5,3},{7,5},{1,7},{10,8},{12,10},{14... | collective-permute-start | bytes 1105928 | tf_op jit(solution)/shard_map/ppermute | solution.py:78
  505.1 37.4 %collective-permute-start.33 = (bf16[2,64,2048]{2,1,0:T(8,128)(2,1)S(1)}, bf16[2,64,2048]{2,1,0:T(8,128)(2,1)S(1)}, u32[]{:S(2)}, u32[]{:S(2)}) collective-permute-start(bf16[2,64,2048]{2,1,0:T(8,128)(2,1)S(1)} %get-tuple-element.191), channel_id=1, source_target_pairs={{0,6},{2,0},{4,2},{6,4},{1,7},{3,1},{5,3},{7,5},{8,14},{10,8},{12,... | collective-permute-start | bytes 1572872 | tf_op jit(solution)/shard_map/ppermute | solution.py:58
  505.2 43.8 %collective-permute-start.32 = (bf16[2,64,2048]{2,1,0:T(8,128)(2,1)S(1)}, bf16[2,64,2048]{2,1,0:T(8,128)(2,1)S(1)}, u32[]{:S(2)}, u32[]{:S(2)}) collective-permute-start(bf16[2,64,2048]{2,1,0:T(8,128)(2,1)S(1)} %get-tuple-element.192), channel_id=1, source_target_pairs={{0,4},{2,6},{4,0},{6,2},{1,5},{3,7},{5,1},{7,3},{8,12},{10,14},{12... | collective-permute-start | bytes 1572872 | tf_op jit(solution)/shard_map/ppermute | solution.py:58
  516.9 42.8 %collective-permute-start.31 = (bf16[2,64,2048]{2,1,0:T(8,128)(2,1)S(1)}, bf16[2,64,2048]{2,1,0:T(8,128)(2,1)S(1)}, u32[]{:S(2)}, u32[]{:S(2)}) collective-permute-start(bf16[2,64,2048]{2,1,0:T(8,128)(2,1)S(1)} %get-tuple-element.190), channel_id=1, source_target_pairs={{0,2},{2,4},{4,6},{6,0},{1,3},{3,5},{5,7},{7,1},{8,10},{10,12},{12... | collective-permute-start | bytes 1572872 | tf_op jit(solution)/shard_map/ppermute | solution.py:58
  534.7 29.4 %collective-permute-start.50 = (bf16[4,144,1280]{2,1,0:T(8,128)(2,1)S(1)}, bf16[4,144,1280]{2,1,0:T(8,128)(2,1)}, u32[]{:S(2)}, u32[]{:S(2)}) collective-permute-start(bf16[4,144,1280]{2,1,0:T(8,128)(2,1)S(1)} %pad_maximum_fusion.8.mine_ref), channel_id=1, source_target_pairs={{0,1},{1,0},{2,3},{3,2},{4,5},{5,4},{6,7},{7,6},{8,9},{9,8},{10,11... | collective-permute-start | bytes 4423688 | tf_op jit(solution)/shard_map/ppermute | solution.py:43
  (56 other events, 742.5 us)
Sparse Core Ops, SparseCore 0:
  19.9 65.6 all-gather.6
  87.8 121.7 all-gather.8
  303.5 143.5 reduce-scatter.3
  462.3 98.2 all-gather.10

commit v2 on v1

--- a/solution.py
+++ b/solution.py
@@ -43,11 +43,15 @@
     return lax.ppermute(v, "dp", [(0, 1), (1, 0)])
 
 
-def gather_rows(own, ring):
+def ring_stack(own, ring):
     pieces = [own]
     for k in range(1, ring):
         pieces.append(lax.ppermute(own, "context", [((i + k) % ring, i) for i in range(ring)]))
-    mine = jnp.stack(pieces)
+    return jnp.stack(pieces)
+
+
+def gather_rows(own, ring):
+    mine = ring_stack(own, ring)
     return jnp.stack([mine, swap(mine)])
 
 
@@ -87,21 +91,21 @@
     return lax.ppermute(v, "experts", moves)
 
 
-def after_kernel(v_ref, token_ref, out_ref):
+def after_kernel(v_ref, *refs):
     pass
 
 
-def after_call(v, token):
+def after_call(v, *tokens):
     anywhere = pl.BlockSpec(memory_space=pl.ANY)
     return pl.pallas_call(
         after_kernel,
-        in_specs=[anywhere, anywhere],
+        in_specs=[anywhere] * (1 + len(tokens)),
         out_specs=anywhere,
         out_shape=jax.ShapeDtypeStruct(v.shape, v.dtype),
         input_output_aliases={0: 0},
         cost_estimate=TINY,
         name="after",
-    )(v, token)
+    )(v, *tokens)
 
 
 def rope(v, cosines, sines):
@@ -188,7 +192,8 @@
 def attend_back_kernel(
     heads,
     scale,
-    da_ref,
+    theirs_da_ref,
+    mine_da_ref,
     x_ref,
     gain_ref,
     w_ref,
@@ -218,7 +223,7 @@
         sum_x_ref[...] = jnp.zeros_like(sum_x_ref)
 
     width = (heads + 2) * size
-    da = flat(da_ref)
+    da = jnp.where(step < 2, flat(theirs_da_ref), flat(mine_da_ref))
     d_heads = None
     for first, last, block in out_blocks(w_ref, width):
         piece = against(da[:, first:last], block)
@@ -275,7 +280,7 @@
         put(mine_ref, part)
 
 
-def attend_call(kernel, operands, extra, outputs, scratch, shape, name, flops):
+def attend_call(kernel, operands, extra, outputs, scratch, shape, name, cost):
     ring, micro, row_count, width = shape
 
     def rows_spec(last):
@@ -286,9 +291,17 @@
     def whole(v):
         return pl.BlockSpec(v.shape, lambda b: (0,) * v.ndim)
 
+    def slot_spec(v, kind):
+        block = (1, ring, 1, row_count, v.shape[-1])
+        if kind == "theirs":
+            return pl.BlockSpec(block, lambda b: (0, 0, jnp.minimum(b, 1), 0, 0))
+        return pl.BlockSpec(block, lambda b: (0, 0, jnp.maximum(b - 2, 0), 0, 0))
+
     in_specs = [
         rows_spec(v.shape[-1])
         if kind == "rows"
+        else slot_spec(v, kind)
+        if kind in ("theirs", "mine")
         else pl.BlockSpec((1,) + v.shape[1:], lambda b: ((1 - b // 2) * micro + b % 2, 0, 0))
         if kind == "bias"
         else pl.BlockSpec(memory_space=pl.ANY)
@@ -318,7 +331,7 @@
         out_shape=out_shape,
         scratch_shapes=scratch,
         compiler_params=pltpu.CompilerParams(vmem_limit_bytes=VMEM),
-        cost_estimate=TINY,
+        cost_estimate=cost,
         name=name,
     )(*operands)
 
@@ -397,7 +410,7 @@
 
 
 def expert_grads_kernel(
-    part, dg_ref, du_ref, hid_ref, h2_ref, dy_ref, after_ref, out_ref, token_ref
+    part, dg_ref, du_ref, hid_ref, h2_ref, dy_ref, out_ref, token_ref
 ):
     width = h2_ref.shape[1]
     group = out_ref.shape[0]
@@ -410,7 +423,7 @@
     token_ref[...] = jnp.zeros_like(token_ref)
 
 
-def expert_grads_call(d_gate, d_up, hidden, h2, dy, after, owners, part):
+def expert_grads_call(d_gate, d_up, hidden, h2, dy, owners, part):
     rows, width = h2.shape
     n = 4
     wide = d_gate.shape[1] // n
@@ -424,7 +437,6 @@
             wide_spec,
             pl.BlockSpec((rows, width), lambda c: (0, 0)),
             pl.BlockSpec((rows, dy.shape[1]), lambda c: (0, 0)),
-            pl.BlockSpec(memory_space=pl.ANY),
         ],
         out_specs=[
             pl.BlockSpec((owners // n, 3 * part, width), lambda c: (c, 0, 0)),
@@ -437,7 +449,39 @@
         compiler_params=pltpu.CompilerParams(vmem_limit_bytes=VMEM),
         cost_estimate=TINY,
         name="experts_weights",
-    )(d_gate, d_up, hidden, h2, dy, after)
+    )(d_gate, d_up, hidden, h2, dy)
+
+
+def add_placed_kernel(where_ref, theirs_ref, mine_ref, token_ref, out_ref):
+    ring = mine_ref.shape[0]
+    for k in range(ring):
+        out_ref[lax.rem(where_ref[0] + k, ring)] = (
+            theirs_ref[k].astype(F32) + mine_ref[k].astype(F32)
+        ).astype(BF16)
+
+
+def add_placed_call(where, theirs, mine, token):
+    vmem = pl.BlockSpec(memory_space=pltpu.VMEM)
+    return pl.pallas_call(
+        add_placed_kernel,
+        grid_spec=pltpu.PrefetchScalarGridSpec(
+            num_scalar_prefetch=1,
+            grid=(),
+            in_specs=[vmem, vmem, pl.BlockSpec(memory_space=pl.ANY)],
+            out_specs=vmem,
+        ),
+        out_shape=jax.ShapeDtypeStruct(mine.shape, BF16),
+        compiler_params=pltpu.CompilerParams(vmem_limit_bytes=VMEM),
+        cost_estimate=TINY,
+        name="add_cores_placed",
+    )(where, theirs, mine, token)
+
+
+def exchange_sum(pieces, token=None):
+    got = lax.all_to_all(pieces, "context", split_axis=0, concat_axis=0, tiled=True)
+    if token is not None:
+        got = after_call(got, token)
+    return jnp.sum(got.astype(F32), axis=0)
 
 
 def add_kernel(theirs_ref, mine_ref, token_ref, *out_refs):
@@ -491,6 +535,28 @@
         cost_estimate=TINY,
         name="experts_results",
     )(gathered)
+
+
+def out_grads_kernel(heads_ref, mine_ref, theirs_ref, out_ref):
+    total = outer(heads_ref[0], mine_ref[...]) + outer(heads_ref[1], theirs_ref[...])
+    out_ref[...] = total.astype(BF16)
+
+
+def out_grads_call(heads_out, mine, theirs):
+    _, half, columns = heads_out.shape
+    width = mine.shape[1]
+    n = 4
+    spec = pl.BlockSpec((half, width // n), lambda c: (0, c))
+    return pl.pallas_call(
+        out_grads_kernel,
+        grid=(n,),
+        in_specs=[pl.BlockSpec(heads_out.shape, lambda c: (0, 0, 0)), spec, spec],
+        out_specs=pl.BlockSpec((columns, width // n), lambda c: (0, c)),
+        out_shape=jax.ShapeDtypeStruct((columns, width), BF16),
+        compiler_params=pltpu.CompilerParams(vmem_limit_bytes=VMEM),
+        cost_estimate=TINY,
+        name="out_weights",
+    )(heads_out, mine, theirs)
 
 
 def attend_grads_kernel(
@@ -558,7 +624,8 @@
 
 
 def half_sum_kernel(place_ref, *refs):
-    firsts, seconds, total = refs[2 * SIDE : 3 * SIDE], refs[3 * SIDE : 4 * SIDE], refs[-1]
+    outs, total = refs[2 * SIDE + 1 : -1], refs[-1]
+    firsts, seconds = outs[:SIDE], outs[SIDE:]
     total[...] = total_of(refs[:SIDE])
     other = total_of(refs[SIDE : 2 * SIDE])
     for k in range(SIDE):
@@ -566,14 +633,14 @@
         seconds[k][...] = other[k]
 
 
-def half_sum_call(place, firsts, seconds):
+def half_sum_call(place, firsts, seconds, token):
     vmem = pl.BlockSpec(memory_space=pltpu.VMEM)
     outs = pl.pallas_call(
         half_sum_kernel,
         grid_spec=pltpu.PrefetchScalarGridSpec(
             num_scalar_prefetch=1,
             grid=(),
-            in_specs=[vmem] * (2 * SIDE),
+            in_specs=[vmem] * (2 * SIDE) + [pl.BlockSpec(memory_space=pl.ANY)],
             out_specs=[vmem] * (2 * SIDE),
             scratch_shapes=[pltpu.VMEM(firsts[0].shape, BF16)],
         ),
@@ -581,53 +648,44 @@
         compiler_params=pltpu.CompilerParams(vmem_limit_bytes=VMEM),
         cost_estimate=TINY,
         name="half_sum",
-    )(place, *firsts, *seconds)
+    )(place, *firsts, *seconds, token)
     return outs[:SIDE], outs[SIDE:]
 
 
-def last_sum_kernel(*refs):
+def last_sum_kernel(token_ref, *refs):
     out = refs[-1]
     cut = refs[0].shape[0]
     out[:cut] = total_of(refs[:SIDE])
     out[cut:] = total_of(refs[SIDE : 2 * SIDE])
 
 
-def last_sum_call(firsts, seconds):
+def last_sum_call(firsts, seconds, token):
     rows, columns = firsts[0].shape[0] + seconds[0].shape[0], firsts[0].shape[1]
     vmem = pl.BlockSpec(memory_space=pltpu.VMEM)
     return pl.pallas_call(
         last_sum_kernel,
-        in_specs=[vmem] * (2 * SIDE),
+        in_specs=[pl.BlockSpec(memory_space=pl.ANY)] + [vmem] * (2 * SIDE),
         out_specs=vmem,
         out_shape=jax.ShapeDtypeStruct((rows, columns), BF16),
         compiler_params=pltpu.CompilerParams(vmem_limit_bytes=VMEM),
         cost_estimate=TINY,
         name="last_sum",
-    )(*firsts, *seconds)
+    )(token, *firsts, *seconds)
 
 
 def plane_send(pieces, dx, dz):
     return [pieces[0]] + [plane(pieces[k], -k * dx, -k * dz) for k in range(1, SIDE)]
 
 
-def columns_kernel(
-    heads_width, size, where_ref, mine_ref, theirs_ref, q_ref, k_ref, v_ref, out_ref, sum_ref
-):
+def columns_kernel(heads_width, size, where_ref, mine_ref, theirs_ref, q_ref, k_ref, v_ref, sum_ref):
     depth = q_ref.shape[0]
-    last = heads_width + 2 * size
     mine, theirs = mine_ref[0].astype(F32), theirs_ref[0].astype(F32)
     first = where_ref[1] == 0
-    low, high = jnp.where(first, mine, theirs), jnp.where(first, theirs, mine)
-    q_ref[:, :heads_width] = low[:depth, :heads_width]
-    q_ref[:, heads_width:] = high[:depth, :heads_width]
+    q_ref[:, :heads_width] = jnp.where(first, mine[:depth, :heads_width], theirs[:depth, :heads_width])
+    q_ref[:, heads_width:] = jnp.where(first, theirs[:depth, :heads_width], mine[:depth, :heads_width])
     both = mine + theirs
     k_ref[...] = both[:depth, heads_width : heads_width + size]
-    v_ref[...] = both[:depth, heads_width + size : last]
-    columns = mine.shape[1] - last
-    rows = out_ref.shape[0] // 2
-    for k in range(depth // rows):
-        out_ref[:rows, k * columns : (k + 1) * columns] = low[k * rows : (k + 1) * rows, last:]
-        out_ref[rows:, k * columns : (k + 1) * columns] = high[k * rows : (k + 1) * rows, last:]
+    v_ref[...] = both[:depth, heads_width + size :]
 
     @pl.when(pl.program_id(0) == 0)
     def _():
@@ -636,15 +694,12 @@
     sum_ref[...] += both[depth:]
 
 
-def columns_call(where, mine, theirs, depth, heads_width, size, out_rows, width):
+def columns_call(where, mine, theirs, depth, heads_width, size):
     ring, rows, last = mine.shape
     cores = 2
 
     def at(k, where):
         return (0, lax.rem(where[0] + k, ring))
-
-    def row_at(k, where):
-        return (lax.rem(where[0] + k, ring), 0)
 
     return pl.pallas_call(
         functools.partial(columns_kernel, heads_width, size),
@@ -656,7 +711,6 @@
                 pl.BlockSpec((depth, cores * heads_width), at),
                 pl.BlockSpec((depth, size), at),
                 pl.BlockSpec((depth, size), at),
-                pl.BlockSpec((out_rows // ring, width), row_at),
                 pl.BlockSpec((rows - depth, last), lambda k, where: (0, 0)),
             ],
         ),
@@ -664,12 +718,39 @@
             jax.ShapeDtypeStruct((depth, ring * cores * heads_width), F32),
             jax.ShapeDtypeStruct((depth, ring * size), F32),
             jax.ShapeDtypeStruct((depth, ring * size), F32),
-            jax.ShapeDtypeStruct((out_rows, width), F32),
             jax.ShapeDtypeStruct((rows - depth, last), F32),
         ],
         compiler_params=pltpu.CompilerParams(vmem_limit_bytes=VMEM),
         cost_estimate=TINY,
-        name="attention_results",
+        name="columns_results",
+    )(where, mine, theirs)
+
+
+def rows_kernel(where_ref, mine_ref, theirs_ref, out_ref):
+    count = mine_ref.shape[1]
+    mine, theirs = mine_ref[0].astype(F32), theirs_ref[0].astype(F32)
+    first = where_ref[1] == 0
+    out_ref[:count] = jnp.where(first, mine, theirs)
+    out_ref[count:] = jnp.where(first, theirs, mine)
+
+
+def rows_call(where, mine, theirs):
+    ring, count, width = mine.shape
+    cores = 2
+    return pl.pallas_call(
+        rows_kernel,
+        grid_spec=pltpu.PrefetchScalarGridSpec(
+            num_scalar_prefetch=1,
+            grid=(ring,),
+            in_specs=[pl.BlockSpec((1, count, width), lambda k, where: (k, 0, 0))] * 2,
+            out_specs=pl.BlockSpec(
+                (cores * count, width), lambda k, where: (lax.rem(where[0] + k, ring), 0)
+            ),
+        ),
+        out_shape=jax.ShapeDtypeStruct((ring * cores * count, width), F32),
+        compiler_params=pltpu.CompilerParams(vmem_limit_bytes=VMEM),
+        cost_estimate=TINY,
+        name="rows_results",
     )(where, mine, theirs)
 
 
@@ -707,7 +788,9 @@
         ],
         out_shape=[half, half],
         compiler_params=pltpu.CompilerParams(vmem_limit_bytes=VMEM),
-        cost_estimate=TINY,
+        cost_estimate=pl.CostEstimate(
+            flops=2 * rows * wide * width, bytes_accessed=20_000_000, transcendentals=0
+        ),
         name="experts_out",
     )(hidden, weights, token)
 
@@ -793,6 +876,7 @@
     gain_key = gain_row[:, 2 * depth + eighth : 2 * depth + 2 * eighth].reshape(-1)
     hidden_width = owners * ff_part
 
+    where = jnp.stack([y, d]).astype(jnp.int32)
     x_own = tokens[:, 0]
     x_rows = gather_rows(x_own, ring)
     len_all = jnp.stack([lengths[:, 0], swap(lengths[:, 0])]).reshape(seqs)
@@ -842,7 +926,7 @@
         [pltpu.VMEM((span, q_width), BF16), pltpu.VMEM((span, width), BF16)],
         shape,
         "attention",
-        6_000_000_000,
+        TINY,
     )
     attn_own = scatter_rows(theirs[0], mine[0])
     x1 = x_own.astype(F32) + attn_own
@@ -850,27 +934,34 @@
     h2 = gather_rows((x1 * inverse_mid * gain_moe).astype(BF16), ring).reshape(rows, width)
 
     d_gate, d_up, hidden, theirs, mine = experts_call(h2, dy_mix, expert_all, spread, ff_part)
-    pieces = add_call(swap(theirs.reshape(shape)), mine.reshape(shape), d_gate)
+    grad_experts, token = expert_grads_call(
+        d_gate, d_up, hidden, h2, dy_mix, owners, ff_part
+    )
+    pieces = add_call(swap(theirs.reshape(shape)), mine.reshape(shape), token)
     d_h2 = ring_sum(pieces)
-    grad_experts, token = expert_grads_call(
-        d_gate, d_up, hidden, h2, dy_mix, pieces[1], owners, ff_part
-    )
     moe_theirs, moe_mine = expert_out_call(hidden, expert_all, token, ff_part)
 
     grad_gain_moe = jnp.sum(d_h2 * x1 * inverse_mid, axis=(0, 1))
     d_x1 = dy_own.astype(F32) + norm_back(d_h2, x1, inverse_mid, gain_moe)
     grad_experts = lax.psum_scatter(
-        after_call(grad_experts, d_x1), "experts", scatter_dimension=0, tiled=False
-    )
-    d_attn = gather_rows(d_x1.astype(BF16), ring)
-    moe_pieces = add_call(swap(moe_theirs.reshape(shape)), moe_mine.reshape(shape), d_attn)
-    output = (x1 + ring_sum(moe_pieces)).astype(BF16)[:, None]
-    grad_out = outer(heads_out.reshape(rows, q_width), d_attn.reshape(rows, width)).astype(BF16)
+        grad_experts, "experts", scatter_dimension=0, tiled=False
+    )
+    moe_pieces = add_placed_call(
+        where, swap(moe_theirs.reshape(shape)), moe_mine.reshape(shape), hidden
+    )
+    d_mine = after_call(ring_stack(d_x1.astype(BF16), ring), moe_pieces)
+    d_theirs = swap(d_mine)
+    grad_out = out_grads_call(
+        heads_out.reshape(2, rows // 2, q_width),
+        d_mine.reshape(-1, width),
+        d_theirs.reshape(-1, width),
+    )
     grad_out = grad_out.reshape(owners, out_part, width)
     d_qkv, theirs, mine, sum_q, sum_k, sum_x = attend_call(
         functools.partial(attend_back_kernel, q_heads, scale),
         (
-            d_attn,
+            d_theirs[None],
+            d_mine[None],
             x_rows,
             gain_attn[None],
             shared,
@@ -879,10 +970,24 @@
             bias,
             *head_gains,
             qkv,
-            moe_pieces[0],
+            moe_pieces,
             grad_out,
         ),
-        ("rows", "rows", "", "", "", "", "bias", "", "", "rows", "token", "token"),
+        (
+            "theirs",
+            "mine",
+            "rows",
+            "",
+            "",
+            "",
+            "",
+            "bias",
+            "",
+            "",
+            "rows",
+            "token",
+            "token",
+        ),
         (
             ("rows", qkv_width, BF16),
             ("parts", width, BF16),
@@ -893,15 +998,12 @@
         [pltpu.VMEM((span, qkv_width), BF16)],
         shape,
         "attention_back",
-        9_000_000_000,
-    )
+        pl.CostEstimate(flops=9_000_000_000, bytes_accessed=90_000_000, transcendentals=0),
+    )
+    output = (x1 + exchange_sum(moe_pieces, d_qkv)).astype(BF16)[:, None]
     grad_gain_query, grad_gain_key, grad_gain_attn = sum_q[0], sum_k[0], sum_x[0]
-    d_h1 = scatter_rows(theirs[0], mine[0])
-    x_f32 = x_own.astype(F32)
-    input_grad = (d_x1 + norm_back(d_h1, x_f32, inverse_rms(x_f32), gain_attn))[:, None]
     h1, d_qkv = h1.reshape(rows, width), d_qkv.reshape(rows, qkv_width)
 
-    where = jnp.stack([y, d]).astype(jnp.int32)
     grad_gains = jnp.concatenate(
         [
             grad_gain_attn.reshape(owners, depth),
@@ -919,21 +1021,25 @@
     firsts, seconds = attend_grads_call(
         place, h1, d_qkv, grad_out, grad_gains, output, depth // 2 + 16
     )
-    firsts, seconds = half_sum_call(
-        place, plane_send(firsts, 1, 0), plane_send(seconds, 0, 1)
-    )
-    grads = last_sum_call(plane_send(firsts, 0, 1), plane_send(seconds, 1, 0))
-    out_back = lax.ppermute(grads[:depth, qkv_width:], EVERY, back)
-    grads = jnp.concatenate(
-        [grads[:, :qkv_width], jnp.pad(out_back, ((0, 16), (0, 0)))], axis=1
-    )
-    result_q, result_k, result_v, result_out, gain_sum = columns_call(
-        where, *gather_members(grads), depth, q_width, head, w_out.shape[0], width
-    )
+    d_h1 = exchange_sum(add_placed_call(where, swap(theirs[0]), mine[0], firsts[1]))
+    x_f32 = x_own.astype(F32)
+    input_grad = (d_x1 + norm_back(d_h1, x_f32, inverse_rms(x_f32), gain_attn))[:, None]
+    grad_experts = after_call(grad_experts, firsts[1])
+    all_experts = lax.all_gather(grad_experts, GROUP, axis=0, tiled=False)
+    firsts, seconds = plane_send(firsts, 1, 0), plane_send(seconds, 0, 1)
+    firsts, seconds = half_sum_call(place, firsts, seconds, grad_out)
+    grads = last_sum_call(plane_send(firsts, 0, 1), plane_send(seconds, 1, 0), d_h1)
+    result_gate, result_up, result_down = gate_up_down_call(all_experts, ff_part)
+    out_sum = jnp.concatenate(
+        [grads[k * out_part : (k + 1) * out_part, qkv_width:] for k in range(depth // out_part)],
+        axis=1,
+    )
+    result_q, result_k, result_v, gain_sum = columns_call(
+        where, *gather_members(grads[:, :qkv_width]), depth, q_width, head
+    )
+    out_sum = after_call(lax.ppermute(out_sum, EVERY, back), result_down)
+    result_out = rows_call(where, *gather_members(out_sum))
     gain_sum = gain_sum[0]
-    grad_experts = after_call(grad_experts, seconds[1])
-    all_experts = lax.all_gather(grad_experts, GROUP, axis=0, tiled=False)
-    result_gate, result_up, result_down = gate_up_down_call(all_experts, ff_part)
     return (
         output,
         input_grad,

time: 601 us -> 588 us (0.978)
  the two profiles are of different devices: /device:TPU:4 before, /device:TPU:49 now
where the time goes in v2:
time: 588 us; the launch traced here: 577 us
  Pallas kernels  195 us (33%)
  waiting for transfers between devices  194 us (33%)
  starting transfers between devices  99.6 us (17%)
  other arithmetic  50.2 us (9%)
  local copies, waits for them, and re-layouts  23.8 us (4%)
  between operations  14.7 us (2%)
    ppermute x12, waiting for transfers between devices, ring_stack(): lax.ppermute(own, 'context', [((i + k) % ring, i) for i in range(ring)])  78 us
    pallas_call x2, Pallas kernels, attend_call(): pl.pallas_call(kernel, grid=(2 * micro,), in_specs=in_specs, out_specs=ou...  48.9 us
    pallas_call x1, Pallas kernels, experts_call(): pl.pallas_call(functools.partial(experts_kernel, part), grid=(n, blocks),...  48.9 us
    ppermute x12, waiting for transfers between devices, plane(): return lax.ppermute(v, 'experts', moves)  36.5 us
    ppermute x11, starting transfers between devices, swap(): return lax.ppermute(v, 'dp', [(0, 1), (1, 0)])  33.1 us
    ppermute x6, waiting for transfers between devices, ring_sum(): lax.ppermute(pieces[k], 'context', [(i, (i + k) % ring) for i in range(ri...  31.3 us
    pallas_call x1, Pallas kernels, expert_grads_call(): pl.pallas_call(functools.partial(expert_grads_kernel, part), grid=(n,), i...  26.9 us
    ppermute x12, starting transfers between devices, plane(): return lax.ppermute(v, 'experts', moves)  21.9 us
  transfers between devices with their start and end apart: 55, of which 34 were waited for; matrix products, arithmetic and copies ran while one was open for 11% of the time, Pallas kernels for 20%

profile of v2, /device:TPU:49, one launch (start us, length us, event | category | flops | bytes accessed | tf_op | source)
XLA Modules:
  0.0 577.2 jit_solution(4065050389081223383)
XLA Ops:
  8.3 4.7 collective-permute-start.4
  15.5 6.9 %collective-permute-done.4 = bf16[32,2048]{1,0:T(8,128)(2,1)S(1)} collective-permute-done((bf16[32,2048]{1,0:T(8,128)(2,1)S(1)}, bf16[32,2048]{1,0:T(8,128)(2,1)S(1)}, u32[]{:S(2)}, u32[]{:S(2)}) %collective-permute-start.4) | collective-permute-done | bytes 131104 | tf_op jit(solution)/shard_map/ppermute | solution.py:843
  38.6 8.3 %collective-permute-done.1 = bf16[2,64,2048]{2,1,0:T(8,128)(2,1)S(1)} collective-permute-done((bf16[2,64,2048]{2,1,0:T(8,128)(2,1)S(1)}, bf16[2,64,2048]{2,1,0:T(8,128)(2,1)S(1)}, u32[]{:S(2)}, u32[]{:S(2)}) %collective-permute-start.1) | collective-permute-done | bytes 524320 | tf_op jit(solution)/shard_map/ppermute | solution.py:49
  47.5 10.3 %collective-permute-done = bf16[2,64,2048]{2,1,0:T(8,128)(2,1)S(1)} collective-permute-done((bf16[2,64,2048]{2,1,0:T(8,128)(2,1)S(1)}, bf16[2,64,2048]{2,1,0:T(8,128)(2,1)S(1)}, u32[]{:S(2)}, u32[]{:S(2)}) %collective-permute-start) | collective-permute-done | bytes 524320 | tf_op jit(solution)/shard_map/ppermute | solution.py:49
  62.5 8.3 %collective-permute-done.8 = bf16[2,64,2176]{2,1,0:T(8,128)(2,1)S(1)} collective-permute-done((bf16[2,64,2176]{2,1,0:T(8,128)(2,1)S(1)}, bf16[2,64,2176]{2,1,0:T(8,128)(2,1)S(1)}, u32[]{:S(2)}, u32[]{:S(2)}) %collective-permute-start.8) | collective-permute-done | bytes 557088 | tf_op jit(solution)/shard_map/ppermute | solution.py:49
  70.8 11.3 %collective-permute-done.7 = bf16[2,64,2176]{2,1,0:T(8,128)(2,1)S(1)} collective-permute-done((bf16[2,64,2176]{2,1,0:T(8,128)(2,1)S(1)}, bf16[2,64,2176]{2,1,0:T(8,128)(2,1)S(1)}, u32[]{:S(2)}, u32[]{:S(2)}) %collective-permute-start.7) | collective-permute-done | bytes 557088 | tf_op jit(solution)/shard_map/ppermute | solution.py:49
  90.7 4.6 pad_maximum_fusion.1.x_ref
  102.6 22.0 %attention.1 = (bf16[2,4,2,64,2048]{4,3,2,1,0:T(8,128)(2,1)}, f32[2,4,2,64,768]{4,3,2,1,0:T(8,128)}, bf16[2,4,2,64,512]{4,3,2,1,0:T(8,128)(2,1)}, bf16[1,4,2,64,...) custom-call(bf16[2,4,2,64,2048]{4,3,2,1,0:T(8,128)(2,1)} %pad_maximum_fusion.1.x_ref, f32[1,2048]{1,0:T(1,128)} %bitcast.207, ...), custom_call_target="tpu_custom_call" | custom-call | bytes 1000 | tf_op jit(solution)/shard_map/attention/pallas_call | solution.py:326
  136.0 9.2 %collective-permute-done.11 = bf16[2,64,2048]{2,1,0:T(8,128)(2,1)S(1)} collective-permute-done((bf16[2,64,2048]{2,1,0:T(8,128)(2,1)S(1)}, bf16[2,64,2048]{2,1,0:T(8,128)(2,1)S(1)}, u32[]{:S(2)}, u32[]{:S(2)}) %collective-permute-start.11) | collective-permute-done | bytes 524320 | tf_op jit(solution)/shard_map/ppermute | solution.py:62
  146.8 10.0 %collective-permute-done.12 = bf16[2,64,2048]{2,1,0:T(8,128)(2,1)S(1)} collective-permute-done((bf16[2,64,2048]{2,1,0:T(8,128)(2,1)S(1)}, bf16[2,64,2048]{2,1,0:T(8,128)(2,1)S(1)}, u32[]{:S(2)}, u32[]{:S(2)}) %collective-permute-start.12) | collective-permute-done | bytes 524320 | tf_op jit(solution)/shard_map/ppermute | solution.py:62
  163.2 10.0 %collective-permute-done.15 = bf16[2,64,2048]{2,1,0:T(8,128)(2,1)S(1)} collective-permute-done((bf16[2,64,2048]{2,1,0:T(8,128)(2,1)S(1)}, bf16[2,64,2048]{2,1,0:T(8,128)(2,1)S(1)}, u32[]{:S(2)}, u32[]{:S(2)}) %collective-permute-start.15) | collective-permute-done | bytes 524320 | tf_op jit(solution)/shard_map/ppermute | solution.py:49
  173.1 12.3 %collective-permute-done.14 = bf16[2,64,2048]{2,1,0:T(8,128)(2,1)S(1)} collective-permute-done((bf16[2,64,2048]{2,1,0:T(8,128)(2,1)S(1)}, bf16[2,64,2048]{2,1,0:T(8,128)(2,1)S(1)}, u32[]{:S(2)}, u32[]{:S(2)}) %collective-permute-start.14) | collective-permute-done | bytes 524320 | tf_op jit(solution)/shard_map/ppermute | solution.py:49
  193.5 15.3 %all-gather.9.cloned.1.call-done = bf16[4608,2048]{1,0:T(8,128)(2,1)} async-done(((bf16[288,2048]{1,0:T(8,128)(2,1)}), bf16[4608,2048]{1,0:T(8,128)(2,1)}) %all-gather.9.cloned.1.call-update) | async-done | bytes 18874384 | tf_op jit(solution)/shard_map/all_gather | solution.py:869
  208.9 48.9 %experts_rows.1 = (bf16[1024,1536]{1,0:T(8,128)(2,1)}, bf16[1024,1536]{1,0:T(8,128)(2,1)}, bf16[1024,1536]{1,0:T(8,128)(2,1)}, bf16[512,2048]{1,0:T(8,128)(2,1)}, bf16[512,2048]{1,0:T(8,128)(2,1)}) custom-call(bf16[1024,2048]{1,0:T(8,128)(2,1)} %bitcast.158, bf16[1024,2176]{1,0:T(8,128)(2,1)} %bitcast.156, bf16[16,288,2048]{2,1,0:T(8,128)(2,1)} %bitcast.165, ...), custom_call_target="tpu_custom_call" | custom-call | bytes 1000 | tf_op jit(solution)/shard_map/experts_rows/pallas_call | solution.py:388
  257.7 26.9 %experts_weights.1 = (bf16[16,288,2048]{2,1,0:T(8,128)(2,1)}, f32[8,128]{1,0:T(8,128)}) custom-call(bf16[1024,1536]{1,0:T(8,128)(2,1)} %get-tuple-element.63.dg_ref, bf16[1024,1536]{1,0:T(8,128)(2,1)} %get-tuple-element.64.du_ref, bf16[1024,1536]{1,0:T(8,128)(2,1)} %get-tuple-element.62.hid_ref.token_ref, bf16[1024,2048]{1,0:T(8,128)(2,1)} %bitcast.159, ...), custom_call_target="tpu_custom_call" | custom-call | bytes 1000 | tf_op jit(solution)/shard_map/experts_weights/pallas_call | solution.py:431
  284.7 13.8 %collective-permute-start.19 = (bf16[4,2,64,2048]{3,2,1,0:T(8,128)(2,1)}, bf16[4,2,64,2048]{3,2,1,0:T(8,128)(2,1)S(1)}, u32[]{:S(2)}, u32[]{:S(2)}) collective-permute-start(bf16[4,2,64,2048]{3,2,1,0:T(8,128)(2,1)} %bitcast.220), channel_id=1, source_target_pairs={{0,1},{1,0},{2,3},{3,2},{4,5},{5,4},{6,7},{7,6},{8,9},{9,8},{10,11... | collective-permute-start | bytes 6291464 | tf_op jit(solution)/shard_map/ppermute | solution.py:43
  309.9 12.1 %experts_out.1 = (bf16[512,2048]{1,0:T(8,128)(2,1)}, bf16[512,2048]{1,0:T(8,128)(2,1)}) custom-call(bf16[1024,1536]{1,0:T(8,128)(2,1)} %get-tuple-element.62.hid_ref.token_ref, bf16[16,288,2048]{2,1,0:T(8,128)(2,1)} %bitcast.166, f32[8,128]{1,0:T(8,128)} %get-tuple-element.65.token_ref), custom_call_target="tpu_custom_call" | custom-call | flops 6442450944 | bytes 20000000 | tf_op jit(solution)/shard_map/experts_out/pallas_call | solution.py:777
  323.4 8.9 %collective-permute-done.21 = bf16[2,64,2048]{2,1,0:T(8,128)(2,1)S(1)} collective-permute-done((bf16[2,64,2048]{2,1,0:T(8,128)(2,1)}, bf16[2,64,2048]{2,1,0:T(8,128)(2,1)S(1)}, u32[]{:S(2)}, u32[]{:S(2)}) %collective-permute-start.21) | collective-permute-done | bytes 524320 | tf_op jit(solution)/shard_map/ppermute | solution.py:62
  341.4 4.8 add_cores_placed.2.refs_0_.token_ref
  350.0 11.2 %collective-permute-done.24 = bf16[2,64,2048]{2,1,0:T(8,128)(2,1)S(1)} collective-permute-done((bf16[2,64,2048]{2,1,0:T(8,128)(2,1)S(1)}, bf16[2,64,2048]{2,1,0:T(8,128)(2,1)S(1)}, u32[]{:S(2)}, u32[]{:S(2)}) %collective-permute-start.24) | collective-permute-done | bytes 524320 | tf_op jit(solution)/shard_map/ppermute | solution.py:49
  367.2 5.3 all-to-all-start
  373.1 6.2 %out_weights.1 = bf16[512,2048]{1,0:T(8,128)(2,1)} custom-call(bf16[2,512,512]{2,1,0:T(8,128)(2,1)} %bitcast.187, bf16[512,2048]{1,0:T(8,128)(2,1)} %bitcast.160, bf16[512,2048]{1,0:T(8,128)(2,1)} %bitcast.60.theirs_ref), custom_call_target="tpu_custom_call" | custom-call | bytes 1000 | tf_op jit(solution)/shard_map/out_weights/pallas_call | solution.py:550
  379.3 26.9 %attention_back.1 = (bf16[2,4,2,64,768]{4,3,2,1,0:T(8,128)(2,1)}, bf16[1,4,2,64,2048]{4,3,2,1,0:T(8,128)(2,1)}, bf16[1,4,2,64,2048]{4,3,2,1,0:T(8,128)(2,1)}, f3...) custom-call(bf16[1,4,2,64,2048]{4,3,2,1,0:T(8,128)(2,1)} %bitcast.56.theirs_da_ref, ...), custom_call_target="tpu_custom_call" | custom-call | flops 8999999488 | bytes 90000000 | tf_op jit(solution)/shard_map/attention_back/pallas_call | solution.py:326
  413.9 10.0 %attention_weights.1 = (bf16[4,80,1280]{2,1,0:T(8,128)(2,1)}, bf16[4,80,1280]{2,1,0:T(8,128)(2,1)}, bf16[4,80,1280]{2,1,0:T(8,128)(2,1)}, bf16[4,80,1280]{2,1,0:...) custom-call(s32[2]{0:T(128)} %pad_add_fusion.2.place_ref, ...), custom_call_target="tpu_custom_call" | custom-call | bytes 1000 | tf_op jit(solution)/shard_map/attention_weights/pallas_call | solution.py:595
  430.2 4.9 add_cores_placed.3
  446.0 9.0 %collective-permute-done.31.refs_5_ = bf16[4,64,1280]{2,1,0:T(8,128)(2,1)S(1)} collective-permute-done((bf16[4,64,1280]{2,1,0:T(8,128)(2,1)}, bf16[4,64,1280]{2,1,0:T(8,128)(2,1)S(1)}, u32[]{:S(2)}, u32[]{:S(2)}) %collective-permute-start.31) | collective-permute-done | bytes 655392 | tf_op jit(solution)/shard_map/ppermute | solution.py:91
  459.2 13.1 %collective-permute-done.33.refs_7_ = bf16[4,64,1280]{2,1,0:T(8,128)(2,1)S(1)} collective-permute-done((bf16[4,64,1280]{2,1,0:T(8,128)(2,1)}, bf16[4,64,1280]{2,1,0:T(8,128)(2,1)S(1)}, u32[]{:S(2)}, u32[]{:S(2)}) %collective-permute-start.33) | collective-permute-done | bytes 655392 | tf_op jit(solution)/shard_map/ppermute | solution.py:91
  481.2 5.6 half_sum.1
  487.0 7.5 %collective-permute-start.38 = (bf16[64,1280]{1,0:T(8,128)(2,1)}, bf16[64,1280]{1,0:T(8,128)(2,1)S(1)}, u32[]{:S(2)}, u32[]{:S(2)}) collective-permute-start(bf16[64,1280]{1,0:T(8,128)(2,1)} %get-tuple-element.97), channel_id=1, source_target_pairs={{64,0},{72,8},{80,16},{88,24},{96,32},{104,40},{112,48},{120,56},{... | collective-permute-start | bytes 491528 | tf_op jit(solution)/shard_map/ppermute | solution.py:91
  519.6 11.2 %collective-permute-start.43 = (bf16[4,144,768]{2,1,0:T(8,128)(2,1)}, bf16[4,144,768]{2,1,0:T(8,128)(2,1)}, u32[]{:S(2)}, u32[]{:S(2)}) collective-permute-start(bf16[4,144,768]{2,1,0:T(8,128)(2,1)} %pad_maximum_fusion.8.mine_ref), channel_id=1, source_target_pairs={{0,1},{1,0},{2,3},{3,2},{4,5},{5,4},{6,7},{7,6},{8,9},{9,8},{10,11... | collective-permute-start | bytes 2654216 | tf_op jit(solution)/shard_map/ppermute | solution.py:43
  530.8 11.5 %experts_results.1 = (f32[2048,768]{1,0:T(8,128)}, f32[2048,768]{1,0:T(8,128)}, f32[768,2048]{1,0:T(8,128)}) custom-call(bf16[8,288,2048]{2,1,0:T(8,128)(2,1)} %bitcast.167), custom_call_target="tpu_custom_call" | custom-call | bytes 1000 | tf_op jit(solution)/shard_map/experts_results/pallas_call | solution.py:520
  558.8 4.7 columns_results.1
  (251 shorter events, 186.7 us)
Async XLA Ops:
  7.2 92.5 %all-gather.7.cloned.1.call-start = ((), (), s32[]{:S(2)}) async-start(), calls=%async_computation.3 | async-start | bytes 6266880 | tf_op jit(solution)/shard_map/all_gather | solution.py:866
  23.3 185.6 %all-gather.9.cloned.1.call-start = ((), (), s32[]{:S(2)}) async-start(), calls=%async_computation.4 | async-start | bytes 20054016 | tf_op jit(solution)/shard_map/all_gather | solution.py:869
  31.7 392.2 %reduce-scatter.4.cloned.1.call-start = ((), (), s32[]{:S(2)}) async-start(), calls=%async_computation.6 | async-start | bytes 20054016
  31.8 15.1 %collective-permute-start.1 = (bf16[2,64,2048]{2,1,0:T(8,128)(2,1)S(1)}, bf16[2,64,2048]{2,1,0:T(8,128)(2,1)S(1)}, u32[]{:S(2)}, u32[]{:S(2)}) collective-permute-start(bf16[2,64,2048]{2,1,0:T(8,128)(2,1)S(1)} %bitcast.168), channel_id=1, source_target_pairs={{4,0},{6,2},{0,4},{2,6},{5,1},{7,3},{1,5},{3,7},{12,8},{14,10},{8,... | collective-permute-start | bytes 1572872 | tf_op jit(solution)/shard_map/ppermute | solution.py:49
  31.9 25.9 %collective-permute-start = (bf16[2,64,2048]{2,1,0:T(8,128)(2,1)S(1)}, bf16[2,64,2048]{2,1,0:T(8,128)(2,1)S(1)}, u32[]{:S(2)}, u32[]{:S(2)}) collective-permute-start(bf16[2,64,2048]{2,1,0:T(8,128)(2,1)S(1)} %bitcast.169), channel_id=1, source_target_pairs={{2,0},{4,2},{6,4},{0,6},{3,1},{5,3},{7,5},{1,7},{10,8},{12,10},{14... | collective-permute-start | bytes 1572872 | tf_op jit(solution)/shard_map/ppermute | solution.py:49
  35.1 23.5 %collective-permute-start.2 = (bf16[2,64,2048]{2,1,0:T(8,128)(2,1)S(1)}, bf16[2,64,2048]{2,1,0:T(8,128)(2,1)}, u32[]{:S(2)}, u32[]{:S(2)}) collective-permute-start(bf16[2,64,2048]{2,1,0:T(8,128)(2,1)S(1)} %bitcast.170), channel_id=1, source_target_pairs={{6,0},{0,2},{2,4},{4,6},{7,1},{1,3},{3,5},{5,7},{14,8},{8,10},{10,... | collective-permute-start | bytes 1572872 | tf_op jit(solution)/shard_map/ppermute | solution.py:49
  35.9 34.9 %collective-permute-start.8 = (bf16[2,64,2176]{2,1,0:T(8,128)(2,1)S(1)}, bf16[2,64,2176]{2,1,0:T(8,128)(2,1)S(1)}, u32[]{:S(2)}, u32[]{:S(2)}) collective-permute-start(bf16[2,64,2176]{2,1,0:T(8,128)(2,1)S(1)} %concatenate.52), channel_id=1, source_target_pairs={{6,0},{0,2},{2,4},{4,6},{7,1},{1,3},{3,5},{5,7},{14,8},{8,10},{10,... | collective-permute-start | bytes 1671176 | tf_op jit(solution)/shard_map/ppermute | solution.py:49
  37.5 44.6 %collective-permute-start.7 = (bf16[2,64,2176]{2,1,0:T(8,128)(2,1)S(1)}, bf16[2,64,2176]{2,1,0:T(8,128)(2,1)S(1)}, u32[]{:S(2)}, u32[]{:S(2)}) collective-permute-start(bf16[2,64,2176]{2,1,0:T(8,128)(2,1)S(1)} %concatenate.52), channel_id=1, source_target_pairs={{4,0},{6,2},{0,4},{2,6},{5,1},{7,3},{1,5},{3,7},{12,8},{14,10},{8,... | collective-permute-start | bytes 1671176 | tf_op jit(solution)/shard_map/ppermute | solution.py:49
  47.0 35.2 %collective-permute-start.6 = (bf16[2,64,2176]{2,1,0:T(8,128)(2,1)S(1)}, bf16[2,64,2176]{2,1,0:T(8,128)(2,1)S(1)}, u32[]{:S(2)}, u32[]{:S(2)}) collective-permute-start(bf16[2,64,2176]{2,1,0:T(8,128)(2,1)S(1)} %concatenate.52), channel_id=1, source_target_pairs={{2,0},{4,2},{6,4},{0,6},{3,1},{5,3},{7,5},{1,7},{10,8},{12,10},{14... | collective-permute-start | bytes 1671176 | tf_op jit(solution)/shard_map/ppermute | solution.py:49
  62.0 28.8 %collective-permute-start.3 = (bf16[4,2,64,2048]{3,2,1,0:T(8,128)(2,1)}, bf16[4,2,64,2048]{3,2,1,0:T(8,128)(2,1)}, u32[]{:S(2)}, u32[]{:S(2)}) collective-permute-start(bf16[4,2,64,2048]{3,2,1,0:T(8,128)(2,1)} %get-tuple-element.187), channel_id=1, source_target_pairs={{0,1},{1,0},{2,3},{3,2},{4,5},{5,4},{6,7},{7,6},{8,9},{9,8},{10,11... | collective-permute-start | bytes 6291464 | tf_op jit(solution)/shard_map/ppermute | solution.py:43
  133.6 23.2 %collective-permute-start.12 = (bf16[2,64,2048]{2,1,0:T(8,128)(2,1)S(1)}, bf16[2,64,2048]{2,1,0:T(8,128)(2,1)S(1)}, u32[]{:S(2)}, u32[]{:S(2)}) collective-permute-start(bf16[2,64,2048]{2,1,0:T(8,128)(2,1)S(1)} %get-tuple-element.181), channel_id=1, source_target_pairs={{0,4},{2,6},{4,0},{6,2},{1,5},{3,7},{5,1},{7,3},{8,12},{10,14},{12... | collective-permute-start | bytes 1572872 | tf_op jit(solution)/shard_map/ppermute | solution.py:62
  161.6 23.9 %collective-permute-start.14 = (bf16[2,64,2048]{2,1,0:T(8,128)(2,1)S(1)}, bf16[2,64,2048]{2,1,0:T(8,128)(2,1)S(1)}, u32[]{:S(2)}, u32[]{:S(2)}) collective-permute-start(bf16[2,64,2048]{2,1,0:T(8,128)(2,1)S(1)} %multiply_convert_fusion), channel_id=1, source_target_pairs={{2,0},{4,2},{6,4},{0,6},{3,1},{5,3},{7,5},{1,7},{10,8},{12,10},{14... | collective-permute-start | bytes 1572872 | tf_op jit(solution)/shard_map/ppermute | solution.py:49
  162.8 22.7 %collective-permute-start.16 = (bf16[2,64,2048]{2,1,0:T(8,128)(2,1)S(1)}, bf16[2,64,2048]{2,1,0:T(8,128)(2,1)S(1)}, u32[]{:S(2)}, u32[]{:S(2)}) collective-permute-start(bf16[2,64,2048]{2,1,0:T(8,128)(2,1)S(1)} %multiply_convert_fusion), channel_id=1, source_target_pairs={{6,0},{0,2},{2,4},{4,6},{7,1},{1,3},{3,5},{5,7},{14,8},{8,10},{10,... | collective-permute-start | bytes 1572872 | tf_op jit(solution)/shard_map/ppermute | solution.py:49
  284.7 17.8 %collective-permute-start.19 = (bf16[4,2,64,2048]{3,2,1,0:T(8,128)(2,1)}, bf16[4,2,64,2048]{3,2,1,0:T(8,128)(2,1)S(1)}, u32[]{:S(2)}, u32[]{:S(2)}) collective-permute-start(bf16[4,2,64,2048]{3,2,1,0:T(8,128)(2,1)} %bitcast.220), channel_id=1, source_target_pairs={{0,1},{1,0},{2,3},{3,2},{4,5},{5,4},{6,7},{7,6},{8,9},{9,8},{10,11... | collective-permute-start | bytes 6291464 | tf_op jit(solution)/shard_map/ppermute | solution.py:43
  307.6 15.8 %collective-permute-start.20 = (bf16[2,64,2048]{2,1,0:T(8,128)(2,1)}, bf16[2,64,2048]{2,1,0:T(8,128)(2,1)S(1)}, u32[]{:S(2)}, u32[]{:S(2)}) collective-permute-start(bf16[2,64,2048]{2,1,0:T(8,128)(2,1)} %get-tuple-element.71), channel_id=1, source_target_pairs={{0,2},{2,4},{4,6},{6,0},{1,3},{3,5},{5,7},{7,1},{8,10},{10,12},{12... | collective-permute-start | bytes 1572872 | tf_op jit(solution)/shard_map/ppermute | solution.py:62
  308.5 23.8 %collective-permute-start.21 = (bf16[2,64,2048]{2,1,0:T(8,128)(2,1)}, bf16[2,64,2048]{2,1,0:T(8,128)(2,1)S(1)}, u32[]{:S(2)}, u32[]{:S(2)}) collective-permute-start(bf16[2,64,2048]{2,1,0:T(8,128)(2,1)} %get-tuple-element.72), channel_id=1, source_target_pairs={{0,4},{2,6},{4,0},{6,2},{1,5},{3,7},{5,1},{7,3},{8,12},{10,14},{12... | collective-permute-start | bytes 1572872 | tf_op jit(solution)/shard_map/ppermute | solution.py:62
  309.0 24.8 %collective-permute-start.22 = (bf16[2,64,2048]{2,1,0:T(8,128)(2,1)}, bf16[2,64,2048]{2,1,0:T(8,128)(2,1)S(1)}, u32[]{:S(2)}, u32[]{:S(2)}) collective-permute-start(bf16[2,64,2048]{2,1,0:T(8,128)(2,1)} %get-tuple-element.73), channel_id=1, source_target_pairs={{0,6},{2,0},{4,2},{6,4},{1,7},{3,1},{5,3},{7,5},{8,14},{10,8},{12,... | collective-permute-start | bytes 1572872 | tf_op jit(solution)/shard_map/ppermute | solution.py:62
  322.0 19.4 %collective-permute-start.18 = (bf16[4,2,64,2048]{3,2,1,0:T(8,128)(2,1)}, bf16[4,2,64,2048]{3,2,1,0:T(8,128)(2,1)}, u32[]{:S(2)}, u32[]{:S(2)}) collective-permute-start(bf16[4,2,64,2048]{3,2,1,0:T(8,128)(2,1)} %bitcast.219), channel_id=1, source_target_pairs={{0,1},{1,0},{2,3},{3,2},{4,5},{5,4},{6,7},{7,6},{8,9},{9,8},{10,11... | collective-permute-start | bytes 6291464 | tf_op jit(solution)/shard_map/ppermute | solution.py:43
  338.9 22.3 %collective-permute-start.24 = (bf16[2,64,2048]{2,1,0:T(8,128)(2,1)S(1)}, bf16[2,64,2048]{2,1,0:T(8,128)(2,1)S(1)}, u32[]{:S(2)}, u32[]{:S(2)}) collective-permute-start(bf16[2,64,2048]{2,1,0:T(8,128)(2,1)S(1)} %fusion.38), channel_id=1, source_target_pairs={{4,0},{6,2},{0,4},{2,6},{5,1},{7,3},{1,5},{3,7},{12,8},{14,10},{8,... | collective-permute-start | bytes 1572872 | tf_op jit(solution)/shard_map/ppermute | solution.py:49
  338.9 24.0 %collective-permute-start.23 = (bf16[2,64,2048]{2,1,0:T(8,128)(2,1)S(1)}, bf16[2,64,2048]{2,1,0:T(8,128)(2,1)}, u32[]{:S(2)}, u32[]{:S(2)}) collective-permute-start(bf16[2,64,2048]{2,1,0:T(8,128)(2,1)S(1)} %fusion.38), channel_id=1, source_target_pairs={{2,0},{4,2},{6,4},{0,6},{3,1},{5,3},{7,5},{1,7},{10,8},{12,10},{14... | collective-permute-start | bytes 1572872 | tf_op jit(solution)/shard_map/ppermute | solution.py:49
  367.2 40.6 %all-to-all-start = ((bf16[4,2,64,2048]{3,2,1,0:T(8,128)(2,1)}), bf16[4,2,64,2048]{3,2,1,0:T(8,128)(2,1)S(1)}, u32[]{:S(2)}, u32[]{:S(2)}) async-start(bf16[4,2,64,2048]{3,2,1,0:T(8,128)(2,1)} %add_cores_placed.2.refs_0_.token_ref), calls=%async_computation | async-start | bytes 4194304 | tf_op jit(solution)/shard_map/all_to_all | solution.py:481
  372.5 158.3 %all-gather.11.cloned.1.call-start = ((), (), s32[]{:S(2)}) async-start(), calls=%async_computation.5 | async-start | bytes 10616832 | tf_op jit(solution)/shard_map/all_gather | solution.py:1028
  435.1 65.4 %all-to-all-start.1 = ((bf16[4,2,64,2048]{3,2,1,0:T(8,128)(2,1)}), bf16[4,2,64,2048]{3,2,1,0:T(8,128)(2,1)S(1)}, u32[]{:S(2)}, u32[]{:S(2)}) async-start(bf16[4,2,64,2048]{3,2,1,0:T(8,128)(2,1)} %add_cores_placed.3), calls=%async_computation.1 | async-start | bytes 4194304 | tf_op jit(solution)/shard_map/all_to_all | solution.py:481
  439.5 15.6 %collective-permute-start.31 = (bf16[4,64,1280]{2,1,0:T(8,128)(2,1)}, bf16[4,64,1280]{2,1,0:T(8,128)(2,1)S(1)}, u32[]{:S(2)}, u32[]{:S(2)}) collective-permute-start(bf16[4,64,1280]{2,1,0:T(8,128)(2,1)} %get-tuple-element.88), channel_id=1, source_target_pairs={{24,0},{0,8},{8,16},{16,24},{56,32},{32,40},{40,48},{48,56},{88,64... | collective-permute-start | bytes 1966088 | tf_op jit(solution)/shard_map/ppermute | solution.py:91
  440.9 31.5 %collective-permute-start.29 = (bf16[4,80,1280]{2,1,0:T(8,128)(2,1)}, bf16[4,80,1280]{2,1,0:T(8,128)(2,1)S(1)}, u32[]{:S(2)}, u32[]{:S(2)}) collective-permute-start(bf16[4,80,1280]{2,1,0:T(8,128)(2,1)} %get-tuple-element.85), channel_id=1, source_target_pairs={{64,0},{72,8},{80,16},{88,24},{96,32},{104,40},{112,48},{120,56},{... | collective-permute-start | bytes 2457608 | tf_op jit(solution)/shard_map/ppermute | solution.py:91
  441.0 35.8 %collective-permute-start.30 = (bf16[4,80,1280]{2,1,0:T(8,128)(2,1)}, bf16[4,80,1280]{2,1,0:T(8,128)(2,1)S(1)}, u32[]{:S(2)}, u32[]{:S(2)}) collective-permute-start(bf16[4,80,1280]{2,1,0:T(8,128)(2,1)} %get-tuple-element.86), channel_id=1, source_target_pairs={{32,0},{40,8},{48,16},{56,24},{64,32},{72,40},{80,48},{88,56},{96,... | collective-permute-start | bytes 2457608 | tf_op jit(solution)/shard_map/ppermute | solution.py:91
  442.1 38.2 %collective-permute-start.28 = (bf16[4,80,1280]{2,1,0:T(8,128)(2,1)S(1)}, bf16[4,80,1280]{2,1,0:T(8,128)(2,1)S(1)}, u32[]{:S(2)}, u32[]{:S(2)}) collective-permute-start(bf16[4,80,1280]{2,1,0:T(8,128)(2,1)S(1)} %copy-done.10), channel_id=1, source_target_pairs={{96,0},{104,8},{112,16},{120,24},{0,32},{8,40},{16,48},{24,56},{32... | collective-permute-start | bytes 2457608 | tf_op jit(solution)/shard_map/ppermute | solution.py:91
  442.5 16.7 %collective-permute-start.32 = (bf16[4,64,1280]{2,1,0:T(8,128)(2,1)}, bf16[4,64,1280]{2,1,0:T(8,128)(2,1)S(1)}, u32[]{:S(2)}, u32[]{:S(2)}) collective-permute-start(bf16[4,64,1280]{2,1,0:T(8,128)(2,1)} %get-tuple-element.89), channel_id=1, source_target_pairs={{16,0},{24,8},{0,16},{8,24},{48,32},{56,40},{32,48},{40,56},{80,64... | collective-permute-start | bytes 1966088 | tf_op jit(solution)/shard_map/ppermute | solution.py:91
  455.1 17.3 %collective-permute-start.33 = (bf16[4,64,1280]{2,1,0:T(8,128)(2,1)}, bf16[4,64,1280]{2,1,0:T(8,128)(2,1)S(1)}, u32[]{:S(2)}, u32[]{:S(2)}) collective-permute-start(bf16[4,64,1280]{2,1,0:T(8,128)(2,1)} %get-tuple-element.90), channel_id=1, source_target_pairs={{8,0},{16,8},{24,16},{0,24},{40,32},{48,40},{56,48},{32,56},{72,64... | collective-permute-start | bytes 1966088 | tf_op jit(solution)/shard_map/ppermute | solution.py:91
  487.0 14.8 %collective-permute-start.38 = (bf16[64,1280]{1,0:T(8,128)(2,1)}, bf16[64,1280]{1,0:T(8,128)(2,1)S(1)}, u32[]{:S(2)}, u32[]{:S(2)}) collective-permute-start(bf16[64,1280]{1,0:T(8,128)(2,1)} %get-tuple-element.97), channel_id=1, source_target_pairs={{64,0},{72,8},{80,16},{88,24},{96,32},{104,40},{112,48},{120,56},{... | collective-permute-start | bytes 491528 | tf_op jit(solution)/shard_map/ppermute | solution.py:91
  513.5 28.8 %collective-permute-start.44 = (bf16[32,2048]{1,0:T(8,128)(2,1)S(1)}, bf16[32,2048]{1,0:T(8,128)(2,1)S(1)}, u32[]{:S(2)}, u32[]{:S(2)}) collective-permute-start(bf16[32,2048]{1,0:T(8,128)(2,1)S(1)} %pad_maximum_fusion.12), channel_id=1, source_target_pairs={{0,0},{8,1},{16,2},{24,3},{32,4},{40,5},{48,6},{56,7},{64,8},{72,9... | collective-permute-start | bytes 393224 | tf_op jit(solution)/shard_map/ppermute | solution.py:1040
  519.6 39.2 %collective-permute-start.43 = (bf16[4,144,768]{2,1,0:T(8,128)(2,1)}, bf16[4,144,768]{2,1,0:T(8,128)(2,1)}, u32[]{:S(2)}, u32[]{:S(2)}) collective-permute-start(bf16[4,144,768]{2,1,0:T(8,128)(2,1)} %pad_maximum_fusion.8.mine_ref), channel_id=1, source_target_pairs={{0,1},{1,0},{2,3},{3,2},{4,5},{5,4},{6,7},{7,6},{8,9},{9,8},{10,11... | collective-permute-start | bytes 2654216 | tf_op jit(solution)/shard_map/ppermute | solution.py:43
  (57 other events, 719.9 us)
Sparse Core Ops, SparseCore 0:
  23.4 61.4 all-gather.6
  87.0 121.7 all-gather.8
  284.8 120.8 reduce-scatter.3
  424.1 75.1 all-gather.10

commit v3 on v2

--- a/solution.py
+++ b/solution.py
@@ -652,25 +652,25 @@
     return outs[:SIDE], outs[SIDE:]
 
 
-def last_sum_kernel(token_ref, *refs):
+def last_sum_kernel(token_ref, other_token_ref, *refs):
     out = refs[-1]
     cut = refs[0].shape[0]
     out[:cut] = total_of(refs[:SIDE])
     out[cut:] = total_of(refs[SIDE : 2 * SIDE])
 
 
-def last_sum_call(firsts, seconds, token):
+def last_sum_call(firsts, seconds, *tokens):
     rows, columns = firsts[0].shape[0] + seconds[0].shape[0], firsts[0].shape[1]
     vmem = pl.BlockSpec(memory_space=pltpu.VMEM)
     return pl.pallas_call(
         last_sum_kernel,
-        in_specs=[pl.BlockSpec(memory_space=pl.ANY)] + [vmem] * (2 * SIDE),
+        in_specs=[pl.BlockSpec(memory_space=pl.ANY)] * 2 + [vmem] * (2 * SIDE),
         out_specs=vmem,
         out_shape=jax.ShapeDtypeStruct((rows, columns), BF16),
         compiler_params=pltpu.CompilerParams(vmem_limit_bytes=VMEM),
         cost_estimate=TINY,
         name="last_sum",
-    )(token, *firsts, *seconds)
+    )(*tokens, *firsts, *seconds)
 
 
 def plane_send(pieces, dx, dz):
@@ -944,7 +944,7 @@
     grad_gain_moe = jnp.sum(d_h2 * x1 * inverse_mid, axis=(0, 1))
     d_x1 = dy_own.astype(F32) + norm_back(d_h2, x1, inverse_mid, gain_moe)
     grad_experts = lax.psum_scatter(
-        grad_experts, "experts", scatter_dimension=0, tiled=False
+        after_call(grad_experts, pieces[1]), "experts", scatter_dimension=0, tiled=False
     )
     moe_pieces = add_placed_call(
         where, swap(moe_theirs.reshape(shape)), moe_mine.reshape(shape), hidden
@@ -1021,15 +1021,16 @@
     firsts, seconds = attend_grads_call(
         place, h1, d_qkv, grad_out, grad_gains, output, depth // 2 + 16
     )
-    d_h1 = exchange_sum(add_placed_call(where, swap(theirs[0]), mine[0], firsts[1]))
+    h1_pieces = add_placed_call(where, swap(theirs[0]), mine[0], firsts[1])
+    d_h1 = exchange_sum(h1_pieces)
     x_f32 = x_own.astype(F32)
     input_grad = (d_x1 + norm_back(d_h1, x_f32, inverse_rms(x_f32), gain_attn))[:, None]
-    grad_experts = after_call(grad_experts, firsts[1])
+    grad_experts = after_call(grad_experts, h1_pieces)
     all_experts = lax.all_gather(grad_experts, GROUP, axis=0, tiled=False)
     firsts, seconds = plane_send(firsts, 1, 0), plane_send(seconds, 0, 1)
     firsts, seconds = half_sum_call(place, firsts, seconds, grad_out)
-    grads = last_sum_call(plane_send(firsts, 0, 1), plane_send(seconds, 1, 0), d_h1)
     result_gate, result_up, result_down = gate_up_down_call(all_experts, ff_part)
+    grads = last_sum_call(plane_send(firsts, 0, 1), plane_send(seconds, 1, 0), d_h1, result_down)
     out_sum = jnp.concatenate(
         [grads[k * out_part : (k + 1) * out_part, qkv_width:] for k in range(depth // out_part)],
         axis=1,
@@ -1037,7 +1038,7 @@
     result_q, result_k, result_v, gain_sum = columns_call(
         where, *gather_members(grads[:, :qkv_width]), depth, q_width, head
     )
-    out_sum = after_call(lax.ppermute(out_sum, EVERY, back), result_down)
+    out_sum = after_call(lax.ppermute(out_sum, EVERY, back), input_grad)
     result_out = rows_call(where, *gather_members(out_sum))
     gain_sum = gain_sum[0]
     return (

time: 588 us -> 566 us (0.963)
  the two profiles are of different devices: /device:TPU:49 before, /device:TPU:9 now
where the time goes in v3:
time: 566 us; the launch traced here: 555 us
  Pallas kernels  195 us (34%)
  waiting for transfers between devices  193 us (34%)
  starting transfers between devices  76.3 us (13%)
  other arithmetic  50 us (9%)
  local copies, waits for them, and re-layouts  25.9 us (5%)
  between operations  14.8 us (3%)
    ppermute x12, waiting for transfers between devices, ring_stack(): lax.ppermute(own, 'context', [((i + k) % ring, i) for i in range(ring)])  78.5 us
    pallas_call x1, Pallas kernels, experts_call(): pl.pallas_call(functools.partial(experts_kernel, part), grid=(n, blocks),...  48.9 us
    pallas_call x2, Pallas kernels, attend_call(): pl.pallas_call(kernel, grid=(2 * micro,), in_specs=in_specs, out_specs=ou...  48.5 us
    ppermute x12, waiting for transfers between devices, plane(): return lax.ppermute(v, 'experts', moves)  33.1 us
    ppermute x6, waiting for transfers between devices, ring_sum(): lax.ppermute(pieces[k], 'context', [(i, (i + k) % ring) for i in range(ri...  32.7 us
    pallas_call x1, Pallas kernels, expert_grads_call(): pl.pallas_call(functools.partial(expert_grads_kernel, part), grid=(n,), i...  27 us
    ppermute x12, starting transfers between devices, ring_stack(): lax.ppermute(own, 'context', [((i + k) % ring, i) for i in range(ring)])  19.3 us
    another operation x6, other arithmetic, gather_rows(): return jnp.stack([mine, swap(mine)])  17.7 us
  transfers between devices with their start and end apart: 55, of which 29 were waited for; matrix products, arithmetic and copies ran while one was open for 11% of the time, Pallas kernels for 24%

profile of v3, /device:TPU:9, one launch (start us, length us, event | category | flops | bytes accessed | tf_op | source)
XLA Modules:
  0.0 555.3 jit_solution(3748711594065945953)
XLA Ops:
  8.3 6.1 %collective-permute-start.4 = (bf16[32,2048]{1,0:T(8,128)(2,1)S(1)}, bf16[32,2048]{1,0:T(8,128)(2,1)S(1)}, u32[]{:S(2)}, u32[]{:S(2)}) collective-permute-start(bf16[32,2048]{1,0:T(8,128)(2,1)S(1)} %constant_dynamic-slice_fusion.2), channel_id=1, source_target_pairs={{0,0},{1,8},{2,16},{3,24},{4,32},{5,40},{6,48},{7,56},{8,64},{9,72... | collective-permute-start | bytes 393224 | tf_op jit(solution)/shard_map/ppermute | solution.py:843
  28.8 8.3 %collective-permute-start.1 = (bf16[2,64,2048]{2,1,0:T(8,128)(2,1)S(1)}, bf16[2,64,2048]{2,1,0:T(8,128)(2,1)S(1)}, u32[]{:S(2)}, u32[]{:S(2)}) collective-permute-start(bf16[2,64,2048]{2,1,0:T(8,128)(2,1)S(1)} %bitcast.166), channel_id=1, source_target_pairs={{4,0},{6,2},{0,4},{2,6},{5,1},{7,3},{1,5},{3,7},{12,8},{14,10},{8,... | collective-permute-start | bytes 1572872 | tf_op jit(solution)/shard_map/ppermute | solution.py:49
  41.3 8.6 %collective-permute-done.1 = bf16[2,64,2048]{2,1,0:T(8,128)(2,1)S(1)} collective-permute-done((bf16[2,64,2048]{2,1,0:T(8,128)(2,1)S(1)}, bf16[2,64,2048]{2,1,0:T(8,128)(2,1)S(1)}, u32[]{:S(2)}, u32[]{:S(2)}) %collective-permute-start.1) | collective-permute-done | bytes 524320 | tf_op jit(solution)/shard_map/ppermute | solution.py:49
  49.9 11.3 %collective-permute-done = bf16[2,64,2048]{2,1,0:T(8,128)(2,1)S(1)} collective-permute-done((bf16[2,64,2048]{2,1,0:T(8,128)(2,1)S(1)}, bf16[2,64,2048]{2,1,0:T(8,128)(2,1)S(1)}, u32[]{:S(2)}, u32[]{:S(2)}) %collective-permute-start) | collective-permute-done | bytes 524320 | tf_op jit(solution)/shard_map/ppermute | solution.py:49
  64.5 8.5 %collective-permute-done.8 = bf16[2,64,2176]{2,1,0:T(8,128)(2,1)S(1)} collective-permute-done((bf16[2,64,2176]{2,1,0:T(8,128)(2,1)S(1)}, bf16[2,64,2176]{2,1,0:T(8,128)(2,1)S(1)}, u32[]{:S(2)}, u32[]{:S(2)}) %collective-permute-start.8) | collective-permute-done | bytes 557088 | tf_op jit(solution)/shard_map/ppermute | solution.py:49
  73.1 9.3 %collective-permute-done.6 = bf16[2,64,2176]{2,1,0:T(8,128)(2,1)S(1)} collective-permute-done((bf16[2,64,2176]{2,1,0:T(8,128)(2,1)S(1)}, bf16[2,64,2176]{2,1,0:T(8,128)(2,1)S(1)}, u32[]{:S(2)}, u32[]{:S(2)}) %collective-permute-start.6) | collective-permute-done | bytes 557088 | tf_op jit(solution)/shard_map/ppermute | solution.py:49
  90.6 4.6 pad_maximum_fusion.1.x_ref
  102.3 21.9 %attention.1 = (bf16[2,4,2,64,2048]{4,3,2,1,0:T(8,128)(2,1)}, f32[2,4,2,64,768]{4,3,2,1,0:T(8,128)}, bf16[2,4,2,64,512]{4,3,2,1,0:T(8,128)(2,1)}, bf16[1,4,2,64,...) custom-call(bf16[2,4,2,64,2048]{4,3,2,1,0:T(8,128)(2,1)} %pad_maximum_fusion.1.x_ref, f32[1,2048]{1,0:T(1,128)} %bitcast.202, ...), custom_call_target="tpu_custom_call" | custom-call | bytes 1000 | tf_op jit(solution)/shard_map/attention/pallas_call | solution.py:326
  136.1 9.6 %collective-permute-done.11 = bf16[2,64,2048]{2,1,0:T(8,128)(2,1)S(1)} collective-permute-done((bf16[2,64,2048]{2,1,0:T(8,128)(2,1)S(1)}, bf16[2,64,2048]{2,1,0:T(8,128)(2,1)S(1)}, u32[]{:S(2)}, u32[]{:S(2)}) %collective-permute-start.11) | collective-permute-done | bytes 524320 | tf_op jit(solution)/shard_map/ppermute | solution.py:62
  146.8 12.1 %collective-permute-done.12 = bf16[2,64,2048]{2,1,0:T(8,128)(2,1)S(1)} collective-permute-done((bf16[2,64,2048]{2,1,0:T(8,128)(2,1)S(1)}, bf16[2,64,2048]{2,1,0:T(8,128)(2,1)S(1)}, u32[]{:S(2)}, u32[]{:S(2)}) %collective-permute-start.12) | collective-permute-done | bytes 524320 | tf_op jit(solution)/shard_map/ppermute | solution.py:62
  164.2 10.2 %collective-permute-done.15 = bf16[2,64,2048]{2,1,0:T(8,128)(2,1)S(1)} collective-permute-done((bf16[2,64,2048]{2,1,0:T(8,128)(2,1)S(1)}, bf16[2,64,2048]{2,1,0:T(8,128)(2,1)S(1)}, u32[]{:S(2)}, u32[]{:S(2)}) %collective-permute-start.15) | collective-permute-done | bytes 524320 | tf_op jit(solution)/shard_map/ppermute | solution.py:49
  174.5 13.0 %collective-permute-done.14 = bf16[2,64,2048]{2,1,0:T(8,128)(2,1)S(1)} collective-permute-done((bf16[2,64,2048]{2,1,0:T(8,128)(2,1)S(1)}, bf16[2,64,2048]{2,1,0:T(8,128)(2,1)S(1)}, u32[]{:S(2)}, u32[]{:S(2)}) %collective-permute-start.14) | collective-permute-done | bytes 524320 | tf_op jit(solution)/shard_map/ppermute | solution.py:49
  194.4 15.1 %all-gather.9.cloned.1.call-done = bf16[4608,2048]{1,0:T(8,128)(2,1)} async-done(((bf16[288,2048]{1,0:T(8,128)(2,1)}), bf16[4608,2048]{1,0:T(8,128)(2,1)}) %all-gather.9.cloned.1.call-update) | async-done | bytes 18874384 | tf_op jit(solution)/shard_map/all_gather | solution.py:869
  209.5 48.9 %experts_rows.1 = (bf16[1024,1536]{1,0:T(8,128)(2,1)}, bf16[1024,1536]{1,0:T(8,128)(2,1)}, bf16[1024,1536]{1,0:T(8,128)(2,1)}, bf16[512,2048]{1,0:T(8,128)(2,1)}, bf16[512,2048]{1,0:T(8,128)(2,1)}) custom-call(bf16[1024,2048]{1,0:T(8,128)(2,1)} %bitcast.156, bf16[1024,2176]{1,0:T(8,128)(2,1)} %bitcast.154, bf16[16,288,2048]{2,1,0:T(8,128)(2,1)} %bitcast.163, ...), custom_call_target="tpu_custom_call" | custom-call | bytes 1000 | tf_op jit(solution)/shard_map/experts_rows/pallas_call | solution.py:388
  259.2 27.0 %experts_weights.1 = (bf16[16,288,2048]{2,1,0:T(8,128)(2,1)}, f32[8,128]{1,0:T(8,128)}) custom-call(bf16[1024,1536]{1,0:T(8,128)(2,1)} %get-tuple-element.63.dg_ref, bf16[1024,1536]{1,0:T(8,128)(2,1)} %get-tuple-element.64.du_ref, bf16[1024,1536]{1,0:T(8,128)(2,1)} %get-tuple-element.62.hid_ref.token_ref, bf16[1024,2048]{1,0:T(8,128)(2,1)} %bitcast.157, ...), custom_call_target="tpu_custom_call" | custom-call | bytes 1000 | tf_op jit(solution)/shard_map/experts_weights/pallas_call | solution.py:431
  296.2 12.1 %experts_out.1 = (bf16[512,2048]{1,0:T(8,128)(2,1)}, bf16[512,2048]{1,0:T(8,128)(2,1)}) custom-call(bf16[1024,1536]{1,0:T(8,128)(2,1)} %get-tuple-element.62.hid_ref.token_ref, bf16[16,288,2048]{2,1,0:T(8,128)(2,1)} %bitcast.164, f32[8,128]{1,0:T(8,128)} %get-tuple-element.65.token_ref), custom_call_target="tpu_custom_call" | custom-call | flops 6442450944 | bytes 20000000 | tf_op jit(solution)/shard_map/experts_out/pallas_call | solution.py:777
  309.2 9.9 %collective-permute-done.22 = bf16[2,64,2048]{2,1,0:T(8,128)(2,1)S(1)} collective-permute-done((bf16[2,64,2048]{2,1,0:T(8,128)(2,1)}, bf16[2,64,2048]{2,1,0:T(8,128)(2,1)S(1)}, u32[]{:S(2)}, u32[]{:S(2)}) %collective-permute-start.22) | collective-permute-done | bytes 524320 | tf_op jit(solution)/shard_map/ppermute | solution.py:62
  327.0 4.8 add_cores_placed.2.refs_0_.token_ref
  337.2 12.3 %collective-permute-done.23 = bf16[2,64,2048]{2,1,0:T(8,128)(2,1)} collective-permute-done((bf16[2,64,2048]{2,1,0:T(8,128)(2,1)S(1)}, bf16[2,64,2048]{2,1,0:T(8,128)(2,1)}, u32[]{:S(2)}, u32[]{:S(2)}) %collective-permute-start.23) | collective-permute-done | bytes 524320 | tf_op jit(solution)/shard_map/ppermute | solution.py:49
  357.0 6.5 %out_weights.1 = bf16[512,2048]{1,0:T(8,128)(2,1)} custom-call(bf16[2,512,512]{2,1,0:T(8,128)(2,1)} %bitcast.185, bf16[512,2048]{1,0:T(8,128)(2,1)} %bitcast.158, bf16[512,2048]{1,0:T(8,128)(2,1)} %bitcast.60.theirs_ref), custom_call_target="tpu_custom_call" | custom-call | bytes 1000 | tf_op jit(solution)/shard_map/out_weights/pallas_call | solution.py:550
  363.6 26.5 %attention_back.1 = (bf16[2,4,2,64,768]{4,3,2,1,0:T(8,128)(2,1)}, bf16[1,4,2,64,2048]{4,3,2,1,0:T(8,128)(2,1)}, bf16[1,4,2,64,2048]{4,3,2,1,0:T(8,128)(2,1)}, f3...) custom-call(bf16[1,4,2,64,2048]{4,3,2,1,0:T(8,128)(2,1)} %bitcast.56.theirs_da_ref, ...), custom_call_target="tpu_custom_call" | custom-call | flops 8999999488 | bytes 90000000 | tf_op jit(solution)/shard_map/attention_back/pallas_call | solution.py:326
  398.8 10.2 %attention_weights.1 = (bf16[4,80,1280]{2,1,0:T(8,128)(2,1)}, bf16[4,80,1280]{2,1,0:T(8,128)(2,1)}, bf16[4,80,1280]{2,1,0:T(8,128)(2,1)}, bf16[4,80,1280]{2,1,0:...) custom-call(s32[2]{0:T(128)} %pad_add_fusion.2.place_ref, ...), custom_call_target="tpu_custom_call" | custom-call | bytes 1000 | tf_op jit(solution)/shard_map/attention_weights/pallas_call | solution.py:595
  409.0 4.8 add_cores_placed.3.refs_0_
  413.8 4.8 all-to-all-start.1
  424.6 11.0 %collective-permute-done.31.refs_5_ = bf16[4,64,1280]{2,1,0:T(8,128)(2,1)S(1)} collective-permute-done((bf16[4,64,1280]{2,1,0:T(8,128)(2,1)}, bf16[4,64,1280]{2,1,0:T(8,128)(2,1)S(1)}, u32[]{:S(2)}, u32[]{:S(2)}) %collective-permute-start.31) | collective-permute-done | bytes 655392 | tf_op jit(solution)/shard_map/ppermute | solution.py:91
  436.7 13.7 %collective-permute-done.32.refs_6_ = bf16[4,64,1280]{2,1,0:T(8,128)(2,1)S(1)} collective-permute-done((bf16[4,64,1280]{2,1,0:T(8,128)(2,1)}, bf16[4,64,1280]{2,1,0:T(8,128)(2,1)S(1)}, u32[]{:S(2)}, u32[]{:S(2)}) %collective-permute-start.32) | collective-permute-done | bytes 655392 | tf_op jit(solution)/shard_map/ppermute | solution.py:91
  459.7 5.6 %half_sum.1 = (bf16[80,1280]{1,0:T(8,128)(2,1)}, bf16[80,1280]{1,0:T(8,128)(2,1)}, bf16[80,1280]{1,0:T(8,128)(2,1)}, bf16[80,1280]{1,0:T(8,128)(2,1)}, bf16[64,1...) custom-call(s32[2]{0:T(128)} %pad_add_fusion.2.place_ref, ...), custom_call_target="tpu_custom_call" | custom-call | bytes 1000 | tf_op jit(solution)/shard_map/half_sum/pallas_call | solution.py:638
  476.8 6.6 %all-gather.11.cloned.1.call-done = bf16[2304,2048]{1,0:T(8,128)(2,1)} async-done(((bf16[288,2048]{1,0:T(8,128)(2,1)}), bf16[2304,2048]{1,0:T(8,128)(2,1)}) %all-gather.11.cloned.1.call-update) | async-done | bytes 9437200 | tf_op jit(solution)/shard_map/all_gather | solution.py:1029
  483.4 11.5 %experts_results.1 = (f32[2048,768]{1,0:T(8,128)}, f32[2048,768]{1,0:T(8,128)}, f32[768,2048]{1,0:T(8,128)}) custom-call(bf16[8,288,2048]{2,1,0:T(8,128)(2,1)} %bitcast.165), custom_call_target="tpu_custom_call" | custom-call | bytes 1000 | tf_op jit(solution)/shard_map/experts_results/pallas_call | solution.py:520
  503.7 5.9 %collective-permute-start.44 = (bf16[32,2048]{1,0:T(8,128)(2,1)S(1)}, bf16[32,2048]{1,0:T(8,128)(2,1)S(1)}, u32[]{:S(2)}, u32[]{:S(2)}) collective-permute-start(bf16[32,2048]{1,0:T(8,128)(2,1)S(1)} %pad_maximum_fusion.12), channel_id=1, source_target_pairs={{0,0},{8,1},{16,2},{24,3},{32,4},{40,5},{48,6},{56,7},{64,8},{72,9... | collective-permute-start | bytes 393224 | tf_op jit(solution)/shard_map/ppermute | solution.py:1041
  512.4 10.0 %collective-permute-done.44.v_ref = bf16[32,2048]{1,0:T(8,128)(2,1)S(1)} collective-permute-done((bf16[32,2048]{1,0:T(8,128)(2,1)S(1)}, bf16[32,2048]{1,0:T(8,128)(2,1)S(1)}, u32[]{:S(2)}, u32[]{:S(2)}) %collective-permute-start.44) | collective-permute-done | bytes 131104 | tf_op jit(solution)/shard_map/ppermute | solution.py:1041
  541.1 4.7 columns_results.1
  (254 shorter events, 165.3 us)
Async XLA Ops:
  7.2 92.2 %all-gather.7.cloned.1.call-start = ((), (), s32[]{:S(2)}) async-start(), calls=%async_computation.3 | async-start | bytes 6266880 | tf_op jit(solution)/shard_map/all_gather | solution.py:866
  20.2 189.3 %all-gather.9.cloned.1.call-start = ((), (), s32[]{:S(2)}) async-start(), calls=%async_computation.4 | async-start | bytes 20054016 | tf_op jit(solution)/shard_map/all_gather | solution.py:869
  28.8 385.0 %reduce-scatter.4.cloned.1.call-start = ((), (), s32[]{:S(2)}) async-start(), calls=%async_computation.6 | async-start | bytes 20054016
  28.8 21.0 %collective-permute-start.1 = (bf16[2,64,2048]{2,1,0:T(8,128)(2,1)S(1)}, bf16[2,64,2048]{2,1,0:T(8,128)(2,1)S(1)}, u32[]{:S(2)}, u32[]{:S(2)}) collective-permute-start(bf16[2,64,2048]{2,1,0:T(8,128)(2,1)S(1)} %bitcast.166), channel_id=1, source_target_pairs={{4,0},{6,2},{0,4},{2,6},{5,1},{7,3},{1,5},{3,7},{12,8},{14,10},{8,... | collective-permute-start | bytes 1572872 | tf_op jit(solution)/shard_map/ppermute | solution.py:49
  37.2 24.0 %collective-permute-start = (bf16[2,64,2048]{2,1,0:T(8,128)(2,1)S(1)}, bf16[2,64,2048]{2,1,0:T(8,128)(2,1)S(1)}, u32[]{:S(2)}, u32[]{:S(2)}) collective-permute-start(bf16[2,64,2048]{2,1,0:T(8,128)(2,1)S(1)} %bitcast.167), channel_id=1, source_target_pairs={{2,0},{4,2},{6,4},{0,6},{3,1},{5,3},{7,5},{1,7},{10,8},{12,10},{14... | collective-permute-start | bytes 1572872 | tf_op jit(solution)/shard_map/ppermute | solution.py:49
  37.2 24.0 %collective-permute-start.2 = (bf16[2,64,2048]{2,1,0:T(8,128)(2,1)S(1)}, bf16[2,64,2048]{2,1,0:T(8,128)(2,1)}, u32[]{:S(2)}, u32[]{:S(2)}) collective-permute-start(bf16[2,64,2048]{2,1,0:T(8,128)(2,1)S(1)} %bitcast.168), channel_id=1, source_target_pairs={{6,0},{0,2},{2,4},{4,6},{7,1},{1,3},{3,5},{5,7},{14,8},{8,10},{10,... | collective-permute-start | bytes 1572872 | tf_op jit(solution)/shard_map/ppermute | solution.py:49
  39.4 33.6 %collective-permute-start.8 = (bf16[2,64,2176]{2,1,0:T(8,128)(2,1)S(1)}, bf16[2,64,2176]{2,1,0:T(8,128)(2,1)S(1)}, u32[]{:S(2)}, u32[]{:S(2)}) collective-permute-start(bf16[2,64,2176]{2,1,0:T(8,128)(2,1)S(1)} %concatenate.52), channel_id=1, source_target_pairs={{6,0},{0,2},{2,4},{4,6},{7,1},{1,3},{3,5},{5,7},{14,8},{8,10},{10,... | collective-permute-start | bytes 1671176 | tf_op jit(solution)/shard_map/ppermute | solution.py:49
  39.5 33.5 %collective-permute-start.7 = (bf16[2,64,2176]{2,1,0:T(8,128)(2,1)S(1)}, bf16[2,64,2176]{2,1,0:T(8,128)(2,1)S(1)}, u32[]{:S(2)}, u32[]{:S(2)}) collective-permute-start(bf16[2,64,2176]{2,1,0:T(8,128)(2,1)S(1)} %concatenate.52), channel_id=1, source_target_pairs={{4,0},{6,2},{0,4},{2,6},{5,1},{7,3},{1,5},{3,7},{12,8},{14,10},{8,... | collective-permute-start | bytes 1671176 | tf_op jit(solution)/shard_map/ppermute | solution.py:49
  49.9 32.5 %collective-permute-start.6 = (bf16[2,64,2176]{2,1,0:T(8,128)(2,1)S(1)}, bf16[2,64,2176]{2,1,0:T(8,128)(2,1)S(1)}, u32[]{:S(2)}, u32[]{:S(2)}) collective-permute-start(bf16[2,64,2176]{2,1,0:T(8,128)(2,1)S(1)} %concatenate.52), channel_id=1, source_target_pairs={{2,0},{4,2},{6,4},{0,6},{3,1},{5,3},{7,5},{1,7},{10,8},{12,10},{14... | collective-permute-start | bytes 1671176 | tf_op jit(solution)/shard_map/ppermute | solution.py:49
  64.5 26.0 %collective-permute-start.3 = (bf16[4,2,64,2048]{3,2,1,0:T(8,128)(2,1)}, bf16[4,2,64,2048]{3,2,1,0:T(8,128)(2,1)}, u32[]{:S(2)}, u32[]{:S(2)}) collective-permute-start(bf16[4,2,64,2048]{3,2,1,0:T(8,128)(2,1)} %get-tuple-element.187), channel_id=1, source_target_pairs={{0,1},{1,0},{2,3},{3,2},{4,5},{5,4},{6,7},{7,6},{8,9},{9,8},{10,11... | collective-permute-start | bytes 6291464 | tf_op jit(solution)/shard_map/ppermute | solution.py:43
  133.6 25.3 %collective-permute-start.12 = (bf16[2,64,2048]{2,1,0:T(8,128)(2,1)S(1)}, bf16[2,64,2048]{2,1,0:T(8,128)(2,1)S(1)}, u32[]{:S(2)}, u32[]{:S(2)}) collective-permute-start(bf16[2,64,2048]{2,1,0:T(8,128)(2,1)S(1)} %get-tuple-element.181), channel_id=1, source_target_pairs={{0,4},{2,6},{4,0},{6,2},{1,5},{3,7},{5,1},{7,3},{8,12},{10,14},{12... | collective-permute-start | bytes 1572872 | tf_op jit(solution)/shard_map/ppermute | solution.py:62
  162.6 24.8 %collective-permute-start.14 = (bf16[2,64,2048]{2,1,0:T(8,128)(2,1)S(1)}, bf16[2,64,2048]{2,1,0:T(8,128)(2,1)S(1)}, u32[]{:S(2)}, u32[]{:S(2)}) collective-permute-start(bf16[2,64,2048]{2,1,0:T(8,128)(2,1)S(1)} %multiply_convert_fusion), channel_id=1, source_target_pairs={{2,0},{4,2},{6,4},{0,6},{3,1},{5,3},{7,5},{1,7},{10,8},{12,10},{14... | collective-permute-start | bytes 1572872 | tf_op jit(solution)/shard_map/ppermute | solution.py:49
  162.6 24.8 %collective-permute-start.16 = (bf16[2,64,2048]{2,1,0:T(8,128)(2,1)S(1)}, bf16[2,64,2048]{2,1,0:T(8,128)(2,1)S(1)}, u32[]{:S(2)}, u32[]{:S(2)}) collective-permute-start(bf16[2,64,2048]{2,1,0:T(8,128)(2,1)S(1)} %multiply_convert_fusion), channel_id=1, source_target_pairs={{6,0},{0,2},{2,4},{4,6},{7,1},{1,3},{3,5},{5,7},{14,8},{8,10},{10,... | collective-permute-start | bytes 1572872 | tf_op jit(solution)/shard_map/ppermute | solution.py:49
  258.4 27.8 %collective-permute-start.19 = (bf16[4,2,64,2048]{3,2,1,0:T(8,128)(2,1)}, bf16[4,2,64,2048]{3,2,1,0:T(8,128)(2,1)S(1)}, u32[]{:S(2)}, u32[]{:S(2)}) collective-permute-start(bf16[4,2,64,2048]{3,2,1,0:T(8,128)(2,1)} %bitcast.215), channel_id=1, source_target_pairs={{0,1},{1,0},{2,3},{3,2},{4,5},{5,4},{6,7},{7,6},{8,9},{9,8},{10,11... | collective-permute-start | bytes 6291464 | tf_op jit(solution)/shard_map/ppermute | solution.py:43
  292.3 26.8 %collective-permute-start.20 = (bf16[2,64,2048]{2,1,0:T(8,128)(2,1)S(1)}, bf16[2,64,2048]{2,1,0:T(8,128)(2,1)S(1)}, u32[]{:S(2)}, u32[]{:S(2)}) collective-permute-start(bf16[2,64,2048]{2,1,0:T(8,128)(2,1)S(1)} %copy-done.23), channel_id=1, source_target_pairs={{0,2},{2,4},{4,6},{6,0},{1,3},{3,5},{5,7},{7,1},{8,10},{10,12},{12... | collective-permute-start | bytes 1572872 | tf_op jit(solution)/shard_map/ppermute | solution.py:62
  294.3 24.7 %collective-permute-start.22 = (bf16[2,64,2048]{2,1,0:T(8,128)(2,1)}, bf16[2,64,2048]{2,1,0:T(8,128)(2,1)S(1)}, u32[]{:S(2)}, u32[]{:S(2)}) collective-permute-start(bf16[2,64,2048]{2,1,0:T(8,128)(2,1)} %get-tuple-element.73), channel_id=1, source_target_pairs={{0,6},{2,0},{4,2},{6,4},{1,7},{3,1},{5,3},{7,5},{8,14},{10,8},{12,... | collective-permute-start | bytes 1572872 | tf_op jit(solution)/shard_map/ppermute | solution.py:62
  324.6 24.8 %collective-permute-start.23 = (bf16[2,64,2048]{2,1,0:T(8,128)(2,1)S(1)}, bf16[2,64,2048]{2,1,0:T(8,128)(2,1)}, u32[]{:S(2)}, u32[]{:S(2)}) collective-permute-start(bf16[2,64,2048]{2,1,0:T(8,128)(2,1)S(1)} %fusion.38), channel_id=1, source_target_pairs={{2,0},{4,2},{6,4},{0,6},{3,1},{5,3},{7,5},{1,7},{10,8},{12,10},{14... | collective-permute-start | bytes 1572872 | tf_op jit(solution)/shard_map/ppermute | solution.py:49
  352.9 39.8 %all-to-all-start = ((bf16[4,2,64,2048]{3,2,1,0:T(8,128)(2,1)}), bf16[4,2,64,2048]{3,2,1,0:T(8,128)(2,1)S(1)}, u32[]{:S(2)}, u32[]{:S(2)}) async-start(bf16[4,2,64,2048]{3,2,1,0:T(8,128)(2,1)} %add_cores_placed.2.refs_0_.token_ref), calls=%async_computation | async-start | bytes 4194304 | tf_op jit(solution)/shard_map/all_to_all | solution.py:481
  356.8 126.6 %all-gather.11.cloned.1.call-start = ((), (), s32[]{:S(2)}) async-start(), calls=%async_computation.5 | async-start | bytes 10616832 | tf_op jit(solution)/shard_map/all_gather | solution.py:1029
  390.1 18.9 %collective-permute-start.27 = (bf16[4,2,64,2048]{3,2,1,0:T(8,128)(2,1)}, bf16[4,2,64,2048]{3,2,1,0:T(8,128)(2,1)}, u32[]{:S(2)}, u32[]{:S(2)}) collective-permute-start(bf16[4,2,64,2048]{3,2,1,0:T(8,128)(2,1)} %bitcast.213), channel_id=1, source_target_pairs={{0,1},{1,0},{2,3},{3,2},{4,5},{5,4},{6,7},{7,6},{8,9},{9,8},{10,11... | collective-permute-start | bytes 6291464 | tf_op jit(solution)/shard_map/ppermute | solution.py:43
  413.8 59.6 %all-to-all-start.1 = ((bf16[4,2,64,2048]{3,2,1,0:T(8,128)(2,1)}), bf16[4,2,64,2048]{3,2,1,0:T(8,128)(2,1)}, u32[]{:S(2)}, u32[]{:S(2)}) async-start(bf16[4,2,64,2048]{3,2,1,0:T(8,128)(2,1)} %add_cores_placed.3.refs_0_), calls=%async_computation.1 | async-start | bytes 4194304 | tf_op jit(solution)/shard_map/all_to_all | solution.py:481
  419.4 33.7 %collective-permute-start.29 = (bf16[4,80,1280]{2,1,0:T(8,128)(2,1)}, bf16[4,80,1280]{2,1,0:T(8,128)(2,1)S(1)}, u32[]{:S(2)}, u32[]{:S(2)}) collective-permute-start(bf16[4,80,1280]{2,1,0:T(8,128)(2,1)} %get-tuple-element.87), channel_id=1, source_target_pairs={{64,0},{72,8},{80,16},{88,24},{96,32},{104,40},{112,48},{120,56},{... | collective-permute-start | bytes 2457608 | tf_op jit(solution)/shard_map/ppermute | solution.py:91
  421.1 35.8 %collective-permute-start.30 = (bf16[4,80,1280]{2,1,0:T(8,128)(2,1)}, bf16[4,80,1280]{2,1,0:T(8,128)(2,1)S(1)}, u32[]{:S(2)}, u32[]{:S(2)}) collective-permute-start(bf16[4,80,1280]{2,1,0:T(8,128)(2,1)} %get-tuple-element.88), channel_id=1, source_target_pairs={{32,0},{40,8},{48,16},{56,24},{64,32},{72,40},{80,48},{88,56},{96,... | collective-permute-start | bytes 2457608 | tf_op jit(solution)/shard_map/ppermute | solution.py:91
  421.9 36.9 %collective-permute-start.28 = (bf16[4,80,1280]{2,1,0:T(8,128)(2,1)S(1)}, bf16[4,80,1280]{2,1,0:T(8,128)(2,1)S(1)}, u32[]{:S(2)}, u32[]{:S(2)}) collective-permute-start(bf16[4,80,1280]{2,1,0:T(8,128)(2,1)S(1)} %copy-done.16), channel_id=1, source_target_pairs={{96,0},{104,8},{112,16},{120,24},{0,32},{8,40},{16,48},{24,56},{32... | collective-permute-start | bytes 2457608 | tf_op jit(solution)/shard_map/ppermute | solution.py:91
  422.5 27.8 %collective-permute-start.32 = (bf16[4,64,1280]{2,1,0:T(8,128)(2,1)}, bf16[4,64,1280]{2,1,0:T(8,128)(2,1)S(1)}, u32[]{:S(2)}, u32[]{:S(2)}) collective-permute-start(bf16[4,64,1280]{2,1,0:T(8,128)(2,1)} %get-tuple-element.91), channel_id=1, source_target_pairs={{16,0},{24,8},{0,16},{8,24},{48,32},{56,40},{32,48},{40,56},{80,64... | collective-permute-start | bytes 1966088 | tf_op jit(solution)/shard_map/ppermute | solution.py:91
  466.1 28.9 %collective-permute-start.38 = (bf16[64,1280]{1,0:T(8,128)(2,1)}, bf16[64,1280]{1,0:T(8,128)(2,1)}, u32[]{:S(2)}, u32[]{:S(2)}) collective-permute-start(bf16[64,1280]{1,0:T(8,128)(2,1)} %get-tuple-element.99), channel_id=1, source_target_pairs={{64,0},{72,8},{80,16},{88,24},{96,32},{104,40},{112,48},{120,56},{... | collective-permute-start | bytes 491528 | tf_op jit(solution)/shard_map/ppermute | solution.py:91
  468.4 26.6 %collective-permute-start.39 = (bf16[64,1280]{1,0:T(8,128)(2,1)}, bf16[64,1280]{1,0:T(8,128)(2,1)}, u32[]{:S(2)}, u32[]{:S(2)}) collective-permute-start(bf16[64,1280]{1,0:T(8,128)(2,1)} %get-tuple-element.100), channel_id=1, source_target_pairs={{32,0},{40,8},{48,16},{56,24},{64,32},{72,40},{80,48},{88,56},{96,... | collective-permute-start | bytes 491528 | tf_op jit(solution)/shard_map/ppermute | solution.py:91
  469.4 25.5 %collective-permute-start.34 = (bf16[80,1280]{1,0:T(8,128)(2,1)}, bf16[80,1280]{1,0:T(8,128)(2,1)S(1)}, u32[]{:S(2)}, u32[]{:S(2)}) collective-permute-start(bf16[80,1280]{1,0:T(8,128)(2,1)} %get-tuple-element.94), channel_id=1, source_target_pairs={{24,0},{0,8},{8,16},{16,24},{56,32},{32,40},{40,48},{48,56},{88,64... | collective-permute-start | bytes 614408 | tf_op jit(solution)/shard_map/ppermute | solution.py:91
  470.3 24.6 %collective-permute-start.35 = (bf16[80,1280]{1,0:T(8,128)(2,1)}, bf16[80,1280]{1,0:T(8,128)(2,1)S(1)}, u32[]{:S(2)}, u32[]{:S(2)}) collective-permute-start(bf16[80,1280]{1,0:T(8,128)(2,1)} %get-tuple-element.95), channel_id=1, source_target_pairs={{16,0},{24,8},{0,16},{8,24},{48,32},{56,40},{32,48},{40,56},{80,64... | collective-permute-start | bytes 614408 | tf_op jit(solution)/shard_map/ppermute | solution.py:91
  500.8 22.2 %collective-permute-start.41 = (bf16[144,768]{1,0:T(8,128)(2,1)}, bf16[144,768]{1,0:T(8,128)(2,1)}, u32[]{:S(2)}, u32[]{:S(2)}) collective-permute-start(bf16[144,768]{1,0:T(8,128)(2,1)} %get-tuple-element.193), channel_id=1, source_target_pairs={{4,0},{6,2},{0,4},{2,6},{5,1},{7,3},{1,5},{3,7},{12,8},{14,10},{8,... | collective-permute-start | bytes 663560 | tf_op jit(solution)/shard_map/ppermute | solution.py:82
  502.2 22.3 %collective-permute-start.40 = (bf16[144,768]{1,0:T(8,128)(2,1)}, bf16[144,768]{1,0:T(8,128)(2,1)}, u32[]{:S(2)}, u32[]{:S(2)}) collective-permute-start(bf16[144,768]{1,0:T(8,128)(2,1)} %get-tuple-element.193), channel_id=1, source_target_pairs={{2,0},{4,2},{6,4},{0,6},{3,1},{5,3},{7,5},{1,7},{10,8},{12,10},{14... | collective-permute-start | bytes 663560 | tf_op jit(solution)/shard_map/ppermute | solution.py:82
  503.5 21.0 %collective-permute-start.42 = (bf16[144,768]{1,0:T(8,128)(2,1)}, bf16[144,768]{1,0:T(8,128)(2,1)}, u32[]{:S(2)}, u32[]{:S(2)}) collective-permute-start(bf16[144,768]{1,0:T(8,128)(2,1)} %get-tuple-element.193), channel_id=1, source_target_pairs={{6,0},{0,2},{2,4},{4,6},{7,1},{1,3},{3,5},{5,7},{14,8},{8,10},{10,... | collective-permute-start | bytes 663560 | tf_op jit(solution)/shard_map/ppermute | solution.py:82
  (58 other events, 576.5 us)
Sparse Core Ops, SparseCore 0:
  20.3 65.2 all-gather.6
  87.8 121.7 all-gather.8
  291.4 120.2 reduce-scatter.3
  413.9 69.4 all-gather.10

commit v4 on v2

--- a/solution.py
+++ b/solution.py
@@ -944,7 +944,7 @@
     grad_gain_moe = jnp.sum(d_h2 * x1 * inverse_mid, axis=(0, 1))
     d_x1 = dy_own.astype(F32) + norm_back(d_h2, x1, inverse_mid, gain_moe)
     grad_experts = lax.psum_scatter(
-        grad_experts, "experts", scatter_dimension=0, tiled=False
+        after_call(grad_experts, pieces[1]), "experts", scatter_dimension=0, tiled=False
     )
     moe_pieces = add_placed_call(
         where, swap(moe_theirs.reshape(shape)), moe_mine.reshape(shape), hidden
@@ -1021,15 +1021,16 @@
     firsts, seconds = attend_grads_call(
         place, h1, d_qkv, grad_out, grad_gains, output, depth // 2 + 16
     )
-    d_h1 = exchange_sum(add_placed_call(where, swap(theirs[0]), mine[0], firsts[1]))
+    h1_pieces = add_placed_call(where, swap(theirs[0]), mine[0], firsts[1])
+    d_h1 = exchange_sum(h1_pieces)
     x_f32 = x_own.astype(F32)
     input_grad = (d_x1 + norm_back(d_h1, x_f32, inverse_rms(x_f32), gain_attn))[:, None]
-    grad_experts = after_call(grad_experts, firsts[1])
+    grad_experts = after_call(grad_experts, h1_pieces)
     all_experts = lax.all_gather(grad_experts, GROUP, axis=0, tiled=False)
     firsts, seconds = plane_send(firsts, 1, 0), plane_send(seconds, 0, 1)
     firsts, seconds = half_sum_call(place, firsts, seconds, grad_out)
+    result_gate, result_up, result_down = gate_up_down_call(all_experts, ff_part)
     grads = last_sum_call(plane_send(firsts, 0, 1), plane_send(seconds, 1, 0), d_h1)
-    result_gate, result_up, result_down = gate_up_down_call(all_experts, ff_part)
     out_sum = jnp.concatenate(
         [grads[k * out_part : (k + 1) * out_part, qkv_width:] for k in range(depth // out_part)],
         axis=1,
@@ -1037,7 +1038,7 @@
     result_q, result_k, result_v, gain_sum = columns_call(
         where, *gather_members(grads[:, :qkv_width]), depth, q_width, head
     )
-    out_sum = after_call(lax.ppermute(out_sum, EVERY, back), result_down)
+    out_sum = after_call(lax.ppermute(out_sum, EVERY, back), input_grad, result_down)
     result_out = rows_call(where, *gather_members(out_sum))
     gain_sum = gain_sum[0]
     return (

time: 588 us -> 559 us (0.951)
  starting transfers between devices: 99.6 us -> 74.9 us
    ppermute x11, starting transfers between devices: 33.1 us -> 15.9 us  [swap(): return lax.ppermute(v, 'dp', [(0, 1), (1, 0)])]
    ppermute x11, waiting for transfers between devices: 16.6 us -> 8.68 us  [swap(): return lax.ppermute(v, 'dp', [(0, 1), (1, 0)])]
    ppermute x12, starting transfers between devices: 21.9 us -> 14.2 us  [plane(): return lax.ppermute(v, 'experts', moves)]
  transfers between devices with their start and end apart: 55 -> 55, of which waited for: 34 -> 33; matrix products, arithmetic and copies ran while one was open for 11% -> 12% of each run, Pallas kernels for 20% -> 25%
where the time goes in v4:
time: 559 us; the launch traced here: 549 us
  Pallas kernels  195 us (35%)
  waiting for transfers between devices  193 us (35%)
  starting transfers between devices  74.9 us (13%)
  other arithmetic  48.5 us (9%)
  local copies, waits for them, and re-layouts  22.7 us (4%)
  between operations  14.7 us (3%)
    ppermute x12, waiting for transfers between devices, ring_stack(): lax.ppermute(own, 'context', [((i + k) % ring, i) for i in range(ring)])  78.6 us
    pallas_call x1, Pallas kernels, experts_call(): pl.pallas_call(functools.partial(experts_kernel, part), grid=(n, blocks),...  48.9 us
    pallas_call x2, Pallas kernels, attend_call(): pl.pallas_call(kernel, grid=(2 * micro,), in_specs=in_specs, out_specs=ou...  48.6 us
    ppermute x12, waiting for transfers between devices, plane(): return lax.ppermute(v, 'experts', moves)  39.1 us
    ppermute x6, waiting for transfers between devices, ring_sum(): lax.ppermute(pieces[k], 'context', [(i, (i + k) % ring) for i in range(ri...  32.1 us
    pallas_call x1, Pallas kernels, expert_grads_call(): pl.pallas_call(functools.partial(expert_grads_kernel, part), grid=(n,), i...  27 us
    another operation x6, other arithmetic, gather_rows(): return jnp.stack([mine, swap(mine)])  17.9 us
    ppermute x11, starting transfers between devices, swap(): return lax.ppermute(v, 'dp', [(0, 1), (1, 0)])  15.9 us
  transfers between devices with their start and end apart: 55, of which 33 were waited for; matrix products, arithmetic and copies ran while one was open for 12% of the time, Pallas kernels for 25%

profile of v4, /device:TPU:49, one launch (start us, length us, event | category | flops | bytes accessed | tf_op | source)
XLA Modules:
  0.0 548.8 jit_solution(17703323537418703710)
XLA Ops:
  8.3 4.7 collective-permute-start.4
  15.5 6.9 %collective-permute-done.4 = bf16[32,2048]{1,0:T(8,128)(2,1)S(1)} collective-permute-done((bf16[32,2048]{1,0:T(8,128)(2,1)S(1)}, bf16[32,2048]{1,0:T(8,128)(2,1)S(1)}, u32[]{:S(2)}, u32[]{:S(2)}) %collective-permute-start.4) | collective-permute-done | bytes 131104 | tf_op jit(solution)/shard_map/ppermute | solution.py:843
  38.7 8.3 %collective-permute-done.1 = bf16[2,64,2048]{2,1,0:T(8,128)(2,1)S(1)} collective-permute-done((bf16[2,64,2048]{2,1,0:T(8,128)(2,1)S(1)}, bf16[2,64,2048]{2,1,0:T(8,128)(2,1)S(1)}, u32[]{:S(2)}, u32[]{:S(2)}) %collective-permute-start.1) | collective-permute-done | bytes 524320 | tf_op jit(solution)/shard_map/ppermute | solution.py:49
  47.6 10.3 %collective-permute-done = bf16[2,64,2048]{2,1,0:T(8,128)(2,1)S(1)} collective-permute-done((bf16[2,64,2048]{2,1,0:T(8,128)(2,1)S(1)}, bf16[2,64,2048]{2,1,0:T(8,128)(2,1)S(1)}, u32[]{:S(2)}, u32[]{:S(2)}) %collective-permute-start) | collective-permute-done | bytes 524320 | tf_op jit(solution)/shard_map/ppermute | solution.py:49
  62.6 8.3 %collective-permute-done.8 = bf16[2,64,2176]{2,1,0:T(8,128)(2,1)S(1)} collective-permute-done((bf16[2,64,2176]{2,1,0:T(8,128)(2,1)S(1)}, bf16[2,64,2176]{2,1,0:T(8,128)(2,1)S(1)}, u32[]{:S(2)}, u32[]{:S(2)}) %collective-permute-start.8) | collective-permute-done | bytes 557088 | tf_op jit(solution)/shard_map/ppermute | solution.py:49
  70.9 11.3 %collective-permute-done.7 = bf16[2,64,2176]{2,1,0:T(8,128)(2,1)S(1)} collective-permute-done((bf16[2,64,2176]{2,1,0:T(8,128)(2,1)S(1)}, bf16[2,64,2176]{2,1,0:T(8,128)(2,1)S(1)}, u32[]{:S(2)}, u32[]{:S(2)}) %collective-permute-start.7) | collective-permute-done | bytes 557088 | tf_op jit(solution)/shard_map/ppermute | solution.py:49
  90.9 4.6 pad_maximum_fusion.1.x_ref
  102.8 22.0 %attention.1 = (bf16[2,4,2,64,2048]{4,3,2,1,0:T(8,128)(2,1)}, f32[2,4,2,64,768]{4,3,2,1,0:T(8,128)}, bf16[2,4,2,64,512]{4,3,2,1,0:T(8,128)(2,1)}, bf16[1,4,2,64,...) custom-call(bf16[2,4,2,64,2048]{4,3,2,1,0:T(8,128)(2,1)} %pad_maximum_fusion.1.x_ref, f32[1,2048]{1,0:T(1,128)} %bitcast.205, ...), custom_call_target="tpu_custom_call" | custom-call | bytes 1000 | tf_op jit(solution)/shard_map/attention/pallas_call | solution.py:326
  136.3 9.5 %collective-permute-done.11 = bf16[2,64,2048]{2,1,0:T(8,128)(2,1)S(1)} collective-permute-done((bf16[2,64,2048]{2,1,0:T(8,128)(2,1)S(1)}, bf16[2,64,2048]{2,1,0:T(8,128)(2,1)S(1)}, u32[]{:S(2)}, u32[]{:S(2)}) %collective-permute-start.11) | collective-permute-done | bytes 524320 | tf_op jit(solution)/shard_map/ppermute | solution.py:62
  147.1 10.0 %collective-permute-done.12 = bf16[2,64,2048]{2,1,0:T(8,128)(2,1)S(1)} collective-permute-done((bf16[2,64,2048]{2,1,0:T(8,128)(2,1)S(1)}, bf16[2,64,2048]{2,1,0:T(8,128)(2,1)S(1)}, u32[]{:S(2)}, u32[]{:S(2)}) %collective-permute-start.12) | collective-permute-done | bytes 524320 | tf_op jit(solution)/shard_map/ppermute | solution.py:62
  163.5 9.8 %collective-permute-done.15 = bf16[2,64,2048]{2,1,0:T(8,128)(2,1)S(1)} collective-permute-done((bf16[2,64,2048]{2,1,0:T(8,128)(2,1)S(1)}, bf16[2,64,2048]{2,1,0:T(8,128)(2,1)S(1)}, u32[]{:S(2)}, u32[]{:S(2)}) %collective-permute-start.15) | collective-permute-done | bytes 524320 | tf_op jit(solution)/shard_map/ppermute | solution.py:49
  173.3 12.4 %collective-permute-done.14 = bf16[2,64,2048]{2,1,0:T(8,128)(2,1)S(1)} collective-permute-done((bf16[2,64,2048]{2,1,0:T(8,128)(2,1)S(1)}, bf16[2,64,2048]{2,1,0:T(8,128)(2,1)S(1)}, u32[]{:S(2)}, u32[]{:S(2)}) %collective-permute-start.14) | collective-permute-done | bytes 524320 | tf_op jit(solution)/shard_map/ppermute | solution.py:49
  193.8 15.0 %all-gather.9.cloned.1.call-done = bf16[4608,2048]{1,0:T(8,128)(2,1)} async-done(((bf16[288,2048]{1,0:T(8,128)(2,1)}), bf16[4608,2048]{1,0:T(8,128)(2,1)}) %all-gather.9.cloned.1.call-update) | async-done | bytes 18874384 | tf_op jit(solution)/shard_map/all_gather | solution.py:869
  208.8 48.9 %experts_rows.1 = (bf16[1024,1536]{1,0:T(8,128)(2,1)}, bf16[1024,1536]{1,0:T(8,128)(2,1)}, bf16[1024,1536]{1,0:T(8,128)(2,1)}, bf16[512,2048]{1,0:T(8,128)(2,1)}, bf16[512,2048]{1,0:T(8,128)(2,1)}) custom-call(bf16[1024,2048]{1,0:T(8,128)(2,1)} %bitcast.156, bf16[1024,2176]{1,0:T(8,128)(2,1)} %bitcast.154, bf16[16,288,2048]{2,1,0:T(8,128)(2,1)} %bitcast.163, ...), custom_call_target="tpu_custom_call" | custom-call | bytes 1000 | tf_op jit(solution)/shard_map/experts_rows/pallas_call | solution.py:388
  258.6 27.0 %experts_weights.1 = (bf16[16,288,2048]{2,1,0:T(8,128)(2,1)}, f32[8,128]{1,0:T(8,128)}) custom-call(bf16[1024,1536]{1,0:T(8,128)(2,1)} %get-tuple-element.63.dg_ref, bf16[1024,1536]{1,0:T(8,128)(2,1)} %get-tuple-element.64.du_ref, bf16[1024,1536]{1,0:T(8,128)(2,1)} %get-tuple-element.62.hid_ref.token_ref, bf16[1024,2048]{1,0:T(8,128)(2,1)} %bitcast.157, ...), custom_call_target="tpu_custom_call" | custom-call | bytes 1000 | tf_op jit(solution)/shard_map/experts_weights/pallas_call | solution.py:431
  294.0 12.1 %experts_out.1 = (bf16[512,2048]{1,0:T(8,128)(2,1)}, bf16[512,2048]{1,0:T(8,128)(2,1)}) custom-call(bf16[1024,1536]{1,0:T(8,128)(2,1)} %get-tuple-element.62.hid_ref.token_ref, bf16[16,288,2048]{2,1,0:T(8,128)(2,1)} %bitcast.164, f32[8,128]{1,0:T(8,128)} %get-tuple-element.65.token_ref), custom_call_target="tpu_custom_call" | custom-call | flops 6442450944 | bytes 20000000 | tf_op jit(solution)/shard_map/experts_out/pallas_call | solution.py:777
  306.9 9.6 %collective-permute-done.21 = bf16[2,64,2048]{2,1,0:T(8,128)(2,1)S(1)} collective-permute-done((bf16[2,64,2048]{2,1,0:T(8,128)(2,1)}, bf16[2,64,2048]{2,1,0:T(8,128)(2,1)S(1)}, u32[]{:S(2)}, u32[]{:S(2)}) %collective-permute-start.21) | collective-permute-done | bytes 524320 | tf_op jit(solution)/shard_map/ppermute | solution.py:62
  324.8 4.8 add_cores_placed.2.refs_0_.token_ref
  329.5 4.5 collective-permute-done.25
  334.0 11.4 %collective-permute-done.24 = bf16[2,64,2048]{2,1,0:T(8,128)(2,1)S(1)} collective-permute-done((bf16[2,64,2048]{2,1,0:T(8,128)(2,1)S(1)}, bf16[2,64,2048]{2,1,0:T(8,128)(2,1)S(1)}, u32[]{:S(2)}, u32[]{:S(2)}) %collective-permute-start.24) | collective-permute-done | bytes 524320 | tf_op jit(solution)/shard_map/ppermute | solution.py:49
  351.7 4.5 all-to-all-start
  356.4 6.4 %out_weights.1 = bf16[512,2048]{1,0:T(8,128)(2,1)} custom-call(bf16[2,512,512]{2,1,0:T(8,128)(2,1)} %bitcast.185, bf16[512,2048]{1,0:T(8,128)(2,1)} %bitcast.158, bf16[512,2048]{1,0:T(8,128)(2,1)} %bitcast.60.theirs_ref), custom_call_target="tpu_custom_call" | custom-call | bytes 1000 | tf_op jit(solution)/shard_map/out_weights/pallas_call | solution.py:550
  362.7 26.6 %attention_back.1 = (bf16[2,4,2,64,768]{4,3,2,1,0:T(8,128)(2,1)}, bf16[1,4,2,64,2048]{4,3,2,1,0:T(8,128)(2,1)}, bf16[1,4,2,64,2048]{4,3,2,1,0:T(8,128)(2,1)}, f3...) custom-call(bf16[1,4,2,64,2048]{4,3,2,1,0:T(8,128)(2,1)} %bitcast.56.theirs_da_ref, ...), custom_call_target="tpu_custom_call" | custom-call | flops 8999999488 | bytes 90000000 | tf_op jit(solution)/shard_map/attention_back/pallas_call | solution.py:326
  397.9 10.2 %attention_weights.1 = (bf16[4,80,1280]{2,1,0:T(8,128)(2,1)}, bf16[4,80,1280]{2,1,0:T(8,128)(2,1)}, bf16[4,80,1280]{2,1,0:T(8,128)(2,1)}, bf16[4,80,1280]{2,1,0:...) custom-call(s32[2]{0:T(128)} %pad_add_fusion.2.place_ref, ...), custom_call_target="tpu_custom_call" | custom-call | bytes 1000 | tf_op jit(solution)/shard_map/attention_weights/pallas_call | solution.py:595
  408.1 4.8 add_cores_placed.3.refs_0_
  423.5 9.2 %collective-permute-done.31.refs_5_ = bf16[4,64,1280]{2,1,0:T(8,128)(2,1)S(1)} collective-permute-done((bf16[4,64,1280]{2,1,0:T(8,128)(2,1)}, bf16[4,64,1280]{2,1,0:T(8,128)(2,1)S(1)}, u32[]{:S(2)}, u32[]{:S(2)}) %collective-permute-start.31) | collective-permute-done | bytes 655392 | tf_op jit(solution)/shard_map/ppermute | solution.py:91
  437.4 15.4 %collective-permute-done.33.refs_7_ = bf16[4,64,1280]{2,1,0:T(8,128)(2,1)S(1)} collective-permute-done((bf16[4,64,1280]{2,1,0:T(8,128)(2,1)}, bf16[4,64,1280]{2,1,0:T(8,128)(2,1)S(1)}, u32[]{:S(2)}, u32[]{:S(2)}) %collective-permute-start.33) | collective-permute-done | bytes 655392 | tf_op jit(solution)/shard_map/ppermute | solution.py:91
  458.0 5.5 %half_sum.1 = (bf16[80,1280]{1,0:T(8,128)(2,1)}, bf16[80,1280]{1,0:T(8,128)(2,1)}, bf16[80,1280]{1,0:T(8,128)(2,1)}, bf16[80,1280]{1,0:T(8,128)(2,1)}, bf16[64,1...) custom-call(s32[2]{0:T(128)} %pad_add_fusion.2.place_ref, ...), custom_call_target="tpu_custom_call" | custom-call | bytes 1000 | tf_op jit(solution)/shard_map/half_sum/pallas_call | solution.py:638
  481.4 5.2 collective-permute-start.41
  496.9 7.6 %collective-permute-start.43 = (bf16[4,144,768]{2,1,0:T(8,128)(2,1)}, bf16[4,144,768]{2,1,0:T(8,128)(2,1)}, u32[]{:S(2)}, u32[]{:S(2)}) collective-permute-start(bf16[4,144,768]{2,1,0:T(8,128)(2,1)} %pad_maximum_fusion.8.mine_ref), channel_id=1, source_target_pairs={{0,1},{1,0},{2,3},{3,2},{4,5},{5,4},{6,7},{7,6},{8,9},{9,8},{10,11... | collective-permute-start | bytes 2654216 | tf_op jit(solution)/shard_map/ppermute | solution.py:43
  506.1 11.5 %experts_results.1 = (f32[2048,768]{1,0:T(8,128)}, f32[2048,768]{1,0:T(8,128)}, f32[768,2048]{1,0:T(8,128)}) custom-call(bf16[8,288,2048]{2,1,0:T(8,128)(2,1)} %bitcast.165), custom_call_target="tpu_custom_call" | custom-call | bytes 1000 | tf_op jit(solution)/shard_map/experts_results/pallas_call | solution.py:520
  530.3 4.7 columns_results.1
  (240 shorter events, 171.2 us)
Async XLA Ops:
  7.2 92.7 %all-gather.7.cloned.1.call-start = ((), (), s32[]{:S(2)}) async-start(), calls=%async_computation.3 | async-start | bytes 6266880 | tf_op jit(solution)/shard_map/all_gather | solution.py:866
  23.3 185.6 %all-gather.9.cloned.1.call-start = ((), (), s32[]{:S(2)}) async-start(), calls=%async_computation.4 | async-start | bytes 20054016 | tf_op jit(solution)/shard_map/all_gather | solution.py:869
  31.9 381.0 %reduce-scatter.4.cloned.1.call-start = ((), (), s32[]{:S(2)}) async-start(), calls=%async_computation.6 | async-start | bytes 20054016
  31.9 15.1 %collective-permute-start.1 = (bf16[2,64,2048]{2,1,0:T(8,128)(2,1)S(1)}, bf16[2,64,2048]{2,1,0:T(8,128)(2,1)S(1)}, u32[]{:S(2)}, u32[]{:S(2)}) collective-permute-start(bf16[2,64,2048]{2,1,0:T(8,128)(2,1)S(1)} %bitcast.166), channel_id=1, source_target_pairs={{4,0},{6,2},{0,4},{2,6},{5,1},{7,3},{1,5},{3,7},{12,8},{14,10},{8,... | collective-permute-start | bytes 1572872 | tf_op jit(solution)/shard_map/ppermute | solution.py:49
  32.0 25.9 %collective-permute-start = (bf16[2,64,2048]{2,1,0:T(8,128)(2,1)S(1)}, bf16[2,64,2048]{2,1,0:T(8,128)(2,1)S(1)}, u32[]{:S(2)}, u32[]{:S(2)}) collective-permute-start(bf16[2,64,2048]{2,1,0:T(8,128)(2,1)S(1)} %bitcast.167), channel_id=1, source_target_pairs={{2,0},{4,2},{6,4},{0,6},{3,1},{5,3},{7,5},{1,7},{10,8},{12,10},{14... | collective-permute-start | bytes 1572872 | tf_op jit(solution)/shard_map/ppermute | solution.py:49
  35.2 23.5 %collective-permute-start.2 = (bf16[2,64,2048]{2,1,0:T(8,128)(2,1)S(1)}, bf16[2,64,2048]{2,1,0:T(8,128)(2,1)}, u32[]{:S(2)}, u32[]{:S(2)}) collective-permute-start(bf16[2,64,2048]{2,1,0:T(8,128)(2,1)S(1)} %bitcast.168), channel_id=1, source_target_pairs={{6,0},{0,2},{2,4},{4,6},{7,1},{1,3},{3,5},{5,7},{14,8},{8,10},{10,... | collective-permute-start | bytes 1572872 | tf_op jit(solution)/shard_map/ppermute | solution.py:49
  36.0 34.9 %collective-permute-start.8 = (bf16[2,64,2176]{2,1,0:T(8,128)(2,1)S(1)}, bf16[2,64,2176]{2,1,0:T(8,128)(2,1)S(1)}, u32[]{:S(2)}, u32[]{:S(2)}) collective-permute-start(bf16[2,64,2176]{2,1,0:T(8,128)(2,1)S(1)} %concatenate.52), channel_id=1, source_target_pairs={{6,0},{0,2},{2,4},{4,6},{7,1},{1,3},{3,5},{5,7},{14,8},{8,10},{10,... | collective-permute-start | bytes 1671176 | tf_op jit(solution)/shard_map/ppermute | solution.py:49
  37.7 44.6 %collective-permute-start.7 = (bf16[2,64,2176]{2,1,0:T(8,128)(2,1)S(1)}, bf16[2,64,2176]{2,1,0:T(8,128)(2,1)S(1)}, u32[]{:S(2)}, u32[]{:S(2)}) collective-permute-start(bf16[2,64,2176]{2,1,0:T(8,128)(2,1)S(1)} %concatenate.52), channel_id=1, source_target_pairs={{4,0},{6,2},{0,4},{2,6},{5,1},{7,3},{1,5},{3,7},{12,8},{14,10},{8,... | collective-permute-start | bytes 1671176 | tf_op jit(solution)/shard_map/ppermute | solution.py:49
  47.1 35.2 %collective-permute-start.6 = (bf16[2,64,2176]{2,1,0:T(8,128)(2,1)S(1)}, bf16[2,64,2176]{2,1,0:T(8,128)(2,1)S(1)}, u32[]{:S(2)}, u32[]{:S(2)}) collective-permute-start(bf16[2,64,2176]{2,1,0:T(8,128)(2,1)S(1)} %concatenate.52), channel_id=1, source_target_pairs={{2,0},{4,2},{6,4},{0,6},{3,1},{5,3},{7,5},{1,7},{10,8},{12,10},{14... | collective-permute-start | bytes 1671176 | tf_op jit(solution)/shard_map/ppermute | solution.py:49
  62.1 28.8 %collective-permute-start.3 = (bf16[4,2,64,2048]{3,2,1,0:T(8,128)(2,1)}, bf16[4,2,64,2048]{3,2,1,0:T(8,128)(2,1)}, u32[]{:S(2)}, u32[]{:S(2)}) collective-permute-start(bf16[4,2,64,2048]{3,2,1,0:T(8,128)(2,1)} %get-tuple-element.187), channel_id=1, source_target_pairs={{0,1},{1,0},{2,3},{3,2},{4,5},{5,4},{6,7},{7,6},{8,9},{9,8},{10,11... | collective-permute-start | bytes 6291464 | tf_op jit(solution)/shard_map/ppermute | solution.py:43
  133.9 23.1 %collective-permute-start.12 = (bf16[2,64,2048]{2,1,0:T(8,128)(2,1)S(1)}, bf16[2,64,2048]{2,1,0:T(8,128)(2,1)S(1)}, u32[]{:S(2)}, u32[]{:S(2)}) collective-permute-start(bf16[2,64,2048]{2,1,0:T(8,128)(2,1)S(1)} %get-tuple-element.181), channel_id=1, source_target_pairs={{0,4},{2,6},{4,0},{6,2},{1,5},{3,7},{5,1},{7,3},{8,12},{10,14},{12... | collective-permute-start | bytes 1572872 | tf_op jit(solution)/shard_map/ppermute | solution.py:62
  161.9 23.8 %collective-permute-start.14 = (bf16[2,64,2048]{2,1,0:T(8,128)(2,1)S(1)}, bf16[2,64,2048]{2,1,0:T(8,128)(2,1)S(1)}, u32[]{:S(2)}, u32[]{:S(2)}) collective-permute-start(bf16[2,64,2048]{2,1,0:T(8,128)(2,1)S(1)} %multiply_convert_fusion), channel_id=1, source_target_pairs={{2,0},{4,2},{6,4},{0,6},{3,1},{5,3},{7,5},{1,7},{10,8},{12,10},{14... | collective-permute-start | bytes 1572872 | tf_op jit(solution)/shard_map/ppermute | solution.py:49
  163.0 22.7 %collective-permute-start.16 = (bf16[2,64,2048]{2,1,0:T(8,128)(2,1)S(1)}, bf16[2,64,2048]{2,1,0:T(8,128)(2,1)S(1)}, u32[]{:S(2)}, u32[]{:S(2)}) collective-permute-start(bf16[2,64,2048]{2,1,0:T(8,128)(2,1)S(1)} %multiply_convert_fusion), channel_id=1, source_target_pairs={{6,0},{0,2},{2,4},{4,6},{7,1},{1,3},{3,5},{5,7},{14,8},{8,10},{10,... | collective-permute-start | bytes 1572872 | tf_op jit(solution)/shard_map/ppermute | solution.py:49
  257.8 27.9 %collective-permute-start.19 = (bf16[4,2,64,2048]{3,2,1,0:T(8,128)(2,1)}, bf16[4,2,64,2048]{3,2,1,0:T(8,128)(2,1)S(1)}, u32[]{:S(2)}, u32[]{:S(2)}) collective-permute-start(bf16[4,2,64,2048]{3,2,1,0:T(8,128)(2,1)} %bitcast.218), channel_id=1, source_target_pairs={{0,1},{1,0},{2,3},{3,2},{4,5},{5,4},{6,7},{7,6},{8,9},{9,8},{10,11... | collective-permute-start | bytes 6291464 | tf_op jit(solution)/shard_map/ppermute | solution.py:43
  291.7 26.6 %collective-permute-start.20 = (bf16[2,64,2048]{2,1,0:T(8,128)(2,1)S(1)}, bf16[2,64,2048]{2,1,0:T(8,128)(2,1)S(1)}, u32[]{:S(2)}, u32[]{:S(2)}) collective-permute-start(bf16[2,64,2048]{2,1,0:T(8,128)(2,1)S(1)} %copy-done.18), channel_id=1, source_target_pairs={{0,2},{2,4},{4,6},{6,0},{1,3},{3,5},{5,7},{7,1},{8,10},{10,12},{12... | collective-permute-start | bytes 1572872 | tf_op jit(solution)/shard_map/ppermute | solution.py:62
  292.6 23.9 %collective-permute-start.21 = (bf16[2,64,2048]{2,1,0:T(8,128)(2,1)}, bf16[2,64,2048]{2,1,0:T(8,128)(2,1)S(1)}, u32[]{:S(2)}, u32[]{:S(2)}) collective-permute-start(bf16[2,64,2048]{2,1,0:T(8,128)(2,1)} %get-tuple-element.72), channel_id=1, source_target_pairs={{0,4},{2,6},{4,0},{6,2},{1,5},{3,7},{5,1},{7,3},{8,12},{10,14},{12... | collective-permute-start | bytes 1572872 | tf_op jit(solution)/shard_map/ppermute | solution.py:62
  293.1 25.1 %collective-permute-start.22 = (bf16[2,64,2048]{2,1,0:T(8,128)(2,1)}, bf16[2,64,2048]{2,1,0:T(8,128)(2,1)S(1)}, u32[]{:S(2)}, u32[]{:S(2)}) collective-permute-start(bf16[2,64,2048]{2,1,0:T(8,128)(2,1)} %get-tuple-element.73), channel_id=1, source_target_pairs={{0,6},{2,0},{4,2},{6,4},{1,7},{3,1},{5,3},{7,5},{8,14},{10,8},{12,... | collective-permute-start | bytes 1572872 | tf_op jit(solution)/shard_map/ppermute | solution.py:62
  306.1 18.7 %collective-permute-start.18 = (bf16[4,2,64,2048]{3,2,1,0:T(8,128)(2,1)}, bf16[4,2,64,2048]{3,2,1,0:T(8,128)(2,1)}, u32[]{:S(2)}, u32[]{:S(2)}) collective-permute-start(bf16[4,2,64,2048]{3,2,1,0:T(8,128)(2,1)} %bitcast.217), channel_id=1, source_target_pairs={{0,1},{1,0},{2,3},{3,2},{4,5},{5,4},{6,7},{7,6},{8,9},{9,8},{10,11... | collective-permute-start | bytes 6291464 | tf_op jit(solution)/shard_map/ppermute | solution.py:43
  322.8 22.6 %collective-permute-start.24 = (bf16[2,64,2048]{2,1,0:T(8,128)(2,1)S(1)}, bf16[2,64,2048]{2,1,0:T(8,128)(2,1)S(1)}, u32[]{:S(2)}, u32[]{:S(2)}) collective-permute-start(bf16[2,64,2048]{2,1,0:T(8,128)(2,1)S(1)} %fusion.38), channel_id=1, source_target_pairs={{4,0},{6,2},{0,4},{2,6},{5,1},{7,3},{1,5},{3,7},{12,8},{14,10},{8,... | collective-permute-start | bytes 1572872 | tf_op jit(solution)/shard_map/ppermute | solution.py:49
  323.1 23.7 %collective-permute-start.23 = (bf16[2,64,2048]{2,1,0:T(8,128)(2,1)S(1)}, bf16[2,64,2048]{2,1,0:T(8,128)(2,1)}, u32[]{:S(2)}, u32[]{:S(2)}) collective-permute-start(bf16[2,64,2048]{2,1,0:T(8,128)(2,1)S(1)} %fusion.38), channel_id=1, source_target_pairs={{2,0},{4,2},{6,4},{0,6},{3,1},{5,3},{7,5},{1,7},{10,8},{12,10},{14... | collective-permute-start | bytes 1572872 | tf_op jit(solution)/shard_map/ppermute | solution.py:49
  351.7 40.1 %all-to-all-start = ((bf16[4,2,64,2048]{3,2,1,0:T(8,128)(2,1)}), bf16[4,2,64,2048]{3,2,1,0:T(8,128)(2,1)S(1)}, u32[]{:S(2)}, u32[]{:S(2)}) async-start(bf16[4,2,64,2048]{3,2,1,0:T(8,128)(2,1)} %add_cores_placed.2.refs_0_.token_ref), calls=%async_computation | async-start | bytes 4194304 | tf_op jit(solution)/shard_map/all_to_all | solution.py:481
  356.1 150.0 %all-gather.11.cloned.1.call-start = ((), (), s32[]{:S(2)}) async-start(), calls=%async_computation.5 | async-start | bytes 10616832 | tf_op jit(solution)/shard_map/all_gather | solution.py:1029
  389.3 18.8 %collective-permute-start.27 = (bf16[4,2,64,2048]{3,2,1,0:T(8,128)(2,1)}, bf16[4,2,64,2048]{3,2,1,0:T(8,128)(2,1)}, u32[]{:S(2)}, u32[]{:S(2)}) collective-permute-start(bf16[4,2,64,2048]{3,2,1,0:T(8,128)(2,1)} %bitcast.216), channel_id=1, source_target_pairs={{0,1},{1,0},{2,3},{3,2},{4,5},{5,4},{6,7},{7,6},{8,9},{9,8},{10,11... | collective-permute-start | bytes 6291464 | tf_op jit(solution)/shard_map/ppermute | solution.py:43
  412.9 59.4 %all-to-all-start.1 = ((bf16[4,2,64,2048]{3,2,1,0:T(8,128)(2,1)}), bf16[4,2,64,2048]{3,2,1,0:T(8,128)(2,1)S(1)}, u32[]{:S(2)}, u32[]{:S(2)}) async-start(bf16[4,2,64,2048]{3,2,1,0:T(8,128)(2,1)} %add_cores_placed.3.refs_0_), calls=%async_computation.1 | async-start | bytes 4194304 | tf_op jit(solution)/shard_map/all_to_all | solution.py:481
  417.1 15.6 %collective-permute-start.31 = (bf16[4,64,1280]{2,1,0:T(8,128)(2,1)}, bf16[4,64,1280]{2,1,0:T(8,128)(2,1)S(1)}, u32[]{:S(2)}, u32[]{:S(2)}) collective-permute-start(bf16[4,64,1280]{2,1,0:T(8,128)(2,1)} %get-tuple-element.88), channel_id=1, source_target_pairs={{24,0},{0,8},{8,16},{16,24},{56,32},{32,40},{40,48},{48,56},{88,64... | collective-permute-start | bytes 1966088 | tf_op jit(solution)/shard_map/ppermute | solution.py:91
  418.4 34.3 %collective-permute-start.29 = (bf16[4,80,1280]{2,1,0:T(8,128)(2,1)}, bf16[4,80,1280]{2,1,0:T(8,128)(2,1)S(1)}, u32[]{:S(2)}, u32[]{:S(2)}) collective-permute-start(bf16[4,80,1280]{2,1,0:T(8,128)(2,1)} %get-tuple-element.85), channel_id=1, source_target_pairs={{64,0},{72,8},{80,16},{88,24},{96,32},{104,40},{112,48},{120,56},{... | collective-permute-start | bytes 2457608 | tf_op jit(solution)/shard_map/ppermute | solution.py:91
  419.7 35.8 %collective-permute-start.30 = (bf16[4,80,1280]{2,1,0:T(8,128)(2,1)}, bf16[4,80,1280]{2,1,0:T(8,128)(2,1)}, u32[]{:S(2)}, u32[]{:S(2)}) collective-permute-start(bf16[4,80,1280]{2,1,0:T(8,128)(2,1)} %get-tuple-element.86), channel_id=1, source_target_pairs={{32,0},{40,8},{48,16},{56,24},{64,32},{72,40},{80,48},{88,56},{96,... | collective-permute-start | bytes 2457608 | tf_op jit(solution)/shard_map/ppermute | solution.py:91
  420.8 37.2 %collective-permute-start.28 = (bf16[4,80,1280]{2,1,0:T(8,128)(2,1)}, bf16[4,80,1280]{2,1,0:T(8,128)(2,1)}, u32[]{:S(2)}, u32[]{:S(2)}) collective-permute-start(bf16[4,80,1280]{2,1,0:T(8,128)(2,1)} %get-tuple-element.83.token_ref), channel_id=1, source_target_pairs={{96,0},{104,8},{112,16},{120,24},{0,32},{8,40},{16,48},{24,56},{32... | collective-permute-start | bytes 2457608 | tf_op jit(solution)/shard_map/ppermute | solution.py:91
  421.2 16.2 %collective-permute-start.32 = (bf16[4,64,1280]{2,1,0:T(8,128)(2,1)}, bf16[4,64,1280]{2,1,0:T(8,128)(2,1)S(1)}, u32[]{:S(2)}, u32[]{:S(2)}) collective-permute-start(bf16[4,64,1280]{2,1,0:T(8,128)(2,1)} %get-tuple-element.89), channel_id=1, source_target_pairs={{16,0},{24,8},{0,16},{8,24},{48,32},{56,40},{32,48},{40,56},{80,64... | collective-permute-start | bytes 1966088 | tf_op jit(solution)/shard_map/ppermute | solution.py:91
  432.8 20.0 %collective-permute-start.33 = (bf16[4,64,1280]{2,1,0:T(8,128)(2,1)}, bf16[4,64,1280]{2,1,0:T(8,128)(2,1)S(1)}, u32[]{:S(2)}, u32[]{:S(2)}) collective-permute-start(bf16[4,64,1280]{2,1,0:T(8,128)(2,1)} %get-tuple-element.90), channel_id=1, source_target_pairs={{8,0},{16,8},{24,16},{0,24},{40,32},{48,40},{56,48},{32,56},{72,64... | collective-permute-start | bytes 1966088 | tf_op jit(solution)/shard_map/ppermute | solution.py:91
  489.0 28.7 %collective-permute-start.44 = (bf16[32,2048]{1,0:T(8,128)(2,1)S(1)}, bf16[32,2048]{1,0:T(8,128)(2,1)S(1)}, u32[]{:S(2)}, u32[]{:S(2)}) collective-permute-start(bf16[32,2048]{1,0:T(8,128)(2,1)S(1)} %pad_maximum_fusion.12), channel_id=1, source_target_pairs={{0,0},{8,1},{16,2},{24,3},{32,4},{40,5},{48,6},{56,7},{64,8},{72,9... | collective-permute-start | bytes 393224 | tf_op jit(solution)/shard_map/ppermute | solution.py:1041
  496.9 33.4 %collective-permute-start.43 = (bf16[4,144,768]{2,1,0:T(8,128)(2,1)}, bf16[4,144,768]{2,1,0:T(8,128)(2,1)}, u32[]{:S(2)}, u32[]{:S(2)}) collective-permute-start(bf16[4,144,768]{2,1,0:T(8,128)(2,1)} %pad_maximum_fusion.8.mine_ref), channel_id=1, source_target_pairs={{0,1},{1,0},{2,3},{3,2},{4,5},{5,4},{6,7},{7,6},{8,9},{9,8},{10,11... | collective-permute-start | bytes 2654216 | tf_op jit(solution)/shard_map/ppermute | solution.py:43
  (51 other events, 473.4 us)
Sparse Core Ops, SparseCore 0:
  23.4 61.4 all-gather.6
  87.0 121.7 all-gather.8
  290.8 120.3 reduce-scatter.3
  413.0 68.6 all-gather.10

commit v5 on v4

--- a/solution.py
+++ b/solution.py
@@ -75,9 +75,9 @@
     return ring_sum(add_cores(theirs, mine))
 
 
-def gather_members(v):
+def gather_members(v, *tokens):
     ring = lax.axis_size("context")
-    pieces = [v]
+    pieces = [after_call(v, *tokens) if tokens else v]
     for k in range(1, ring):
         pieces.append(lax.ppermute(v, "context", [((i + k) % ring, i) for i in range(ring)]))
     mine = jnp.stack(pieces)
@@ -173,7 +173,7 @@
         query = rope(q_pre * inverse_rms(q_pre) * gain_q_ref[...], cosines, sines).astype(BF16)
         logits = against(query, key) * scale + bias
         scaled = jnp.exp(logits - jnp.max(logits, axis=-1, keepdims=True))
-        soft = (scaled / jnp.sum(scaled, axis=-1, keepdims=True)).astype(BF16)
+        soft = (scaled * (1.0 / jnp.sum(scaled, axis=-1, keepdims=True))).astype(BF16)
         heads_out[:, g * size : (g + 1) * size] = matmul(soft, value).astype(BF16)
     out = heads_out[...]
     put(heads_ref, out)
@@ -245,7 +245,7 @@
         query = rope(q_pre * inverse_q * gain_q, cosines, sines).astype(BF16)
         logits = against(query, key) * scale + bias
         scaled = jnp.exp(logits - jnp.max(logits, axis=-1, keepdims=True))
-        probs = scaled / jnp.sum(scaled, axis=-1, keepdims=True)
+        probs = scaled * (1.0 / jnp.sum(scaled, axis=-1, keepdims=True))
         d_head = d_heads[:, g * size : (g + 1) * size]
         d_probs = against(d_head, value)
         d_scores = probs * (d_probs - jnp.sum(probs * d_probs, axis=-1, keepdims=True))
@@ -1021,16 +1021,17 @@
     firsts, seconds = attend_grads_call(
         place, h1, d_qkv, grad_out, grad_gains, output, depth // 2 + 16
     )
-    h1_pieces = add_placed_call(where, swap(theirs[0]), mine[0], firsts[1])
+    h1_theirs = swap(theirs[0])
+    h1_pieces = add_placed_call(where, h1_theirs, mine[0], firsts[1])
     d_h1 = exchange_sum(h1_pieces)
     x_f32 = x_own.astype(F32)
     input_grad = (d_x1 + norm_back(d_h1, x_f32, inverse_rms(x_f32), gain_attn))[:, None]
-    grad_experts = after_call(grad_experts, h1_pieces)
+    grad_experts = after_call(grad_experts, firsts[1], h1_theirs)
     all_experts = lax.all_gather(grad_experts, GROUP, axis=0, tiled=False)
     firsts, seconds = plane_send(firsts, 1, 0), plane_send(seconds, 0, 1)
-    firsts, seconds = half_sum_call(place, firsts, seconds, grad_out)
+    firsts, seconds = half_sum_call(place, firsts, seconds, h1_pieces)
     result_gate, result_up, result_down = gate_up_down_call(all_experts, ff_part)
-    grads = last_sum_call(plane_send(firsts, 0, 1), plane_send(seconds, 1, 0), d_h1)
+    grads = last_sum_call(plane_send(firsts, 0, 1), plane_send(seconds, 1, 0), h1_pieces)
     out_sum = jnp.concatenate(
         [grads[k * out_part : (k + 1) * out_part, qkv_width:] for k in range(depth // out_part)],
         axis=1,
@@ -1039,7 +1040,7 @@
         where, *gather_members(grads[:, :qkv_width]), depth, q_width, head
     )
     out_sum = after_call(lax.ppermute(out_sum, EVERY, back), input_grad, result_down)
-    result_out = rows_call(where, *gather_members(out_sum))
+    result_out = rows_call(where, *gather_members(out_sum, result_q))
     gain_sum = gain_sum[0]
     return (
         output,

time: 559 us -> 559 us (level)
  the two profiles are of different devices: /device:TPU:49 before, /device:TPU:7 now
where the time goes in v5:
time: 559 us; the launch traced here: 549 us
  Pallas kernels  195 us (35%)
  waiting for transfers between devices  194 us (35%)
  starting transfers between devices  70.7 us (13%)
  other arithmetic  51.5 us (9%)
  local copies, waits for them, and re-layouts  22.9 us (4%)
  between operations  14.8 us (3%)
    ppermute x12, waiting for transfers between devices, ring_stack(): lax.ppermute(own, 'context', [((i + k) % ring, i) for i in range(ring)])  80.6 us
    pallas_call x1, Pallas kernels, experts_call(): pl.pallas_call(functools.partial(experts_kernel, part), grid=(n, blocks),...  48.9 us
    pallas_call x2, Pallas kernels, attend_call(): pl.pallas_call(kernel, grid=(2 * micro,), in_specs=in_specs, out_specs=ou...  48.6 us
    ppermute x12, waiting for transfers between devices, plane(): return lax.ppermute(v, 'experts', moves)  32.1 us
    ppermute x6, waiting for transfers between devices, ring_sum(): lax.ppermute(pieces[k], 'context', [(i, (i + k) % ring) for i in range(ri...  32 us
    pallas_call x1, Pallas kernels, expert_grads_call(): pl.pallas_call(functools.partial(expert_grads_kernel, part), grid=(n,), i...  27 us
    another operation x6, other arithmetic, gather_rows(): return jnp.stack([mine, swap(mine)])  18 us
    ppermute x6, waiting for transfers between devices, gather_members(): lax.ppermute(v, 'context', [((i + k) % ring, i) for i in range(ring)])  16.3 us
  transfers between devices with their start and end apart: 55, of which 28 were waited for; matrix products, arithmetic and copies ran while one was open for 12% of the time, Pallas kernels for 25%

profile of v5, /device:TPU:7, one launch (start us, length us, event | category | flops | bytes accessed | tf_op | source)
XLA Modules:
  0.0 549.0 jit_solution(1969166383573797506)
XLA Ops:
  8.3 6.5 %collective-permute-start.4 = (bf16[32,2048]{1,0:T(8,128)(2,1)S(1)}, bf16[32,2048]{1,0:T(8,128)(2,1)S(1)}, u32[]{:S(2)}, u32[]{:S(2)}) collective-permute-start(bf16[32,2048]{1,0:T(8,128)(2,1)S(1)} %constant_dynamic-slice_fusion.2), channel_id=1, source_target_pairs={{0,0},{1,8},{2,16},{3,24},{4,32},{5,40},{6,48},{7,56},{8,64},{9,72... | collective-permute-start | bytes 393224 | tf_op jit(solution)/shard_map/ppermute | solution.py:843
  17.3 7.3 %collective-permute-done.4 = bf16[32,2048]{1,0:T(8,128)(2,1)S(1)} collective-permute-done((bf16[32,2048]{1,0:T(8,128)(2,1)S(1)}, bf16[32,2048]{1,0:T(8,128)(2,1)S(1)}, u32[]{:S(2)}, u32[]{:S(2)}) %collective-permute-start.4) | collective-permute-done | bytes 131104 | tf_op jit(solution)/shard_map/ppermute | solution.py:843
  39.8 9.3 %collective-permute-done.1 = bf16[2,64,2048]{2,1,0:T(8,128)(2,1)S(1)} collective-permute-done((bf16[2,64,2048]{2,1,0:T(8,128)(2,1)S(1)}, bf16[2,64,2048]{2,1,0:T(8,128)(2,1)S(1)}, u32[]{:S(2)}, u32[]{:S(2)}) %collective-permute-start.1) | collective-permute-done | bytes 524320 | tf_op jit(solution)/shard_map/ppermute | solution.py:49
  49.1 6.8 %collective-permute-done = bf16[2,64,2048]{2,1,0:T(8,128)(2,1)S(1)} collective-permute-done((bf16[2,64,2048]{2,1,0:T(8,128)(2,1)S(1)}, bf16[2,64,2048]{2,1,0:T(8,128)(2,1)S(1)}, u32[]{:S(2)}, u32[]{:S(2)}) %collective-permute-start) | collective-permute-done | bytes 524320 | tf_op jit(solution)/shard_map/ppermute | solution.py:49
  55.9 4.8 collective-permute-done.2
  64.8 8.3 %collective-permute-done.8 = bf16[2,64,2176]{2,1,0:T(8,128)(2,1)S(1)} collective-permute-done((bf16[2,64,2176]{2,1,0:T(8,128)(2,1)S(1)}, bf16[2,64,2176]{2,1,0:T(8,128)(2,1)S(1)}, u32[]{:S(2)}, u32[]{:S(2)}) %collective-permute-start.8) | collective-permute-done | bytes 557088 | tf_op jit(solution)/shard_map/ppermute | solution.py:49
  73.0 11.2 %collective-permute-done.7 = bf16[2,64,2176]{2,1,0:T(8,128)(2,1)S(1)} collective-permute-done((bf16[2,64,2176]{2,1,0:T(8,128)(2,1)S(1)}, bf16[2,64,2176]{2,1,0:T(8,128)(2,1)S(1)}, u32[]{:S(2)}, u32[]{:S(2)}) %collective-permute-start.7) | collective-permute-done | bytes 557088 | tf_op jit(solution)/shard_map/ppermute | solution.py:49
  92.9 4.6 pad_maximum_fusion.1.x_ref
  105.0 22.0 %attention.1 = (bf16[2,4,2,64,2048]{4,3,2,1,0:T(8,128)(2,1)}, f32[2,4,2,64,768]{4,3,2,1,0:T(8,128)}, bf16[2,4,2,64,512]{4,3,2,1,0:T(8,128)(2,1)}, bf16[1,4,2,64,...) custom-call(bf16[2,4,2,64,2048]{4,3,2,1,0:T(8,128)(2,1)} %pad_maximum_fusion.1.x_ref, f32[1,2048]{1,0:T(1,128)} %bitcast.204, ...), custom_call_target="tpu_custom_call" | custom-call | bytes 1000 | tf_op jit(solution)/shard_map/attention/pallas_call | solution.py:326
  136.9 23.2 %collective-permute-done.11 = bf16[2,64,2048]{2,1,0:T(8,128)(2,1)S(1)} collective-permute-done((bf16[2,64,2048]{2,1,0:T(8,128)(2,1)S(1)}, bf16[2,64,2048]{2,1,0:T(8,128)(2,1)S(1)}, u32[]{:S(2)}, u32[]{:S(2)}) %collective-permute-start.11) | collective-permute-done | bytes 524320 | tf_op jit(solution)/shard_map/ppermute | solution.py:62
  165.1 11.0 %collective-permute-done.15 = bf16[2,64,2048]{2,1,0:T(8,128)(2,1)S(1)} collective-permute-done((bf16[2,64,2048]{2,1,0:T(8,128)(2,1)S(1)}, bf16[2,64,2048]{2,1,0:T(8,128)(2,1)S(1)}, u32[]{:S(2)}, u32[]{:S(2)}) %collective-permute-start.15) | collective-permute-done | bytes 524320 | tf_op jit(solution)/shard_map/ppermute | solution.py:49
  176.1 11.4 %collective-permute-done.14 = bf16[2,64,2048]{2,1,0:T(8,128)(2,1)S(1)} collective-permute-done((bf16[2,64,2048]{2,1,0:T(8,128)(2,1)S(1)}, bf16[2,64,2048]{2,1,0:T(8,128)(2,1)S(1)}, u32[]{:S(2)}, u32[]{:S(2)}) %collective-permute-start.14) | collective-permute-done | bytes 524320 | tf_op jit(solution)/shard_map/ppermute | solution.py:49
  195.7 13.9 %all-gather.9.cloned.1.call-done = bf16[4608,2048]{1,0:T(8,128)(2,1)} async-done(((bf16[288,2048]{1,0:T(8,128)(2,1)}), bf16[4608,2048]{1,0:T(8,128)(2,1)}) %all-gather.9.cloned.1.call-update) | async-done | bytes 18874384 | tf_op jit(solution)/shard_map/all_gather | solution.py:869
  209.5 48.9 %experts_rows.1 = (bf16[1024,1536]{1,0:T(8,128)(2,1)}, bf16[1024,1536]{1,0:T(8,128)(2,1)}, bf16[1024,1536]{1,0:T(8,128)(2,1)}, bf16[512,2048]{1,0:T(8,128)(2,1)}, bf16[512,2048]{1,0:T(8,128)(2,1)}) custom-call(bf16[1024,2048]{1,0:T(8,128)(2,1)} %bitcast.156, bf16[1024,2176]{1,0:T(8,128)(2,1)} %bitcast.154, bf16[16,288,2048]{2,1,0:T(8,128)(2,1)} %bitcast.160, ...), custom_call_target="tpu_custom_call" | custom-call | bytes 1000 | tf_op jit(solution)/shard_map/experts_rows/pallas_call | solution.py:388
  259.3 27.0 %experts_weights.1 = (bf16[16,288,2048]{2,1,0:T(8,128)(2,1)}, f32[8,128]{1,0:T(8,128)}) custom-call(bf16[1024,1536]{1,0:T(8,128)(2,1)} %get-tuple-element.63.dg_ref, bf16[1024,1536]{1,0:T(8,128)(2,1)} %get-tuple-element.64.du_ref, bf16[1024,1536]{1,0:T(8,128)(2,1)} %get-tuple-element.62.hid_ref.token_ref, bf16[1024,2048]{1,0:T(8,128)(2,1)} %bitcast.157, ...), custom_call_target="tpu_custom_call" | custom-call | bytes 1000 | tf_op jit(solution)/shard_map/experts_weights/pallas_call | solution.py:431
  297.2 12.1 %experts_out.1 = (bf16[512,2048]{1,0:T(8,128)(2,1)}, bf16[512,2048]{1,0:T(8,128)(2,1)}) custom-call(bf16[1024,1536]{1,0:T(8,128)(2,1)} %get-tuple-element.62.hid_ref.token_ref, bf16[16,288,2048]{2,1,0:T(8,128)(2,1)} %bitcast.161, f32[8,128]{1,0:T(8,128)} %get-tuple-element.65.token_ref), custom_call_target="tpu_custom_call" | custom-call | flops 6442450944 | bytes 20000000 | tf_op jit(solution)/shard_map/experts_out/pallas_call | solution.py:777
  310.5 8.8 %collective-permute-done.21 = bf16[2,64,2048]{2,1,0:T(8,128)(2,1)S(1)} collective-permute-done((bf16[2,64,2048]{2,1,0:T(8,128)(2,1)}, bf16[2,64,2048]{2,1,0:T(8,128)(2,1)S(1)}, u32[]{:S(2)}, u32[]{:S(2)}) %collective-permute-start.21) | collective-permute-done | bytes 524320 | tf_op jit(solution)/shard_map/ppermute | solution.py:62
  327.7 4.8 add_cores_placed.2.refs_0_.token_ref
  336.5 12.5 %collective-permute-done.24 = bf16[2,64,2048]{2,1,0:T(8,128)(2,1)S(1)} collective-permute-done((bf16[2,64,2048]{2,1,0:T(8,128)(2,1)S(1)}, bf16[2,64,2048]{2,1,0:T(8,128)(2,1)S(1)}, u32[]{:S(2)}, u32[]{:S(2)}) %collective-permute-start.24) | collective-permute-done | bytes 524320 | tf_op jit(solution)/shard_map/ppermute | solution.py:49
  357.1 6.4 %out_weights.1 = bf16[512,2048]{1,0:T(8,128)(2,1)} custom-call(bf16[2,512,512]{2,1,0:T(8,128)(2,1)} %bitcast.185, bf16[512,2048]{1,0:T(8,128)(2,1)} %bitcast.158, bf16[512,2048]{1,0:T(8,128)(2,1)} %bitcast.60.theirs_ref), custom_call_target="tpu_custom_call" | custom-call | bytes 1000 | tf_op jit(solution)/shard_map/out_weights/pallas_call | solution.py:550
  363.6 26.5 %attention_back.1 = (bf16[2,4,2,64,768]{4,3,2,1,0:T(8,128)(2,1)}, bf16[1,4,2,64,2048]{4,3,2,1,0:T(8,128)(2,1)}, bf16[1,4,2,64,2048]{4,3,2,1,0:T(8,128)(2,1)}, f3...) custom-call(bf16[1,4,2,64,2048]{4,3,2,1,0:T(8,128)(2,1)} %bitcast.56.theirs_da_ref, ...), custom_call_target="tpu_custom_call" | custom-call | flops 8999999488 | bytes 90000000 | tf_op jit(solution)/shard_map/attention_back/pallas_call | solution.py:326
  398.7 10.1 %attention_weights.1 = (bf16[4,80,1280]{2,1,0:T(8,128)(2,1)}, bf16[4,80,1280]{2,1,0:T(8,128)(2,1)}, bf16[4,80,1280]{2,1,0:T(8,128)(2,1)}, bf16[4,80,1280]{2,1,0:...) custom-call(s32[2]{0:T(128)} %pad_add_fusion.2.place_ref, ...), custom_call_target="tpu_custom_call" | custom-call | bytes 1000 | tf_op jit(solution)/shard_map/attention_weights/pallas_call | solution.py:595
  418.2 11.8 %collective-permute-done.31.refs_5_ = bf16[4,64,1280]{2,1,0:T(8,128)(2,1)} collective-permute-done((bf16[4,64,1280]{2,1,0:T(8,128)(2,1)}, bf16[4,64,1280]{2,1,0:T(8,128)(2,1)}, u32[]{:S(2)}, u32[]{:S(2)}) %collective-permute-start.31) | collective-permute-done | bytes 655392 | tf_op jit(solution)/shard_map/ppermute | solution.py:91
  430.0 4.8 add_cores_placed.3.refs_8_.token_ref
  442.4 9.2 %collective-permute-done.30.refs_3_ = bf16[4,80,1280]{2,1,0:T(8,128)(2,1)} collective-permute-done((bf16[4,80,1280]{2,1,0:T(8,128)(2,1)}, bf16[4,80,1280]{2,1,0:T(8,128)(2,1)}, u32[]{:S(2)}, u32[]{:S(2)}) %collective-permute-start.30) | collective-permute-done | bytes 819232 | tf_op jit(solution)/shard_map/ppermute | solution.py:91
  451.6 5.7 %half_sum.1 = (bf16[80,1280]{1,0:T(8,128)(2,1)}, bf16[80,1280]{1,0:T(8,128)(2,1)}, bf16[80,1280]{1,0:T(8,128)(2,1)}, bf16[80,1280]{1,0:T(8,128)(2,1)}, bf16[64,1...) custom-call(s32[2]{0:T(128)} %pad_add_fusion.2.place_ref, ...), custom_call_target="tpu_custom_call" | custom-call | bytes 1000 | tf_op jit(solution)/shard_map/half_sum/pallas_call | solution.py:638
  464.0 5.5 %collective-permute-done.38.refs_6_ = bf16[64,1280]{1,0:T(8,128)(2,1)S(1)} collective-permute-done((bf16[64,1280]{1,0:T(8,128)(2,1)}, bf16[64,1280]{1,0:T(8,128)(2,1)S(1)}, u32[]{:S(2)}, u32[]{:S(2)}) %collective-permute-start.38) | collective-permute-done | bytes 163872 | tf_op jit(solution)/shard_map/ppermute | solution.py:91
  480.8 7.9 %collective-permute-start.44 = (bf16[32,2048]{1,0:T(8,128)(2,1)S(1)}, bf16[32,2048]{1,0:T(8,128)(2,1)S(1)}, u32[]{:S(2)}, u32[]{:S(2)}) collective-permute-start(bf16[32,2048]{1,0:T(8,128)(2,1)S(1)} %pad_maximum_fusion.12), channel_id=1, source_target_pairs={{0,0},{8,1},{16,2},{24,3},{32,4},{40,5},{48,6},{56,7},{64,8},{72,9... | collective-permute-start | bytes 393224 | tf_op jit(solution)/shard_map/ppermute | solution.py:1042
  488.7 5.1 collective-permute-done.40
  493.8 9.0 %collective-permute-done.42 = bf16[144,768]{1,0:T(8,128)(2,1)S(1)} collective-permute-done((bf16[144,768]{1,0:T(8,128)(2,1)S(1)}, bf16[144,768]{1,0:T(8,128)(2,1)S(1)}, u32[]{:S(2)}, u32[]{:S(2)}) %collective-permute-start.42) | collective-permute-done | bytes 221216 | tf_op jit(solution)/shard_map/ppermute | solution.py:82
  511.0 11.5 %experts_results.1 = (f32[2048,768]{1,0:T(8,128)}, f32[2048,768]{1,0:T(8,128)}, f32[768,2048]{1,0:T(8,128)}) custom-call(bf16[8,288,2048]{2,1,0:T(8,128)(2,1)} %bitcast.162), custom_call_target="tpu_custom_call" | custom-call | bytes 1000 | tf_op jit(solution)/shard_map/experts_results/pallas_call | solution.py:520
  525.9 4.7 columns_results.1
  (239 shorter events, 161.7 us)
Async XLA Ops:
  7.2 94.8 %all-gather.7.cloned.1.call-start = ((), (), s32[]{:S(2)}) async-start(), calls=%async_computation.3 | async-start | bytes 6266880 | tf_op jit(solution)/shard_map/all_gather | solution.py:866
  25.4 184.2 %all-gather.9.cloned.1.call-start = ((), (), s32[]{:S(2)}) async-start(), calls=%async_computation.4 | async-start | bytes 20054016 | tf_op jit(solution)/shard_map/all_gather | solution.py:869
  33.9 377.9 %reduce-scatter.4.cloned.1.call-start = ((), (), s32[]{:S(2)}) async-start(), calls=%async_computation.6 | async-start | bytes 20054016
  34.1 21.8 %collective-permute-start = (bf16[2,64,2048]{2,1,0:T(8,128)(2,1)S(1)}, bf16[2,64,2048]{2,1,0:T(8,128)(2,1)S(1)}, u32[]{:S(2)}, u32[]{:S(2)}) collective-permute-start(bf16[2,64,2048]{2,1,0:T(8,128)(2,1)S(1)} %bitcast.166), channel_id=1, source_target_pairs={{2,0},{4,2},{6,4},{0,6},{3,1},{5,3},{7,5},{1,7},{10,8},{12,10},{14... | collective-permute-start | bytes 1572872 | tf_op jit(solution)/shard_map/ppermute | solution.py:49
  35.1 25.7 %collective-permute-start.2 = (bf16[2,64,2048]{2,1,0:T(8,128)(2,1)S(1)}, bf16[2,64,2048]{2,1,0:T(8,128)(2,1)}, u32[]{:S(2)}, u32[]{:S(2)}) collective-permute-start(bf16[2,64,2048]{2,1,0:T(8,128)(2,1)S(1)} %bitcast.167), channel_id=1, source_target_pairs={{6,0},{0,2},{2,4},{4,6},{7,1},{1,3},{3,5},{5,7},{14,8},{8,10},{10,... | collective-permute-start | bytes 1572872 | tf_op jit(solution)/shard_map/ppermute | solution.py:49
  36.4 36.6 %collective-permute-start.8 = (bf16[2,64,2176]{2,1,0:T(8,128)(2,1)S(1)}, bf16[2,64,2176]{2,1,0:T(8,128)(2,1)S(1)}, u32[]{:S(2)}, u32[]{:S(2)}) collective-permute-start(bf16[2,64,2176]{2,1,0:T(8,128)(2,1)S(1)} %concatenate.52), channel_id=1, source_target_pairs={{6,0},{0,2},{2,4},{4,6},{7,1},{1,3},{3,5},{5,7},{14,8},{8,10},{10,... | collective-permute-start | bytes 1671176 | tf_op jit(solution)/shard_map/ppermute | solution.py:49
  37.6 46.6 %collective-permute-start.7 = (bf16[2,64,2176]{2,1,0:T(8,128)(2,1)S(1)}, bf16[2,64,2176]{2,1,0:T(8,128)(2,1)S(1)}, u32[]{:S(2)}, u32[]{:S(2)}) collective-permute-start(bf16[2,64,2176]{2,1,0:T(8,128)(2,1)S(1)} %concatenate.52), channel_id=1, source_target_pairs={{4,0},{6,2},{0,4},{2,6},{5,1},{7,3},{1,5},{3,7},{12,8},{14,10},{8,... | collective-permute-start | bytes 1671176 | tf_op jit(solution)/shard_map/ppermute | solution.py:49
  49.1 35.1 %collective-permute-start.6 = (bf16[2,64,2176]{2,1,0:T(8,128)(2,1)S(1)}, bf16[2,64,2176]{2,1,0:T(8,128)(2,1)S(1)}, u32[]{:S(2)}, u32[]{:S(2)}) collective-permute-start(bf16[2,64,2176]{2,1,0:T(8,128)(2,1)S(1)} %concatenate.52), channel_id=1, source_target_pairs={{2,0},{4,2},{6,4},{0,6},{3,1},{5,3},{7,5},{1,7},{10,8},{12,10},{14... | collective-permute-start | bytes 1671176 | tf_op jit(solution)/shard_map/ppermute | solution.py:49
  64.2 28.8 %collective-permute-start.3 = (bf16[4,2,64,2048]{3,2,1,0:T(8,128)(2,1)}, bf16[4,2,64,2048]{3,2,1,0:T(8,128)(2,1)}, u32[]{:S(2)}, u32[]{:S(2)}) collective-permute-start(bf16[4,2,64,2048]{3,2,1,0:T(8,128)(2,1)} %get-tuple-element.187), channel_id=1, source_target_pairs={{0,1},{1,0},{2,3},{3,2},{4,5},{5,4},{6,7},{7,6},{8,9},{9,8},{10,11... | collective-permute-start | bytes 6291464 | tf_op jit(solution)/shard_map/ppermute | solution.py:43
  133.7 26.4 %collective-permute-start.11 = (bf16[2,64,2048]{2,1,0:T(8,128)(2,1)S(1)}, bf16[2,64,2048]{2,1,0:T(8,128)(2,1)S(1)}, u32[]{:S(2)}, u32[]{:S(2)}) collective-permute-start(bf16[2,64,2048]{2,1,0:T(8,128)(2,1)S(1)} %get-tuple-element.179), channel_id=1, source_target_pairs={{0,2},{2,4},{4,6},{6,0},{1,3},{3,5},{5,7},{7,1},{8,10},{10,12},{12... | collective-permute-start | bytes 1572872 | tf_op jit(solution)/shard_map/ppermute | solution.py:62
  134.3 25.9 %collective-permute-start.13 = (bf16[2,64,2048]{2,1,0:T(8,128)(2,1)S(1)}, bf16[2,64,2048]{2,1,0:T(8,128)(2,1)S(1)}, u32[]{:S(2)}, u32[]{:S(2)}) collective-permute-start(bf16[2,64,2048]{2,1,0:T(8,128)(2,1)S(1)} %get-tuple-element.180), channel_id=1, source_target_pairs={{0,6},{2,0},{4,2},{6,4},{1,7},{3,1},{5,3},{7,5},{8,14},{10,8},{12,... | collective-permute-start | bytes 1572872 | tf_op jit(solution)/shard_map/ppermute | solution.py:62
  136.9 23.2 %collective-permute-start.12 = (bf16[2,64,2048]{2,1,0:T(8,128)(2,1)S(1)}, bf16[2,64,2048]{2,1,0:T(8,128)(2,1)S(1)}, u32[]{:S(2)}, u32[]{:S(2)}) collective-permute-start(bf16[2,64,2048]{2,1,0:T(8,128)(2,1)S(1)} %get-tuple-element.181), channel_id=1, source_target_pairs={{0,4},{2,6},{4,0},{6,2},{1,5},{3,7},{5,1},{7,3},{8,12},{10,14},{12... | collective-permute-start | bytes 1572872 | tf_op jit(solution)/shard_map/ppermute | solution.py:62
  162.6 24.9 %collective-permute-start.14 = (bf16[2,64,2048]{2,1,0:T(8,128)(2,1)S(1)}, bf16[2,64,2048]{2,1,0:T(8,128)(2,1)S(1)}, u32[]{:S(2)}, u32[]{:S(2)}) collective-permute-start(bf16[2,64,2048]{2,1,0:T(8,128)(2,1)S(1)} %multiply_convert_fusion), channel_id=1, source_target_pairs={{2,0},{4,2},{6,4},{0,6},{3,1},{5,3},{7,5},{1,7},{10,8},{12,10},{14... | collective-permute-start | bytes 1572872 | tf_op jit(solution)/shard_map/ppermute | solution.py:49
  165.0 23.7 %collective-permute-start.16 = (bf16[2,64,2048]{2,1,0:T(8,128)(2,1)S(1)}, bf16[2,64,2048]{2,1,0:T(8,128)(2,1)S(1)}, u32[]{:S(2)}, u32[]{:S(2)}) collective-permute-start(bf16[2,64,2048]{2,1,0:T(8,128)(2,1)S(1)} %multiply_convert_fusion), channel_id=1, source_target_pairs={{6,0},{0,2},{2,4},{4,6},{7,1},{1,3},{3,5},{5,7},{14,8},{8,10},{10,... | collective-permute-start | bytes 1572872 | tf_op jit(solution)/shard_map/ppermute | solution.py:49
  258.4 27.9 %collective-permute-start.19 = (bf16[4,2,64,2048]{3,2,1,0:T(8,128)(2,1)}, bf16[4,2,64,2048]{3,2,1,0:T(8,128)(2,1)S(1)}, u32[]{:S(2)}, u32[]{:S(2)}) collective-permute-start(bf16[4,2,64,2048]{3,2,1,0:T(8,128)(2,1)} %bitcast.217), channel_id=1, source_target_pairs={{0,1},{1,0},{2,3},{3,2},{4,5},{5,4},{6,7},{7,6},{8,9},{9,8},{10,11... | collective-permute-start | bytes 6291464 | tf_op jit(solution)/shard_map/ppermute | solution.py:43
  292.3 26.9 %collective-permute-start.20 = (bf16[2,64,2048]{2,1,0:T(8,128)(2,1)S(1)}, bf16[2,64,2048]{2,1,0:T(8,128)(2,1)S(1)}, u32[]{:S(2)}, u32[]{:S(2)}) collective-permute-start(bf16[2,64,2048]{2,1,0:T(8,128)(2,1)S(1)} %copy-done.14), channel_id=1, source_target_pairs={{0,2},{2,4},{4,6},{6,0},{1,3},{3,5},{5,7},{7,1},{8,10},{10,12},{12... | collective-permute-start | bytes 1572872 | tf_op jit(solution)/shard_map/ppermute | solution.py:62
  293.6 25.7 %collective-permute-start.21 = (bf16[2,64,2048]{2,1,0:T(8,128)(2,1)}, bf16[2,64,2048]{2,1,0:T(8,128)(2,1)S(1)}, u32[]{:S(2)}, u32[]{:S(2)}) collective-permute-start(bf16[2,64,2048]{2,1,0:T(8,128)(2,1)} %get-tuple-element.72), channel_id=1, source_target_pairs={{0,4},{2,6},{4,0},{6,2},{1,5},{3,7},{5,1},{7,3},{8,12},{10,14},{12... | collective-permute-start | bytes 1572872 | tf_op jit(solution)/shard_map/ppermute | solution.py:62
  296.0 23.3 %collective-permute-start.22 = (bf16[2,64,2048]{2,1,0:T(8,128)(2,1)}, bf16[2,64,2048]{2,1,0:T(8,128)(2,1)S(1)}, u32[]{:S(2)}, u32[]{:S(2)}) collective-permute-start(bf16[2,64,2048]{2,1,0:T(8,128)(2,1)} %get-tuple-element.73), channel_id=1, source_target_pairs={{0,6},{2,0},{4,2},{6,4},{1,7},{3,1},{5,3},{7,5},{8,14},{10,8},{12,... | collective-permute-start | bytes 1572872 | tf_op jit(solution)/shard_map/ppermute | solution.py:62
  309.2 18.4 %collective-permute-start.18 = (bf16[4,2,64,2048]{3,2,1,0:T(8,128)(2,1)}, bf16[4,2,64,2048]{3,2,1,0:T(8,128)(2,1)}, u32[]{:S(2)}, u32[]{:S(2)}) collective-permute-start(bf16[4,2,64,2048]{3,2,1,0:T(8,128)(2,1)} %bitcast.216), channel_id=1, source_target_pairs={{0,1},{1,0},{2,3},{3,2},{4,5},{5,4},{6,7},{7,6},{8,9},{9,8},{10,11... | collective-permute-start | bytes 6291464 | tf_op jit(solution)/shard_map/ppermute | solution.py:43
  323.6 25.5 %collective-permute-start.24 = (bf16[2,64,2048]{2,1,0:T(8,128)(2,1)S(1)}, bf16[2,64,2048]{2,1,0:T(8,128)(2,1)S(1)}, u32[]{:S(2)}, u32[]{:S(2)}) collective-permute-start(bf16[2,64,2048]{2,1,0:T(8,128)(2,1)S(1)} %fusion.38), channel_id=1, source_target_pairs={{4,0},{6,2},{0,4},{2,6},{5,1},{7,3},{1,5},{3,7},{12,8},{14,10},{8,... | collective-permute-start | bytes 1572872 | tf_op jit(solution)/shard_map/ppermute | solution.py:49
  326.3 22.8 %collective-permute-start.23 = (bf16[2,64,2048]{2,1,0:T(8,128)(2,1)S(1)}, bf16[2,64,2048]{2,1,0:T(8,128)(2,1)}, u32[]{:S(2)}, u32[]{:S(2)}) collective-permute-start(bf16[2,64,2048]{2,1,0:T(8,128)(2,1)S(1)} %fusion.38), channel_id=1, source_target_pairs={{2,0},{4,2},{6,4},{0,6},{3,1},{5,3},{7,5},{1,7},{10,8},{12,10},{14... | collective-permute-start | bytes 1572872 | tf_op jit(solution)/shard_map/ppermute | solution.py:49
  353.0 39.5 %all-to-all-start = ((bf16[4,2,64,2048]{3,2,1,0:T(8,128)(2,1)}), bf16[4,2,64,2048]{3,2,1,0:T(8,128)(2,1)S(1)}, u32[]{:S(2)}, u32[]{:S(2)}) async-start(bf16[4,2,64,2048]{3,2,1,0:T(8,128)(2,1)} %add_cores_placed.2.refs_0_.token_ref), calls=%async_computation | async-start | bytes 4194304 | tf_op jit(solution)/shard_map/all_to_all | solution.py:481
  356.6 154.4 %all-gather.11.cloned.1.call-start = ((), (), s32[]{:S(2)}) async-start(), calls=%async_computation.5 | async-start | bytes 10616832 | tf_op jit(solution)/shard_map/all_gather | solution.py:1030
  390.1 18.7 %collective-permute-start.27 = (bf16[4,2,64,2048]{3,2,1,0:T(8,128)(2,1)}, bf16[4,2,64,2048]{3,2,1,0:T(8,128)(2,1)}, u32[]{:S(2)}, u32[]{:S(2)}) collective-permute-start(bf16[4,2,64,2048]{3,2,1,0:T(8,128)(2,1)} %bitcast.215), channel_id=1, source_target_pairs={{0,1},{1,0},{2,3},{3,2},{4,5},{5,4},{6,7},{7,6},{8,9},{9,8},{10,11... | collective-permute-start | bytes 6291464 | tf_op jit(solution)/shard_map/ppermute | solution.py:43
  412.0 30.4 %collective-permute-start.29 = (bf16[4,80,1280]{2,1,0:T(8,128)(2,1)}, bf16[4,80,1280]{2,1,0:T(8,128)(2,1)S(1)}, u32[]{:S(2)}, u32[]{:S(2)}) collective-permute-start(bf16[4,80,1280]{2,1,0:T(8,128)(2,1)} %get-tuple-element.85), channel_id=1, source_target_pairs={{64,0},{72,8},{80,16},{88,24},{96,32},{104,40},{112,48},{120,56},{... | collective-permute-start | bytes 2457608 | tf_op jit(solution)/shard_map/ppermute | solution.py:91
  413.2 38.4 %collective-permute-start.30 = (bf16[4,80,1280]{2,1,0:T(8,128)(2,1)}, bf16[4,80,1280]{2,1,0:T(8,128)(2,1)}, u32[]{:S(2)}, u32[]{:S(2)}) collective-permute-start(bf16[4,80,1280]{2,1,0:T(8,128)(2,1)} %get-tuple-element.86), channel_id=1, source_target_pairs={{32,0},{40,8},{48,16},{56,24},{64,32},{72,40},{80,48},{88,56},{96,... | collective-permute-start | bytes 2457608 | tf_op jit(solution)/shard_map/ppermute | solution.py:91
  413.8 37.8 %collective-permute-start.28 = (bf16[4,80,1280]{2,1,0:T(8,128)(2,1)S(1)}, bf16[4,80,1280]{2,1,0:T(8,128)(2,1)}, u32[]{:S(2)}, u32[]{:S(2)}) collective-permute-start(bf16[4,80,1280]{2,1,0:T(8,128)(2,1)S(1)} %copy-done.8), channel_id=1, source_target_pairs={{96,0},{104,8},{112,16},{120,24},{0,32},{8,40},{16,48},{24,56},{32... | collective-permute-start | bytes 2457608 | tf_op jit(solution)/shard_map/ppermute | solution.py:91
  415.9 26.5 %collective-permute-start.32 = (bf16[4,64,1280]{2,1,0:T(8,128)(2,1)}, bf16[4,64,1280]{2,1,0:T(8,128)(2,1)}, u32[]{:S(2)}, u32[]{:S(2)}) collective-permute-start(bf16[4,64,1280]{2,1,0:T(8,128)(2,1)} %get-tuple-element.89), channel_id=1, source_target_pairs={{16,0},{24,8},{0,16},{8,24},{48,32},{56,40},{32,48},{40,56},{80,64... | collective-permute-start | bytes 1966088 | tf_op jit(solution)/shard_map/ppermute | solution.py:91
  434.8 69.9 %all-to-all-start.1 = ((bf16[4,2,64,2048]{3,2,1,0:T(8,128)(2,1)}), bf16[4,2,64,2048]{3,2,1,0:T(8,128)(2,1)}, u32[]{:S(2)}, u32[]{:S(2)}) async-start(bf16[4,2,64,2048]{3,2,1,0:T(8,128)(2,1)} %add_cores_placed.3.refs_8_.token_ref), calls=%async_computation.1 | async-start | bytes 4194304 | tf_op jit(solution)/shard_map/all_to_all | solution.py:481
  479.1 23.7 %collective-permute-start.42 = (bf16[144,768]{1,0:T(8,128)(2,1)S(1)}, bf16[144,768]{1,0:T(8,128)(2,1)S(1)}, u32[]{:S(2)}, u32[]{:S(2)}) collective-permute-start(bf16[144,768]{1,0:T(8,128)(2,1)S(1)} %get-tuple-element.193), channel_id=1, source_target_pairs={{6,0},{0,2},{2,4},{4,6},{7,1},{1,3},{3,5},{5,7},{14,8},{8,10},{10,... | collective-permute-start | bytes 663560 | tf_op jit(solution)/shard_map/ppermute | solution.py:82
  480.8 41.7 %collective-permute-start.44 = (bf16[32,2048]{1,0:T(8,128)(2,1)S(1)}, bf16[32,2048]{1,0:T(8,128)(2,1)S(1)}, u32[]{:S(2)}, u32[]{:S(2)}) collective-permute-start(bf16[32,2048]{1,0:T(8,128)(2,1)S(1)} %pad_maximum_fusion.12), channel_id=1, source_target_pairs={{0,0},{8,1},{16,2},{24,3},{32,4},{40,5},{48,6},{56,7},{64,8},{72,9... | collective-permute-start | bytes 393224 | tf_op jit(solution)/shard_map/ppermute | solution.py:1042
  503.8 22.1 %collective-permute-start.43 = (bf16[4,144,768]{2,1,0:T(8,128)(2,1)}, bf16[4,144,768]{2,1,0:T(8,128)(2,1)}, u32[]{:S(2)}, u32[]{:S(2)}) collective-permute-start(bf16[4,144,768]{2,1,0:T(8,128)(2,1)} %pad_maximum_fusion.8.mine_ref), channel_id=1, source_target_pairs={{0,1},{1,0},{2,3},{3,2},{4,5},{5,4},{6,7},{7,6},{8,9},{9,8},{10,11... | collective-permute-start | bytes 2654216 | tf_op jit(solution)/shard_map/ppermute | solution.py:43
  (50 other events, 391.5 us)
Sparse Core Ops, SparseCore 0:
  25.5 60.0 all-gather.6
  87.8 121.7 all-gather.8
  291.5 120.3 reduce-scatter.3
  413.4 71.3 all-gather.10

commit v6 on v5

--- a/solution.py
+++ b/solution.py
@@ -1031,7 +1031,7 @@
     firsts, seconds = plane_send(firsts, 1, 0), plane_send(seconds, 0, 1)
     firsts, seconds = half_sum_call(place, firsts, seconds, h1_pieces)
     result_gate, result_up, result_down = gate_up_down_call(all_experts, ff_part)
-    grads = last_sum_call(plane_send(firsts, 0, 1), plane_send(seconds, 1, 0), h1_pieces)
+    grads = last_sum_call(plane_send(firsts, 0, 1), plane_send(seconds, 1, 0), input_grad)
     out_sum = jnp.concatenate(
         [grads[k * out_part : (k + 1) * out_part, qkv_width:] for k in range(depth // out_part)],
         axis=1,
@@ -1039,7 +1039,7 @@
     result_q, result_k, result_v, gain_sum = columns_call(
         where, *gather_members(grads[:, :qkv_width]), depth, q_width, head
     )
-    out_sum = after_call(lax.ppermute(out_sum, EVERY, back), input_grad, result_down)
+    out_sum = after_call(lax.ppermute(out_sum, EVERY, back), result_down)
     result_out = rows_call(where, *gather_members(out_sum, result_q))
     gain_sum = gain_sum[0]
     return (

time: 559 us -> 560 us (level)
    ppermute x6, waiting for transfers between devices: 16.3 us -> 10.5 us  [gather_members(): lax.ppermute(v, 'context', [((i + k) % ring, i) for i in range(ring)])]
    unnamed x57 -> x63, local copies, waits for them, and re-layouts: 9.38 us -> 11.3 us
where the time goes in v6:
time: 560 us; the launch traced here: 549 us
  Pallas kernels  195 us (35%)
  waiting for transfers between devices  194 us (35%)
  starting transfers between devices  71 us (13%)
  other arithmetic  50.6 us (9%)
  local copies, waits for them, and re-layouts  24.9 us (4%)
  between operations  14.8 us (3%)
    ppermute x12, waiting for transfers between devices, ring_stack(): lax.ppermute(own, 'context', [((i + k) % ring, i) for i in range(ring)])  80.6 us
    pallas_call x1, Pallas kernels, experts_call(): pl.pallas_call(functools.partial(experts_kernel, part), grid=(n, blocks),...  48.9 us
    pallas_call x2, Pallas kernels, attend_call(): pl.pallas_call(kernel, grid=(2 * micro,), in_specs=in_specs, out_specs=ou...  48.6 us
    ppermute x12, waiting for transfers between devices, plane(): return lax.ppermute(v, 'experts', moves)  37.2 us
    ppermute x6, waiting for transfers between devices, ring_sum(): lax.ppermute(pieces[k], 'context', [(i, (i + k) % ring) for i in range(ri...  32 us
    pallas_call x1, Pallas kernels, expert_grads_call(): pl.pallas_call(functools.partial(expert_grads_kernel, part), grid=(n,), i...  27 us
    another operation x6, other arithmetic, gather_rows(): return jnp.stack([mine, swap(mine)])  18 us
    all_gather x1, waiting for transfers between devices, local(): expert_all = lax.all_gather(expert_pack, 'experts', axis=0, tiled=False)  13.9 us
  transfers between devices with their start and end apart: 55, of which 28 were waited for; matrix products, arithmetic and copies ran while one was open for 12% of the time, Pallas kernels for 25%

profile of v6, /device:TPU:7, one launch (start us, length us, event | category | flops | bytes accessed | tf_op | source)
XLA Modules:
  0.0 549.5 jit_solution(2249225467426123734)
XLA Ops:
  8.3 6.5 %collective-permute-start.4 = (bf16[32,2048]{1,0:T(8,128)(2,1)S(1)}, bf16[32,2048]{1,0:T(8,128)(2,1)S(1)}, u32[]{:S(2)}, u32[]{:S(2)}) collective-permute-start(bf16[32,2048]{1,0:T(8,128)(2,1)S(1)} %constant_dynamic-slice_fusion.2), channel_id=1, source_target_pairs={{0,0},{1,8},{2,16},{3,24},{4,32},{5,40},{6,48},{7,56},{8,64},{9,72... | collective-permute-start | bytes 393224 | tf_op jit(solution)/shard_map/ppermute | solution.py:843
  17.3 7.3 %collective-permute-done.4 = bf16[32,2048]{1,0:T(8,128)(2,1)S(1)} collective-permute-done((bf16[32,2048]{1,0:T(8,128)(2,1)S(1)}, bf16[32,2048]{1,0:T(8,128)(2,1)S(1)}, u32[]{:S(2)}, u32[]{:S(2)}) %collective-permute-start.4) | collective-permute-done | bytes 131104 | tf_op jit(solution)/shard_map/ppermute | solution.py:843
  39.8 9.3 %collective-permute-done.1 = bf16[2,64,2048]{2,1,0:T(8,128)(2,1)S(1)} collective-permute-done((bf16[2,64,2048]{2,1,0:T(8,128)(2,1)S(1)}, bf16[2,64,2048]{2,1,0:T(8,128)(2,1)S(1)}, u32[]{:S(2)}, u32[]{:S(2)}) %collective-permute-start.1) | collective-permute-done | bytes 524320 | tf_op jit(solution)/shard_map/ppermute | solution.py:49
  49.1 6.8 %collective-permute-done = bf16[2,64,2048]{2,1,0:T(8,128)(2,1)S(1)} collective-permute-done((bf16[2,64,2048]{2,1,0:T(8,128)(2,1)S(1)}, bf16[2,64,2048]{2,1,0:T(8,128)(2,1)S(1)}, u32[]{:S(2)}, u32[]{:S(2)}) %collective-permute-start) | collective-permute-done | bytes 524320 | tf_op jit(solution)/shard_map/ppermute | solution.py:49
  55.9 4.8 collective-permute-done.2
  64.7 8.3 %collective-permute-done.8 = bf16[2,64,2176]{2,1,0:T(8,128)(2,1)S(1)} collective-permute-done((bf16[2,64,2176]{2,1,0:T(8,128)(2,1)S(1)}, bf16[2,64,2176]{2,1,0:T(8,128)(2,1)S(1)}, u32[]{:S(2)}, u32[]{:S(2)}) %collective-permute-start.8) | collective-permute-done | bytes 557088 | tf_op jit(solution)/shard_map/ppermute | solution.py:49
  73.0 11.2 %collective-permute-done.7 = bf16[2,64,2176]{2,1,0:T(8,128)(2,1)S(1)} collective-permute-done((bf16[2,64,2176]{2,1,0:T(8,128)(2,1)S(1)}, bf16[2,64,2176]{2,1,0:T(8,128)(2,1)S(1)}, u32[]{:S(2)}, u32[]{:S(2)}) %collective-permute-start.7) | collective-permute-done | bytes 557088 | tf_op jit(solution)/shard_map/ppermute | solution.py:49
  92.9 4.6 pad_maximum_fusion.1.x_ref
  104.9 22.0 %attention.1 = (bf16[2,4,2,64,2048]{4,3,2,1,0:T(8,128)(2,1)}, f32[2,4,2,64,768]{4,3,2,1,0:T(8,128)}, bf16[2,4,2,64,512]{4,3,2,1,0:T(8,128)(2,1)}, bf16[1,4,2,64,...) custom-call(bf16[2,4,2,64,2048]{4,3,2,1,0:T(8,128)(2,1)} %pad_maximum_fusion.1.x_ref, f32[1,2048]{1,0:T(1,128)} %bitcast.204, ...), custom_call_target="tpu_custom_call" | custom-call | bytes 1000 | tf_op jit(solution)/shard_map/attention/pallas_call | solution.py:326
  136.9 23.2 %collective-permute-done.11 = bf16[2,64,2048]{2,1,0:T(8,128)(2,1)S(1)} collective-permute-done((bf16[2,64,2048]{2,1,0:T(8,128)(2,1)S(1)}, bf16[2,64,2048]{2,1,0:T(8,128)(2,1)S(1)}, u32[]{:S(2)}, u32[]{:S(2)}) %collective-permute-start.11) | collective-permute-done | bytes 524320 | tf_op jit(solution)/shard_map/ppermute | solution.py:62
  165.1 11.0 %collective-permute-done.15 = bf16[2,64,2048]{2,1,0:T(8,128)(2,1)S(1)} collective-permute-done((bf16[2,64,2048]{2,1,0:T(8,128)(2,1)S(1)}, bf16[2,64,2048]{2,1,0:T(8,128)(2,1)S(1)}, u32[]{:S(2)}, u32[]{:S(2)}) %collective-permute-start.15) | collective-permute-done | bytes 524320 | tf_op jit(solution)/shard_map/ppermute | solution.py:49
  176.1 11.4 %collective-permute-done.14 = bf16[2,64,2048]{2,1,0:T(8,128)(2,1)S(1)} collective-permute-done((bf16[2,64,2048]{2,1,0:T(8,128)(2,1)S(1)}, bf16[2,64,2048]{2,1,0:T(8,128)(2,1)S(1)}, u32[]{:S(2)}, u32[]{:S(2)}) %collective-permute-start.14) | collective-permute-done | bytes 524320 | tf_op jit(solution)/shard_map/ppermute | solution.py:49
  195.7 13.9 %all-gather.9.cloned.1.call-done = bf16[4608,2048]{1,0:T(8,128)(2,1)} async-done(((bf16[288,2048]{1,0:T(8,128)(2,1)}), bf16[4608,2048]{1,0:T(8,128)(2,1)}) %all-gather.9.cloned.1.call-update) | async-done | bytes 18874384 | tf_op jit(solution)/shard_map/all_gather | solution.py:869
  209.5 48.9 %experts_rows.1 = (bf16[1024,1536]{1,0:T(8,128)(2,1)}, bf16[1024,1536]{1,0:T(8,128)(2,1)}, bf16[1024,1536]{1,0:T(8,128)(2,1)}, bf16[512,2048]{1,0:T(8,128)(2,1)}, bf16[512,2048]{1,0:T(8,128)(2,1)}) custom-call(bf16[1024,2048]{1,0:T(8,128)(2,1)} %bitcast.156, bf16[1024,2176]{1,0:T(8,128)(2,1)} %bitcast.154, bf16[16,288,2048]{2,1,0:T(8,128)(2,1)} %bitcast.160, ...), custom_call_target="tpu_custom_call" | custom-call | bytes 1000 | tf_op jit(solution)/shard_map/experts_rows/pallas_call | solution.py:388
  259.3 27.0 %experts_weights.1 = (bf16[16,288,2048]{2,1,0:T(8,128)(2,1)}, f32[8,128]{1,0:T(8,128)}) custom-call(bf16[1024,1536]{1,0:T(8,128)(2,1)} %get-tuple-element.63.dg_ref, bf16[1024,1536]{1,0:T(8,128)(2,1)} %get-tuple-element.64.du_ref, bf16[1024,1536]{1,0:T(8,128)(2,1)} %get-tuple-element.62.hid_ref.token_ref, bf16[1024,2048]{1,0:T(8,128)(2,1)} %bitcast.157, ...), custom_call_target="tpu_custom_call" | custom-call | bytes 1000 | tf_op jit(solution)/shard_map/experts_weights/pallas_call | solution.py:431
  297.2 12.1 %experts_out.1 = (bf16[512,2048]{1,0:T(8,128)(2,1)}, bf16[512,2048]{1,0:T(8,128)(2,1)}) custom-call(bf16[1024,1536]{1,0:T(8,128)(2,1)} %get-tuple-element.62.hid_ref.token_ref, bf16[16,288,2048]{2,1,0:T(8,128)(2,1)} %bitcast.161, f32[8,128]{1,0:T(8,128)} %get-tuple-element.65.token_ref), custom_call_target="tpu_custom_call" | custom-call | flops 6442450944 | bytes 20000000 | tf_op jit(solution)/shard_map/experts_out/pallas_call | solution.py:777
  310.5 8.8 %collective-permute-done.21 = bf16[2,64,2048]{2,1,0:T(8,128)(2,1)S(1)} collective-permute-done((bf16[2,64,2048]{2,1,0:T(8,128)(2,1)}, bf16[2,64,2048]{2,1,0:T(8,128)(2,1)S(1)}, u32[]{:S(2)}, u32[]{:S(2)}) %collective-permute-start.21) | collective-permute-done | bytes 524320 | tf_op jit(solution)/shard_map/ppermute | solution.py:62
  327.6 4.8 add_cores_placed.2.refs_0_.token_ref
  336.5 12.5 %collective-permute-done.24 = bf16[2,64,2048]{2,1,0:T(8,128)(2,1)S(1)} collective-permute-done((bf16[2,64,2048]{2,1,0:T(8,128)(2,1)S(1)}, bf16[2,64,2048]{2,1,0:T(8,128)(2,1)S(1)}, u32[]{:S(2)}, u32[]{:S(2)}) %collective-permute-start.24) | collective-permute-done | bytes 524320 | tf_op jit(solution)/shard_map/ppermute | solution.py:49
  357.1 6.4 %out_weights.1 = bf16[512,2048]{1,0:T(8,128)(2,1)} custom-call(bf16[2,512,512]{2,1,0:T(8,128)(2,1)} %bitcast.185, bf16[512,2048]{1,0:T(8,128)(2,1)} %bitcast.158, bf16[512,2048]{1,0:T(8,128)(2,1)} %bitcast.60.theirs_ref), custom_call_target="tpu_custom_call" | custom-call | bytes 1000 | tf_op jit(solution)/shard_map/out_weights/pallas_call | solution.py:550
  363.6 26.6 %attention_back.1 = (bf16[2,4,2,64,768]{4,3,2,1,0:T(8,128)(2,1)}, bf16[1,4,2,64,2048]{4,3,2,1,0:T(8,128)(2,1)}, bf16[1,4,2,64,2048]{4,3,2,1,0:T(8,128)(2,1)}, f3...) custom-call(bf16[1,4,2,64,2048]{4,3,2,1,0:T(8,128)(2,1)} %bitcast.56.theirs_da_ref, ...), custom_call_target="tpu_custom_call" | custom-call | flops 8999999488 | bytes 90000000 | tf_op jit(solution)/shard_map/attention_back/pallas_call | solution.py:326
  398.7 10.1 %attention_weights.1 = (bf16[4,80,1280]{2,1,0:T(8,128)(2,1)}, bf16[4,80,1280]{2,1,0:T(8,128)(2,1)}, bf16[4,80,1280]{2,1,0:T(8,128)(2,1)}, bf16[4,80,1280]{2,1,0:...) custom-call(s32[2]{0:T(128)} %pad_add_fusion.2.place_ref, ...), custom_call_target="tpu_custom_call" | custom-call | bytes 1000 | tf_op jit(solution)/shard_map/attention_weights/pallas_call | solution.py:595
  411.9 4.7 add_cores_placed.3.refs_8_
  416.6 4.6 all-to-all-start.1
  427.5 11.8 %collective-permute-done.31.refs_5_ = bf16[4,64,1280]{2,1,0:T(8,128)(2,1)S(1)} collective-permute-done((bf16[4,64,1280]{2,1,0:T(8,128)(2,1)}, bf16[4,64,1280]{2,1,0:T(8,128)(2,1)S(1)}, u32[]{:S(2)}, u32[]{:S(2)}) %collective-permute-start.31) | collective-permute-done | bytes 655392 | tf_op jit(solution)/shard_map/ppermute | solution.py:91
  439.3 12.4 %collective-permute-done.32.refs_6_ = bf16[4,64,1280]{2,1,0:T(8,128)(2,1)S(1)} collective-permute-done((bf16[4,64,1280]{2,1,0:T(8,128)(2,1)}, bf16[4,64,1280]{2,1,0:T(8,128)(2,1)S(1)}, u32[]{:S(2)}, u32[]{:S(2)}) %collective-permute-start.32) | collective-permute-done | bytes 655392 | tf_op jit(solution)/shard_map/ppermute | solution.py:91
  451.7 9.2 %collective-permute-done.30.refs_3_ = bf16[4,80,1280]{2,1,0:T(8,128)(2,1)S(1)} collective-permute-done((bf16[4,80,1280]{2,1,0:T(8,128)(2,1)}, bf16[4,80,1280]{2,1,0:T(8,128)(2,1)S(1)}, u32[]{:S(2)}, u32[]{:S(2)}) %collective-permute-start.30) | collective-permute-done | bytes 819232 | tf_op jit(solution)/shard_map/ppermute | solution.py:91
  462.0 5.5 %half_sum.1 = (bf16[80,1280]{1,0:T(8,128)(2,1)}, bf16[80,1280]{1,0:T(8,128)(2,1)}, bf16[80,1280]{1,0:T(8,128)(2,1)}, bf16[80,1280]{1,0:T(8,128)(2,1)}, bf16[64,1...) custom-call(s32[2]{0:T(128)} %pad_add_fusion.2.place_ref, ...), custom_call_target="tpu_custom_call" | custom-call | bytes 1000 | tf_op jit(solution)/shard_map/half_sum/pallas_call | solution.py:638
  494.7 4.6 collective-permute-done.40
  504.7 6.7 %collective-permute-start.44 = (bf16[32,2048]{1,0:T(8,128)(2,1)S(1)}, bf16[32,2048]{1,0:T(8,128)(2,1)S(1)}, u32[]{:S(2)}, u32[]{:S(2)}) collective-permute-start(bf16[32,2048]{1,0:T(8,128)(2,1)S(1)} %pad_maximum_fusion.12), channel_id=1, source_target_pairs={{0,0},{8,1},{16,2},{24,3},{32,4},{40,5},{48,6},{56,7},{64,8},{72,9... | collective-permute-start | bytes 393224 | tf_op jit(solution)/shard_map/ppermute | solution.py:1042
  511.4 11.5 %experts_results.1 = (f32[2048,768]{1,0:T(8,128)}, f32[2048,768]{1,0:T(8,128)}, f32[768,2048]{1,0:T(8,128)}) custom-call(bf16[8,288,2048]{2,1,0:T(8,128)(2,1)} %bitcast.162), custom_call_target="tpu_custom_call" | custom-call | bytes 1000 | tf_op jit(solution)/shard_map/experts_results/pallas_call | solution.py:520
  527.6 4.7 columns_results.1
  (245 shorter events, 161.6 us)
Async XLA Ops:
  7.2 94.8 %all-gather.7.cloned.1.call-start = ((), (), s32[]{:S(2)}) async-start(), calls=%async_computation.3 | async-start | bytes 6266880 | tf_op jit(solution)/shard_map/all_gather | solution.py:866
  25.4 184.2 %all-gather.9.cloned.1.call-start = ((), (), s32[]{:S(2)}) async-start(), calls=%async_computation.4 | async-start | bytes 20054016 | tf_op jit(solution)/shard_map/all_gather | solution.py:869
  33.9 377.9 %reduce-scatter.4.cloned.1.call-start = ((), (), s32[]{:S(2)}) async-start(), calls=%async_computation.6 | async-start | bytes 20054016
  34.1 21.8 %collective-permute-start = (bf16[2,64,2048]{2,1,0:T(8,128)(2,1)S(1)}, bf16[2,64,2048]{2,1,0:T(8,128)(2,1)S(1)}, u32[]{:S(2)}, u32[]{:S(2)}) collective-permute-start(bf16[2,64,2048]{2,1,0:T(8,128)(2,1)S(1)} %bitcast.166), channel_id=1, source_target_pairs={{2,0},{4,2},{6,4},{0,6},{3,1},{5,3},{7,5},{1,7},{10,8},{12,10},{14... | collective-permute-start | bytes 1572872 | tf_op jit(solution)/shard_map/ppermute | solution.py:49
  35.1 25.7 %collective-permute-start.2 = (bf16[2,64,2048]{2,1,0:T(8,128)(2,1)S(1)}, bf16[2,64,2048]{2,1,0:T(8,128)(2,1)}, u32[]{:S(2)}, u32[]{:S(2)}) collective-permute-start(bf16[2,64,2048]{2,1,0:T(8,128)(2,1)S(1)} %bitcast.167), channel_id=1, source_target_pairs={{6,0},{0,2},{2,4},{4,6},{7,1},{1,3},{3,5},{5,7},{14,8},{8,10},{10,... | collective-permute-start | bytes 1572872 | tf_op jit(solution)/shard_map/ppermute | solution.py:49
  36.4 36.6 %collective-permute-start.8 = (bf16[2,64,2176]{2,1,0:T(8,128)(2,1)S(1)}, bf16[2,64,2176]{2,1,0:T(8,128)(2,1)S(1)}, u32[]{:S(2)}, u32[]{:S(2)}) collective-permute-start(bf16[2,64,2176]{2,1,0:T(8,128)(2,1)S(1)} %concatenate.52), channel_id=1, source_target_pairs={{6,0},{0,2},{2,4},{4,6},{7,1},{1,3},{3,5},{5,7},{14,8},{8,10},{10,... | collective-permute-start | bytes 1671176 | tf_op jit(solution)/shard_map/ppermute | solution.py:49
  37.6 46.6 %collective-permute-start.7 = (bf16[2,64,2176]{2,1,0:T(8,128)(2,1)S(1)}, bf16[2,64,2176]{2,1,0:T(8,128)(2,1)S(1)}, u32[]{:S(2)}, u32[]{:S(2)}) collective-permute-start(bf16[2,64,2176]{2,1,0:T(8,128)(2,1)S(1)} %concatenate.52), channel_id=1, source_target_pairs={{4,0},{6,2},{0,4},{2,6},{5,1},{7,3},{1,5},{3,7},{12,8},{14,10},{8,... | collective-permute-start | bytes 1671176 | tf_op jit(solution)/shard_map/ppermute | solution.py:49
  49.1 35.1 %collective-permute-start.6 = (bf16[2,64,2176]{2,1,0:T(8,128)(2,1)S(1)}, bf16[2,64,2176]{2,1,0:T(8,128)(2,1)S(1)}, u32[]{:S(2)}, u32[]{:S(2)}) collective-permute-start(bf16[2,64,2176]{2,1,0:T(8,128)(2,1)S(1)} %concatenate.52), channel_id=1, source_target_pairs={{2,0},{4,2},{6,4},{0,6},{3,1},{5,3},{7,5},{1,7},{10,8},{12,10},{14... | collective-permute-start | bytes 1671176 | tf_op jit(solution)/shard_map/ppermute | solution.py:49
  64.2 28.8 %collective-permute-start.3 = (bf16[4,2,64,2048]{3,2,1,0:T(8,128)(2,1)}, bf16[4,2,64,2048]{3,2,1,0:T(8,128)(2,1)}, u32[]{:S(2)}, u32[]{:S(2)}) collective-permute-start(bf16[4,2,64,2048]{3,2,1,0:T(8,128)(2,1)} %get-tuple-element.187), channel_id=1, source_target_pairs={{0,1},{1,0},{2,3},{3,2},{4,5},{5,4},{6,7},{7,6},{8,9},{9,8},{10,11... | collective-permute-start | bytes 6291464 | tf_op jit(solution)/shard_map/ppermute | solution.py:43
  133.7 26.4 %collective-permute-start.11 = (bf16[2,64,2048]{2,1,0:T(8,128)(2,1)S(1)}, bf16[2,64,2048]{2,1,0:T(8,128)(2,1)S(1)}, u32[]{:S(2)}, u32[]{:S(2)}) collective-permute-start(bf16[2,64,2048]{2,1,0:T(8,128)(2,1)S(1)} %get-tuple-element.179), channel_id=1, source_target_pairs={{0,2},{2,4},{4,6},{6,0},{1,3},{3,5},{5,7},{7,1},{8,10},{10,12},{12... | collective-permute-start | bytes 1572872 | tf_op jit(solution)/shard_map/ppermute | solution.py:62
  134.3 25.9 %collective-permute-start.13 = (bf16[2,64,2048]{2,1,0:T(8,128)(2,1)S(1)}, bf16[2,64,2048]{2,1,0:T(8,128)(2,1)S(1)}, u32[]{:S(2)}, u32[]{:S(2)}) collective-permute-start(bf16[2,64,2048]{2,1,0:T(8,128)(2,1)S(1)} %get-tuple-element.180), channel_id=1, source_target_pairs={{0,6},{2,0},{4,2},{6,4},{1,7},{3,1},{5,3},{7,5},{8,14},{10,8},{12,... | collective-permute-start | bytes 1572872 | tf_op jit(solution)/shard_map/ppermute | solution.py:62
  136.9 23.2 %collective-permute-start.12 = (bf16[2,64,2048]{2,1,0:T(8,128)(2,1)S(1)}, bf16[2,64,2048]{2,1,0:T(8,128)(2,1)S(1)}, u32[]{:S(2)}, u32[]{:S(2)}) collective-permute-start(bf16[2,64,2048]{2,1,0:T(8,128)(2,1)S(1)} %get-tuple-element.181), channel_id=1, source_target_pairs={{0,4},{2,6},{4,0},{6,2},{1,5},{3,7},{5,1},{7,3},{8,12},{10,14},{12... | collective-permute-start | bytes 1572872 | tf_op jit(solution)/shard_map/ppermute | solution.py:62
  162.6 24.9 %collective-permute-start.14 = (bf16[2,64,2048]{2,1,0:T(8,128)(2,1)S(1)}, bf16[2,64,2048]{2,1,0:T(8,128)(2,1)S(1)}, u32[]{:S(2)}, u32[]{:S(2)}) collective-permute-start(bf16[2,64,2048]{2,1,0:T(8,128)(2,1)S(1)} %multiply_convert_fusion), channel_id=1, source_target_pairs={{2,0},{4,2},{6,4},{0,6},{3,1},{5,3},{7,5},{1,7},{10,8},{12,10},{14... | collective-permute-start | bytes 1572872 | tf_op jit(solution)/shard_map/ppermute | solution.py:49
  165.0 23.7 %collective-permute-start.16 = (bf16[2,64,2048]{2,1,0:T(8,128)(2,1)S(1)}, bf16[2,64,2048]{2,1,0:T(8,128)(2,1)S(1)}, u32[]{:S(2)}, u32[]{:S(2)}) collective-permute-start(bf16[2,64,2048]{2,1,0:T(8,128)(2,1)S(1)} %multiply_convert_fusion), channel_id=1, source_target_pairs={{6,0},{0,2},{2,4},{4,6},{7,1},{1,3},{3,5},{5,7},{14,8},{8,10},{10,... | collective-permute-start | bytes 1572872 | tf_op jit(solution)/shard_map/ppermute | solution.py:49
  258.4 27.9 %collective-permute-start.19 = (bf16[4,2,64,2048]{3,2,1,0:T(8,128)(2,1)}, bf16[4,2,64,2048]{3,2,1,0:T(8,128)(2,1)S(1)}, u32[]{:S(2)}, u32[]{:S(2)}) collective-permute-start(bf16[4,2,64,2048]{3,2,1,0:T(8,128)(2,1)} %bitcast.217), channel_id=1, source_target_pairs={{0,1},{1,0},{2,3},{3,2},{4,5},{5,4},{6,7},{7,6},{8,9},{9,8},{10,11... | collective-permute-start | bytes 6291464 | tf_op jit(solution)/shard_map/ppermute | solution.py:43
  292.4 26.9 %collective-permute-start.20 = (bf16[2,64,2048]{2,1,0:T(8,128)(2,1)S(1)}, bf16[2,64,2048]{2,1,0:T(8,128)(2,1)S(1)}, u32[]{:S(2)}, u32[]{:S(2)}) collective-permute-start(bf16[2,64,2048]{2,1,0:T(8,128)(2,1)S(1)} %copy-done.21), channel_id=1, source_target_pairs={{0,2},{2,4},{4,6},{6,0},{1,3},{3,5},{5,7},{7,1},{8,10},{10,12},{12... | collective-permute-start | bytes 1572872 | tf_op jit(solution)/shard_map/ppermute | solution.py:62
  293.6 25.7 %collective-permute-start.21 = (bf16[2,64,2048]{2,1,0:T(8,128)(2,1)}, bf16[2,64,2048]{2,1,0:T(8,128)(2,1)S(1)}, u32[]{:S(2)}, u32[]{:S(2)}) collective-permute-start(bf16[2,64,2048]{2,1,0:T(8,128)(2,1)} %get-tuple-element.72), channel_id=1, source_target_pairs={{0,4},{2,6},{4,0},{6,2},{1,5},{3,7},{5,1},{7,3},{8,12},{10,14},{12... | collective-permute-start | bytes 1572872 | tf_op jit(solution)/shard_map/ppermute | solution.py:62
  296.0 23.3 %collective-permute-start.22 = (bf16[2,64,2048]{2,1,0:T(8,128)(2,1)}, bf16[2,64,2048]{2,1,0:T(8,128)(2,1)S(1)}, u32[]{:S(2)}, u32[]{:S(2)}) collective-permute-start(bf16[2,64,2048]{2,1,0:T(8,128)(2,1)} %get-tuple-element.73), channel_id=1, source_target_pairs={{0,6},{2,0},{4,2},{6,4},{1,7},{3,1},{5,3},{7,5},{8,14},{10,8},{12,... | collective-permute-start | bytes 1572872 | tf_op jit(solution)/shard_map/ppermute | solution.py:62
  309.3 18.4 %collective-permute-start.18 = (bf16[4,2,64,2048]{3,2,1,0:T(8,128)(2,1)}, bf16[4,2,64,2048]{3,2,1,0:T(8,128)(2,1)}, u32[]{:S(2)}, u32[]{:S(2)}) collective-permute-start(bf16[4,2,64,2048]{3,2,1,0:T(8,128)(2,1)} %bitcast.216), channel_id=1, source_target_pairs={{0,1},{1,0},{2,3},{3,2},{4,5},{5,4},{6,7},{7,6},{8,9},{9,8},{10,11... | collective-permute-start | bytes 6291464 | tf_op jit(solution)/shard_map/ppermute | solution.py:43
  323.6 25.5 %collective-permute-start.24 = (bf16[2,64,2048]{2,1,0:T(8,128)(2,1)S(1)}, bf16[2,64,2048]{2,1,0:T(8,128)(2,1)S(1)}, u32[]{:S(2)}, u32[]{:S(2)}) collective-permute-start(bf16[2,64,2048]{2,1,0:T(8,128)(2,1)S(1)} %fusion.38), channel_id=1, source_target_pairs={{4,0},{6,2},{0,4},{2,6},{5,1},{7,3},{1,5},{3,7},{12,8},{14,10},{8,... | collective-permute-start | bytes 1572872 | tf_op jit(solution)/shard_map/ppermute | solution.py:49
  326.3 22.8 %collective-permute-start.23 = (bf16[2,64,2048]{2,1,0:T(8,128)(2,1)S(1)}, bf16[2,64,2048]{2,1,0:T(8,128)(2,1)}, u32[]{:S(2)}, u32[]{:S(2)}) collective-permute-start(bf16[2,64,2048]{2,1,0:T(8,128)(2,1)S(1)} %fusion.38), channel_id=1, source_target_pairs={{2,0},{4,2},{6,4},{0,6},{3,1},{5,3},{7,5},{1,7},{10,8},{12,10},{14... | collective-permute-start | bytes 1572872 | tf_op jit(solution)/shard_map/ppermute | solution.py:49
  353.0 39.5 %all-to-all-start = ((bf16[4,2,64,2048]{3,2,1,0:T(8,128)(2,1)}), bf16[4,2,64,2048]{3,2,1,0:T(8,128)(2,1)S(1)}, u32[]{:S(2)}, u32[]{:S(2)}) async-start(bf16[4,2,64,2048]{3,2,1,0:T(8,128)(2,1)} %add_cores_placed.2.refs_0_.token_ref), calls=%async_computation | async-start | bytes 4194304 | tf_op jit(solution)/shard_map/all_to_all | solution.py:481
  356.6 154.8 %all-gather.11.cloned.1.call-start = ((), (), s32[]{:S(2)}) async-start(), calls=%async_computation.5 | async-start | bytes 10616832 | tf_op jit(solution)/shard_map/all_gather | solution.py:1030
  390.1 18.7 %collective-permute-start.27 = (bf16[4,2,64,2048]{3,2,1,0:T(8,128)(2,1)}, bf16[4,2,64,2048]{3,2,1,0:T(8,128)(2,1)}, u32[]{:S(2)}, u32[]{:S(2)}) collective-permute-start(bf16[4,2,64,2048]{3,2,1,0:T(8,128)(2,1)} %bitcast.215), channel_id=1, source_target_pairs={{0,1},{1,0},{2,3},{3,2},{4,5},{5,4},{6,7},{7,6},{8,9},{9,8},{10,11... | collective-permute-start | bytes 6291464 | tf_op jit(solution)/shard_map/ppermute | solution.py:43
  416.6 57.1 %all-to-all-start.1 = ((bf16[4,2,64,2048]{3,2,1,0:T(8,128)(2,1)}), bf16[4,2,64,2048]{3,2,1,0:T(8,128)(2,1)}, u32[]{:S(2)}, u32[]{:S(2)}) async-start(bf16[4,2,64,2048]{3,2,1,0:T(8,128)(2,1)} %add_cores_placed.3.refs_8_), calls=%async_computation.1 | async-start | bytes 4194304 | tf_op jit(solution)/shard_map/all_to_all | solution.py:481
  421.2 18.1 %collective-permute-start.31 = (bf16[4,64,1280]{2,1,0:T(8,128)(2,1)}, bf16[4,64,1280]{2,1,0:T(8,128)(2,1)S(1)}, u32[]{:S(2)}, u32[]{:S(2)}) collective-permute-start(bf16[4,64,1280]{2,1,0:T(8,128)(2,1)} %get-tuple-element.88), channel_id=1, source_target_pairs={{24,0},{0,8},{8,16},{16,24},{56,32},{32,40},{40,48},{48,56},{88,64... | collective-permute-start | bytes 1966088 | tf_op jit(solution)/shard_map/ppermute | solution.py:91
  421.2 30.4 %collective-permute-start.29 = (bf16[4,80,1280]{2,1,0:T(8,128)(2,1)}, bf16[4,80,1280]{2,1,0:T(8,128)(2,1)S(1)}, u32[]{:S(2)}, u32[]{:S(2)}) collective-permute-start(bf16[4,80,1280]{2,1,0:T(8,128)(2,1)} %get-tuple-element.85), channel_id=1, source_target_pairs={{64,0},{72,8},{80,16},{88,24},{96,32},{104,40},{112,48},{120,56},{... | collective-permute-start | bytes 2457608 | tf_op jit(solution)/shard_map/ppermute | solution.py:91
  422.5 38.4 %collective-permute-start.30 = (bf16[4,80,1280]{2,1,0:T(8,128)(2,1)}, bf16[4,80,1280]{2,1,0:T(8,128)(2,1)S(1)}, u32[]{:S(2)}, u32[]{:S(2)}) collective-permute-start(bf16[4,80,1280]{2,1,0:T(8,128)(2,1)} %get-tuple-element.86), channel_id=1, source_target_pairs={{32,0},{40,8},{48,16},{56,24},{64,32},{72,40},{80,48},{88,56},{96,... | collective-permute-start | bytes 2457608 | tf_op jit(solution)/shard_map/ppermute | solution.py:91
  423.1 37.8 %collective-permute-start.28 = (bf16[4,80,1280]{2,1,0:T(8,128)(2,1)S(1)}, bf16[4,80,1280]{2,1,0:T(8,128)(2,1)S(1)}, u32[]{:S(2)}, u32[]{:S(2)}) collective-permute-start(bf16[4,80,1280]{2,1,0:T(8,128)(2,1)S(1)} %copy-done.9), channel_id=1, source_target_pairs={{96,0},{104,8},{112,16},{120,24},{0,32},{8,40},{16,48},{24,56},{32... | collective-permute-start | bytes 2457608 | tf_op jit(solution)/shard_map/ppermute | solution.py:91
  425.2 26.5 %collective-permute-start.32 = (bf16[4,64,1280]{2,1,0:T(8,128)(2,1)}, bf16[4,64,1280]{2,1,0:T(8,128)(2,1)S(1)}, u32[]{:S(2)}, u32[]{:S(2)}) collective-permute-start(bf16[4,64,1280]{2,1,0:T(8,128)(2,1)} %get-tuple-element.89), channel_id=1, source_target_pairs={{16,0},{24,8},{0,16},{8,24},{48,32},{56,40},{32,48},{40,56},{80,64... | collective-permute-start | bytes 1966088 | tf_op jit(solution)/shard_map/ppermute | solution.py:91
  501.8 24.9 %collective-permute-start.43 = (bf16[4,144,768]{2,1,0:T(8,128)(2,1)S(1)}, bf16[4,144,768]{2,1,0:T(8,128)(2,1)S(1)}, u32[]{:S(2)}, u32[]{:S(2)}) collective-permute-start(bf16[4,144,768]{2,1,0:T(8,128)(2,1)S(1)} %pad_maximum_fusion.8.mine_ref), channel_id=1, source_target_pairs={{0,1},{1,0},{2,3},{3,2},{4,5},{5,4},{6,7},{7,6},{8,9},{9,8},{10,11... | collective-permute-start | bytes 2654216 | tf_op jit(solution)/shard_map/ppermute | solution.py:43
  504.7 18.3 %collective-permute-start.44 = (bf16[32,2048]{1,0:T(8,128)(2,1)S(1)}, bf16[32,2048]{1,0:T(8,128)(2,1)S(1)}, u32[]{:S(2)}, u32[]{:S(2)}) collective-permute-start(bf16[32,2048]{1,0:T(8,128)(2,1)S(1)} %pad_maximum_fusion.12), channel_id=1, source_target_pairs={{0,0},{8,1},{16,2},{24,3},{32,4},{40,5},{48,6},{56,7},{64,8},{72,9... | collective-permute-start | bytes 393224 | tf_op jit(solution)/shard_map/ppermute | solution.py:1042
  (53 other events, 436.0 us)
Sparse Core Ops, SparseCore 0:
  25.5 60.0 all-gather.6
  87.8 121.7 all-gather.8
  291.5 120.3 reduce-scatter.3
  413.4 74.2 all-gather.10

commit v7 on v5

--- a/solution.py
+++ b/solution.py
@@ -1021,17 +1021,16 @@
     firsts, seconds = attend_grads_call(
         place, h1, d_qkv, grad_out, grad_gains, output, depth // 2 + 16
     )
-    h1_theirs = swap(theirs[0])
-    h1_pieces = add_placed_call(where, h1_theirs, mine[0], firsts[1])
+    h1_pieces = add_placed_call(where, swap(theirs[0]), mine[0], firsts[1])
     d_h1 = exchange_sum(h1_pieces)
     x_f32 = x_own.astype(F32)
     input_grad = (d_x1 + norm_back(d_h1, x_f32, inverse_rms(x_f32), gain_attn))[:, None]
-    grad_experts = after_call(grad_experts, firsts[1], h1_theirs)
+    grad_experts = after_call(grad_experts, h1_pieces)
     all_experts = lax.all_gather(grad_experts, GROUP, axis=0, tiled=False)
     firsts, seconds = plane_send(firsts, 1, 0), plane_send(seconds, 0, 1)
-    firsts, seconds = half_sum_call(place, firsts, seconds, h1_pieces)
+    firsts, seconds = half_sum_call(place, firsts, seconds, grad_out)
     result_gate, result_up, result_down = gate_up_down_call(all_experts, ff_part)
-    grads = last_sum_call(plane_send(firsts, 0, 1), plane_send(seconds, 1, 0), h1_pieces)
+    grads = last_sum_call(plane_send(firsts, 0, 1), plane_send(seconds, 1, 0), d_h1)
     out_sum = jnp.concatenate(
         [grads[k * out_part : (k + 1) * out_part, qkv_width:] for k in range(depth // out_part)],
         axis=1,

time: 559 us -> 554 us (level)
  the two profiles are of different devices: /device:TPU:7 before, /device:TPU:49 now
where the time goes in v7:
time: 554 us; the launch traced here: 544 us
  Pallas kernels  195 us (35%)
  waiting for transfers between devices  189 us (34%)
  starting transfers between devices  74.9 us (14%)
  other arithmetic  48.5 us (9%)
  local copies, waits for them, and re-layouts  22.6 us (4%)
  between operations  14.7 us (3%)
    ppermute x12, waiting for transfers between devices, ring_stack(): lax.ppermute(own, 'context', [((i + k) % ring, i) for i in range(ring)])  78.6 us
    pallas_call x1, Pallas kernels, experts_call(): pl.pallas_call(functools.partial(experts_kernel, part), grid=(n, blocks),...  48.9 us
    pallas_call x2, Pallas kernels, attend_call(): pl.pallas_call(kernel, grid=(2 * micro,), in_specs=in_specs, out_specs=ou...  48.6 us
    ppermute x12, waiting for transfers between devices, plane(): return lax.ppermute(v, 'experts', moves)  39.1 us
    ppermute x6, waiting for transfers between devices, ring_sum(): lax.ppermute(pieces[k], 'context', [(i, (i + k) % ring) for i in range(ri...  32.1 us
    pallas_call x1, Pallas kernels, expert_grads_call(): pl.pallas_call(functools.partial(expert_grads_kernel, part), grid=(n,), i...  27 us
    another operation x6, other arithmetic, gather_rows(): return jnp.stack([mine, swap(mine)])  17.9 us
    ppermute x11, starting transfers between devices, swap(): return lax.ppermute(v, 'dp', [(0, 1), (1, 0)])  15.9 us
  transfers between devices with their start and end apart: 55, of which 32 were waited for; matrix products, arithmetic and copies ran while one was open for 11% of the time, Pallas kernels for 25%

profile of v7, /device:TPU:49, one launch (start us, length us, event | category | flops | bytes accessed | tf_op | source)
XLA Modules:
  0.0 544.1 jit_solution(13467719837690412698)
XLA Ops:
  8.3 4.7 collective-permute-start.4
  15.5 6.9 %collective-permute-done.4 = bf16[32,2048]{1,0:T(8,128)(2,1)S(1)} collective-permute-done((bf16[32,2048]{1,0:T(8,128)(2,1)S(1)}, bf16[32,2048]{1,0:T(8,128)(2,1)S(1)}, u32[]{:S(2)}, u32[]{:S(2)}) %collective-permute-start.4) | collective-permute-done | bytes 131104 | tf_op jit(solution)/shard_map/ppermute | solution.py:843
  38.7 8.3 %collective-permute-done.1 = bf16[2,64,2048]{2,1,0:T(8,128)(2,1)S(1)} collective-permute-done((bf16[2,64,2048]{2,1,0:T(8,128)(2,1)S(1)}, bf16[2,64,2048]{2,1,0:T(8,128)(2,1)S(1)}, u32[]{:S(2)}, u32[]{:S(2)}) %collective-permute-start.1) | collective-permute-done | bytes 524320 | tf_op jit(solution)/shard_map/ppermute | solution.py:49
  47.6 10.3 %collective-permute-done = bf16[2,64,2048]{2,1,0:T(8,128)(2,1)S(1)} collective-permute-done((bf16[2,64,2048]{2,1,0:T(8,128)(2,1)S(1)}, bf16[2,64,2048]{2,1,0:T(8,128)(2,1)S(1)}, u32[]{:S(2)}, u32[]{:S(2)}) %collective-permute-start) | collective-permute-done | bytes 524320 | tf_op jit(solution)/shard_map/ppermute | solution.py:49
  62.6 8.3 %collective-permute-done.8 = bf16[2,64,2176]{2,1,0:T(8,128)(2,1)S(1)} collective-permute-done((bf16[2,64,2176]{2,1,0:T(8,128)(2,1)S(1)}, bf16[2,64,2176]{2,1,0:T(8,128)(2,1)S(1)}, u32[]{:S(2)}, u32[]{:S(2)}) %collective-permute-start.8) | collective-permute-done | bytes 557088 | tf_op jit(solution)/shard_map/ppermute | solution.py:49
  70.9 11.3 %collective-permute-done.7 = bf16[2,64,2176]{2,1,0:T(8,128)(2,1)S(1)} collective-permute-done((bf16[2,64,2176]{2,1,0:T(8,128)(2,1)S(1)}, bf16[2,64,2176]{2,1,0:T(8,128)(2,1)S(1)}, u32[]{:S(2)}, u32[]{:S(2)}) %collective-permute-start.7) | collective-permute-done | bytes 557088 | tf_op jit(solution)/shard_map/ppermute | solution.py:49
  90.9 4.6 pad_maximum_fusion.1.x_ref
  102.8 22.0 %attention.1 = (bf16[2,4,2,64,2048]{4,3,2,1,0:T(8,128)(2,1)}, f32[2,4,2,64,768]{4,3,2,1,0:T(8,128)}, bf16[2,4,2,64,512]{4,3,2,1,0:T(8,128)(2,1)}, bf16[1,4,2,64,...) custom-call(bf16[2,4,2,64,2048]{4,3,2,1,0:T(8,128)(2,1)} %pad_maximum_fusion.1.x_ref, f32[1,2048]{1,0:T(1,128)} %bitcast.205, ...), custom_call_target="tpu_custom_call" | custom-call | bytes 1000 | tf_op jit(solution)/shard_map/attention/pallas_call | solution.py:326
  136.3 9.5 %collective-permute-done.11 = bf16[2,64,2048]{2,1,0:T(8,128)(2,1)S(1)} collective-permute-done((bf16[2,64,2048]{2,1,0:T(8,128)(2,1)S(1)}, bf16[2,64,2048]{2,1,0:T(8,128)(2,1)S(1)}, u32[]{:S(2)}, u32[]{:S(2)}) %collective-permute-start.11) | collective-permute-done | bytes 524320 | tf_op jit(solution)/shard_map/ppermute | solution.py:62
  147.1 10.0 %collective-permute-done.12 = bf16[2,64,2048]{2,1,0:T(8,128)(2,1)S(1)} collective-permute-done((bf16[2,64,2048]{2,1,0:T(8,128)(2,1)S(1)}, bf16[2,64,2048]{2,1,0:T(8,128)(2,1)S(1)}, u32[]{:S(2)}, u32[]{:S(2)}) %collective-permute-start.12) | collective-permute-done | bytes 524320 | tf_op jit(solution)/shard_map/ppermute | solution.py:62
  163.5 9.8 %collective-permute-done.15 = bf16[2,64,2048]{2,1,0:T(8,128)(2,1)S(1)} collective-permute-done((bf16[2,64,2048]{2,1,0:T(8,128)(2,1)S(1)}, bf16[2,64,2048]{2,1,0:T(8,128)(2,1)S(1)}, u32[]{:S(2)}, u32[]{:S(2)}) %collective-permute-start.15) | collective-permute-done | bytes 524320 | tf_op jit(solution)/shard_map/ppermute | solution.py:49
  173.3 12.4 %collective-permute-done.14 = bf16[2,64,2048]{2,1,0:T(8,128)(2,1)S(1)} collective-permute-done((bf16[2,64,2048]{2,1,0:T(8,128)(2,1)S(1)}, bf16[2,64,2048]{2,1,0:T(8,128)(2,1)S(1)}, u32[]{:S(2)}, u32[]{:S(2)}) %collective-permute-start.14) | collective-permute-done | bytes 524320 | tf_op jit(solution)/shard_map/ppermute | solution.py:49
  193.8 15.0 %all-gather.9.cloned.1.call-done = bf16[4608,2048]{1,0:T(8,128)(2,1)} async-done(((bf16[288,2048]{1,0:T(8,128)(2,1)}), bf16[4608,2048]{1,0:T(8,128)(2,1)}) %all-gather.9.cloned.1.call-update) | async-done | bytes 18874384 | tf_op jit(solution)/shard_map/all_gather | solution.py:869
  208.8 48.9 %experts_rows.1 = (bf16[1024,1536]{1,0:T(8,128)(2,1)}, bf16[1024,1536]{1,0:T(8,128)(2,1)}, bf16[1024,1536]{1,0:T(8,128)(2,1)}, bf16[512,2048]{1,0:T(8,128)(2,1)}, bf16[512,2048]{1,0:T(8,128)(2,1)}) custom-call(bf16[1024,2048]{1,0:T(8,128)(2,1)} %bitcast.156, bf16[1024,2176]{1,0:T(8,128)(2,1)} %bitcast.154, bf16[16,288,2048]{2,1,0:T(8,128)(2,1)} %bitcast.163, ...), custom_call_target="tpu_custom_call" | custom-call | bytes 1000 | tf_op jit(solution)/shard_map/experts_rows/pallas_call | solution.py:388
  258.6 27.0 %experts_weights.1 = (bf16[16,288,2048]{2,1,0:T(8,128)(2,1)}, f32[8,128]{1,0:T(8,128)}) custom-call(bf16[1024,1536]{1,0:T(8,128)(2,1)} %get-tuple-element.63.dg_ref, bf16[1024,1536]{1,0:T(8,128)(2,1)} %get-tuple-element.64.du_ref, bf16[1024,1536]{1,0:T(8,128)(2,1)} %get-tuple-element.62.hid_ref.token_ref, bf16[1024,2048]{1,0:T(8,128)(2,1)} %bitcast.157, ...), custom_call_target="tpu_custom_call" | custom-call | bytes 1000 | tf_op jit(solution)/shard_map/experts_weights/pallas_call | solution.py:431
  294.0 12.1 %experts_out.1 = (bf16[512,2048]{1,0:T(8,128)(2,1)}, bf16[512,2048]{1,0:T(8,128)(2,1)}) custom-call(bf16[1024,1536]{1,0:T(8,128)(2,1)} %get-tuple-element.62.hid_ref.token_ref, bf16[16,288,2048]{2,1,0:T(8,128)(2,1)} %bitcast.164, f32[8,128]{1,0:T(8,128)} %get-tuple-element.65.token_ref), custom_call_target="tpu_custom_call" | custom-call | flops 6442450944 | bytes 20000000 | tf_op jit(solution)/shard_map/experts_out/pallas_call | solution.py:777
  306.9 9.6 %collective-permute-done.21 = bf16[2,64,2048]{2,1,0:T(8,128)(2,1)S(1)} collective-permute-done((bf16[2,64,2048]{2,1,0:T(8,128)(2,1)}, bf16[2,64,2048]{2,1,0:T(8,128)(2,1)S(1)}, u32[]{:S(2)}, u32[]{:S(2)}) %collective-permute-start.21) | collective-permute-done | bytes 524320 | tf_op jit(solution)/shard_map/ppermute | solution.py:62
  324.8 4.8 add_cores_placed.2.refs_0_.token_ref
  329.5 4.5 collective-permute-done.25
  334.0 11.4 %collective-permute-done.24 = bf16[2,64,2048]{2,1,0:T(8,128)(2,1)S(1)} collective-permute-done((bf16[2,64,2048]{2,1,0:T(8,128)(2,1)S(1)}, bf16[2,64,2048]{2,1,0:T(8,128)(2,1)S(1)}, u32[]{:S(2)}, u32[]{:S(2)}) %collective-permute-start.24) | collective-permute-done | bytes 524320 | tf_op jit(solution)/shard_map/ppermute | solution.py:49
  351.7 4.5 all-to-all-start
  356.4 6.4 %out_weights.1 = bf16[512,2048]{1,0:T(8,128)(2,1)} custom-call(bf16[2,512,512]{2,1,0:T(8,128)(2,1)} %bitcast.186, bf16[512,2048]{1,0:T(8,128)(2,1)} %bitcast.158, bf16[512,2048]{1,0:T(8,128)(2,1)} %bitcast.60.theirs_ref), custom_call_target="tpu_custom_call" | custom-call | bytes 1000 | tf_op jit(solution)/shard_map/out_weights/pallas_call | solution.py:550
  362.7 26.6 %attention_back.1 = (bf16[2,4,2,64,768]{4,3,2,1,0:T(8,128)(2,1)}, bf16[1,4,2,64,2048]{4,3,2,1,0:T(8,128)(2,1)}, bf16[1,4,2,64,2048]{4,3,2,1,0:T(8,128)(2,1)}, f3...) custom-call(bf16[1,4,2,64,2048]{4,3,2,1,0:T(8,128)(2,1)} %bitcast.56.theirs_da_ref, ...), custom_call_target="tpu_custom_call" | custom-call | flops 8999999488 | bytes 90000000 | tf_op jit(solution)/shard_map/attention_back/pallas_call | solution.py:326
  397.9 10.2 %attention_weights.1 = (bf16[4,80,1280]{2,1,0:T(8,128)(2,1)}, bf16[4,80,1280]{2,1,0:T(8,128)(2,1)}, bf16[4,80,1280]{2,1,0:T(8,128)(2,1)}, bf16[4,80,1280]{2,1,0:...) custom-call(s32[2]{0:T(128)} %pad_add_fusion.2.place_ref, ...), custom_call_target="tpu_custom_call" | custom-call | bytes 1000 | tf_op jit(solution)/shard_map/attention_weights/pallas_call | solution.py:595
  408.1 4.8 add_cores_placed.3.refs_0_
  423.5 9.2 %collective-permute-done.31.refs_5_ = bf16[4,64,1280]{2,1,0:T(8,128)(2,1)S(1)} collective-permute-done((bf16[4,64,1280]{2,1,0:T(8,128)(2,1)}, bf16[4,64,1280]{2,1,0:T(8,128)(2,1)S(1)}, u32[]{:S(2)}, u32[]{:S(2)}) %collective-permute-start.31) | collective-permute-done | bytes 655392 | tf_op jit(solution)/shard_map/ppermute | solution.py:91
  437.4 15.4 %collective-permute-done.33.refs_7_ = bf16[4,64,1280]{2,1,0:T(8,128)(2,1)S(1)} collective-permute-done((bf16[4,64,1280]{2,1,0:T(8,128)(2,1)}, bf16[4,64,1280]{2,1,0:T(8,128)(2,1)S(1)}, u32[]{:S(2)}, u32[]{:S(2)}) %collective-permute-start.33) | collective-permute-done | bytes 655392 | tf_op jit(solution)/shard_map/ppermute | solution.py:91
  458.0 5.5 %half_sum.1 = (bf16[80,1280]{1,0:T(8,128)(2,1)}, bf16[80,1280]{1,0:T(8,128)(2,1)}, bf16[80,1280]{1,0:T(8,128)(2,1)}, bf16[80,1280]{1,0:T(8,128)(2,1)}, bf16[64,1...) custom-call(s32[2]{0:T(128)} %pad_add_fusion.2.place_ref, ...), custom_call_target="tpu_custom_call" | custom-call | bytes 1000 | tf_op jit(solution)/shard_map/half_sum/pallas_call | solution.py:638
  481.4 5.2 collective-permute-start.41
  496.9 7.6 %collective-permute-start.43 = (bf16[4,144,768]{2,1,0:T(8,128)(2,1)}, bf16[4,144,768]{2,1,0:T(8,128)(2,1)}, u32[]{:S(2)}, u32[]{:S(2)}) collective-permute-start(bf16[4,144,768]{2,1,0:T(8,128)(2,1)} %pad_maximum_fusion.8.mine_ref), channel_id=1, source_target_pairs={{0,1},{1,0},{2,3},{3,2},{4,5},{5,4},{6,7},{7,6},{8,9},{9,8},{10,11... | collective-permute-start | bytes 2654216 | tf_op jit(solution)/shard_map/ppermute | solution.py:43
  506.1 11.5 %experts_results.1 = (f32[2048,768]{1,0:T(8,128)}, f32[2048,768]{1,0:T(8,128)}, f32[768,2048]{1,0:T(8,128)}) custom-call(bf16[8,288,2048]{2,1,0:T(8,128)(2,1)} %bitcast.165), custom_call_target="tpu_custom_call" | custom-call | bytes 1000 | tf_op jit(solution)/shard_map/experts_results/pallas_call | solution.py:520
  519.8 4.7 columns_results.1
  (241 shorter events, 166.5 us)
Async XLA Ops:
  7.2 92.7 %all-gather.7.cloned.1.call-start = ((), (), s32[]{:S(2)}) async-start(), calls=%async_computation.3 | async-start | bytes 6266880 | tf_op jit(solution)/shard_map/all_gather | solution.py:866
  23.3 185.6 %all-gather.9.cloned.1.call-start = ((), (), s32[]{:S(2)}) async-start(), calls=%async_computation.4 | async-start | bytes 20054016 | tf_op jit(solution)/shard_map/all_gather | solution.py:869
  31.9 381.0 %reduce-scatter.4.cloned.1.call-start = ((), (), s32[]{:S(2)}) async-start(), calls=%async_computation.6 | async-start | bytes 20054016
  31.9 15.1 %collective-permute-start.1 = (bf16[2,64,2048]{2,1,0:T(8,128)(2,1)S(1)}, bf16[2,64,2048]{2,1,0:T(8,128)(2,1)S(1)}, u32[]{:S(2)}, u32[]{:S(2)}) collective-permute-start(bf16[2,64,2048]{2,1,0:T(8,128)(2,1)S(1)} %bitcast.166), channel_id=1, source_target_pairs={{4,0},{6,2},{0,4},{2,6},{5,1},{7,3},{1,5},{3,7},{12,8},{14,10},{8,... | collective-permute-start | bytes 1572872 | tf_op jit(solution)/shard_map/ppermute | solution.py:49
  32.0 25.9 %collective-permute-start = (bf16[2,64,2048]{2,1,0:T(8,128)(2,1)S(1)}, bf16[2,64,2048]{2,1,0:T(8,128)(2,1)S(1)}, u32[]{:S(2)}, u32[]{:S(2)}) collective-permute-start(bf16[2,64,2048]{2,1,0:T(8,128)(2,1)S(1)} %bitcast.167), channel_id=1, source_target_pairs={{2,0},{4,2},{6,4},{0,6},{3,1},{5,3},{7,5},{1,7},{10,8},{12,10},{14... | collective-permute-start | bytes 1572872 | tf_op jit(solution)/shard_map/ppermute | solution.py:49
  35.2 23.5 %collective-permute-start.2 = (bf16[2,64,2048]{2,1,0:T(8,128)(2,1)S(1)}, bf16[2,64,2048]{2,1,0:T(8,128)(2,1)}, u32[]{:S(2)}, u32[]{:S(2)}) collective-permute-start(bf16[2,64,2048]{2,1,0:T(8,128)(2,1)S(1)} %bitcast.168), channel_id=1, source_target_pairs={{6,0},{0,2},{2,4},{4,6},{7,1},{1,3},{3,5},{5,7},{14,8},{8,10},{10,... | collective-permute-start | bytes 1572872 | tf_op jit(solution)/shard_map/ppermute | solution.py:49
  36.0 34.9 %collective-permute-start.8 = (bf16[2,64,2176]{2,1,0:T(8,128)(2,1)S(1)}, bf16[2,64,2176]{2,1,0:T(8,128)(2,1)S(1)}, u32[]{:S(2)}, u32[]{:S(2)}) collective-permute-start(bf16[2,64,2176]{2,1,0:T(8,128)(2,1)S(1)} %concatenate.52), channel_id=1, source_target_pairs={{6,0},{0,2},{2,4},{4,6},{7,1},{1,3},{3,5},{5,7},{14,8},{8,10},{10,... | collective-permute-start | bytes 1671176 | tf_op jit(solution)/shard_map/ppermute | solution.py:49
  37.7 44.6 %collective-permute-start.7 = (bf16[2,64,2176]{2,1,0:T(8,128)(2,1)S(1)}, bf16[2,64,2176]{2,1,0:T(8,128)(2,1)S(1)}, u32[]{:S(2)}, u32[]{:S(2)}) collective-permute-start(bf16[2,64,2176]{2,1,0:T(8,128)(2,1)S(1)} %concatenate.52), channel_id=1, source_target_pairs={{4,0},{6,2},{0,4},{2,6},{5,1},{7,3},{1,5},{3,7},{12,8},{14,10},{8,... | collective-permute-start | bytes 1671176 | tf_op jit(solution)/shard_map/ppermute | solution.py:49
  47.1 35.2 %collective-permute-start.6 = (bf16[2,64,2176]{2,1,0:T(8,128)(2,1)S(1)}, bf16[2,64,2176]{2,1,0:T(8,128)(2,1)S(1)}, u32[]{:S(2)}, u32[]{:S(2)}) collective-permute-start(bf16[2,64,2176]{2,1,0:T(8,128)(2,1)S(1)} %concatenate.52), channel_id=1, source_target_pairs={{2,0},{4,2},{6,4},{0,6},{3,1},{5,3},{7,5},{1,7},{10,8},{12,10},{14... | collective-permute-start | bytes 1671176 | tf_op jit(solution)/shard_map/ppermute | solution.py:49
  62.1 28.8 %collective-permute-start.3 = (bf16[4,2,64,2048]{3,2,1,0:T(8,128)(2,1)}, bf16[4,2,64,2048]{3,2,1,0:T(8,128)(2,1)}, u32[]{:S(2)}, u32[]{:S(2)}) collective-permute-start(bf16[4,2,64,2048]{3,2,1,0:T(8,128)(2,1)} %get-tuple-element.187), channel_id=1, source_target_pairs={{0,1},{1,0},{2,3},{3,2},{4,5},{5,4},{6,7},{7,6},{8,9},{9,8},{10,11... | collective-permute-start | bytes 6291464 | tf_op jit(solution)/shard_map/ppermute | solution.py:43
  133.9 23.1 %collective-permute-start.12 = (bf16[2,64,2048]{2,1,0:T(8,128)(2,1)S(1)}, bf16[2,64,2048]{2,1,0:T(8,128)(2,1)S(1)}, u32[]{:S(2)}, u32[]{:S(2)}) collective-permute-start(bf16[2,64,2048]{2,1,0:T(8,128)(2,1)S(1)} %get-tuple-element.181), channel_id=1, source_target_pairs={{0,4},{2,6},{4,0},{6,2},{1,5},{3,7},{5,1},{7,3},{8,12},{10,14},{12... | collective-permute-start | bytes 1572872 | tf_op jit(solution)/shard_map/ppermute | solution.py:62
  161.9 23.8 %collective-permute-start.14 = (bf16[2,64,2048]{2,1,0:T(8,128)(2,1)S(1)}, bf16[2,64,2048]{2,1,0:T(8,128)(2,1)S(1)}, u32[]{:S(2)}, u32[]{:S(2)}) collective-permute-start(bf16[2,64,2048]{2,1,0:T(8,128)(2,1)S(1)} %multiply_convert_fusion), channel_id=1, source_target_pairs={{2,0},{4,2},{6,4},{0,6},{3,1},{5,3},{7,5},{1,7},{10,8},{12,10},{14... | collective-permute-start | bytes 1572872 | tf_op jit(solution)/shard_map/ppermute | solution.py:49
  163.0 22.7 %collective-permute-start.16 = (bf16[2,64,2048]{2,1,0:T(8,128)(2,1)S(1)}, bf16[2,64,2048]{2,1,0:T(8,128)(2,1)S(1)}, u32[]{:S(2)}, u32[]{:S(2)}) collective-permute-start(bf16[2,64,2048]{2,1,0:T(8,128)(2,1)S(1)} %multiply_convert_fusion), channel_id=1, source_target_pairs={{6,0},{0,2},{2,4},{4,6},{7,1},{1,3},{3,5},{5,7},{14,8},{8,10},{10,... | collective-permute-start | bytes 1572872 | tf_op jit(solution)/shard_map/ppermute | solution.py:49
  257.8 27.9 %collective-permute-start.19 = (bf16[4,2,64,2048]{3,2,1,0:T(8,128)(2,1)}, bf16[4,2,64,2048]{3,2,1,0:T(8,128)(2,1)S(1)}, u32[]{:S(2)}, u32[]{:S(2)}) collective-permute-start(bf16[4,2,64,2048]{3,2,1,0:T(8,128)(2,1)} %bitcast.218), channel_id=1, source_target_pairs={{0,1},{1,0},{2,3},{3,2},{4,5},{5,4},{6,7},{7,6},{8,9},{9,8},{10,11... | collective-permute-start | bytes 6291464 | tf_op jit(solution)/shard_map/ppermute | solution.py:43
  291.7 26.6 %collective-permute-start.20 = (bf16[2,64,2048]{2,1,0:T(8,128)(2,1)S(1)}, bf16[2,64,2048]{2,1,0:T(8,128)(2,1)S(1)}, u32[]{:S(2)}, u32[]{:S(2)}) collective-permute-start(bf16[2,64,2048]{2,1,0:T(8,128)(2,1)S(1)} %copy-done.19), channel_id=1, source_target_pairs={{0,2},{2,4},{4,6},{6,0},{1,3},{3,5},{5,7},{7,1},{8,10},{10,12},{12... | collective-permute-start | bytes 1572872 | tf_op jit(solution)/shard_map/ppermute | solution.py:62
  292.6 23.9 %collective-permute-start.21 = (bf16[2,64,2048]{2,1,0:T(8,128)(2,1)}, bf16[2,64,2048]{2,1,0:T(8,128)(2,1)S(1)}, u32[]{:S(2)}, u32[]{:S(2)}) collective-permute-start(bf16[2,64,2048]{2,1,0:T(8,128)(2,1)} %get-tuple-element.72), channel_id=1, source_target_pairs={{0,4},{2,6},{4,0},{6,2},{1,5},{3,7},{5,1},{7,3},{8,12},{10,14},{12... | collective-permute-start | bytes 1572872 | tf_op jit(solution)/shard_map/ppermute | solution.py:62
  293.1 25.1 %collective-permute-start.22 = (bf16[2,64,2048]{2,1,0:T(8,128)(2,1)}, bf16[2,64,2048]{2,1,0:T(8,128)(2,1)S(1)}, u32[]{:S(2)}, u32[]{:S(2)}) collective-permute-start(bf16[2,64,2048]{2,1,0:T(8,128)(2,1)} %get-tuple-element.73), channel_id=1, source_target_pairs={{0,6},{2,0},{4,2},{6,4},{1,7},{3,1},{5,3},{7,5},{8,14},{10,8},{12,... | collective-permute-start | bytes 1572872 | tf_op jit(solution)/shard_map/ppermute | solution.py:62
  306.1 18.7 %collective-permute-start.18 = (bf16[4,2,64,2048]{3,2,1,0:T(8,128)(2,1)}, bf16[4,2,64,2048]{3,2,1,0:T(8,128)(2,1)}, u32[]{:S(2)}, u32[]{:S(2)}) collective-permute-start(bf16[4,2,64,2048]{3,2,1,0:T(8,128)(2,1)} %bitcast.217), channel_id=1, source_target_pairs={{0,1},{1,0},{2,3},{3,2},{4,5},{5,4},{6,7},{7,6},{8,9},{9,8},{10,11... | collective-permute-start | bytes 6291464 | tf_op jit(solution)/shard_map/ppermute | solution.py:43
  322.8 22.6 %collective-permute-start.24 = (bf16[2,64,2048]{2,1,0:T(8,128)(2,1)S(1)}, bf16[2,64,2048]{2,1,0:T(8,128)(2,1)S(1)}, u32[]{:S(2)}, u32[]{:S(2)}) collective-permute-start(bf16[2,64,2048]{2,1,0:T(8,128)(2,1)S(1)} %fusion.38), channel_id=1, source_target_pairs={{4,0},{6,2},{0,4},{2,6},{5,1},{7,3},{1,5},{3,7},{12,8},{14,10},{8,... | collective-permute-start | bytes 1572872 | tf_op jit(solution)/shard_map/ppermute | solution.py:49
  323.1 23.7 %collective-permute-start.23 = (bf16[2,64,2048]{2,1,0:T(8,128)(2,1)S(1)}, bf16[2,64,2048]{2,1,0:T(8,128)(2,1)}, u32[]{:S(2)}, u32[]{:S(2)}) collective-permute-start(bf16[2,64,2048]{2,1,0:T(8,128)(2,1)S(1)} %fusion.38), channel_id=1, source_target_pairs={{2,0},{4,2},{6,4},{0,6},{3,1},{5,3},{7,5},{1,7},{10,8},{12,10},{14... | collective-permute-start | bytes 1572872 | tf_op jit(solution)/shard_map/ppermute | solution.py:49
  351.7 40.1 %all-to-all-start = ((bf16[4,2,64,2048]{3,2,1,0:T(8,128)(2,1)}), bf16[4,2,64,2048]{3,2,1,0:T(8,128)(2,1)S(1)}, u32[]{:S(2)}, u32[]{:S(2)}) async-start(bf16[4,2,64,2048]{3,2,1,0:T(8,128)(2,1)} %add_cores_placed.2.refs_0_.token_ref), calls=%async_computation | async-start | bytes 4194304 | tf_op jit(solution)/shard_map/all_to_all | solution.py:481
  356.1 150.0 %all-gather.11.cloned.1.call-start = ((), (), s32[]{:S(2)}) async-start(), calls=%async_computation.5 | async-start | bytes 10616832 | tf_op jit(solution)/shard_map/all_gather | solution.py:1029
  389.3 18.8 %collective-permute-start.27 = (bf16[4,2,64,2048]{3,2,1,0:T(8,128)(2,1)}, bf16[4,2,64,2048]{3,2,1,0:T(8,128)(2,1)}, u32[]{:S(2)}, u32[]{:S(2)}) collective-permute-start(bf16[4,2,64,2048]{3,2,1,0:T(8,128)(2,1)} %bitcast.216), channel_id=1, source_target_pairs={{0,1},{1,0},{2,3},{3,2},{4,5},{5,4},{6,7},{7,6},{8,9},{9,8},{10,11... | collective-permute-start | bytes 6291464 | tf_op jit(solution)/shard_map/ppermute | solution.py:43
  412.9 59.4 %all-to-all-start.1 = ((bf16[4,2,64,2048]{3,2,1,0:T(8,128)(2,1)}), bf16[4,2,64,2048]{3,2,1,0:T(8,128)(2,1)S(1)}, u32[]{:S(2)}, u32[]{:S(2)}) async-start(bf16[4,2,64,2048]{3,2,1,0:T(8,128)(2,1)} %add_cores_placed.3.refs_0_), calls=%async_computation.1 | async-start | bytes 4194304 | tf_op jit(solution)/shard_map/all_to_all | solution.py:481
  417.1 15.6 %collective-permute-start.31 = (bf16[4,64,1280]{2,1,0:T(8,128)(2,1)}, bf16[4,64,1280]{2,1,0:T(8,128)(2,1)S(1)}, u32[]{:S(2)}, u32[]{:S(2)}) collective-permute-start(bf16[4,64,1280]{2,1,0:T(8,128)(2,1)} %get-tuple-element.88), channel_id=1, source_target_pairs={{24,0},{0,8},{8,16},{16,24},{56,32},{32,40},{40,48},{48,56},{88,64... | collective-permute-start | bytes 1966088 | tf_op jit(solution)/shard_map/ppermute | solution.py:91
  418.4 34.3 %collective-permute-start.29 = (bf16[4,80,1280]{2,1,0:T(8,128)(2,1)}, bf16[4,80,1280]{2,1,0:T(8,128)(2,1)S(1)}, u32[]{:S(2)}, u32[]{:S(2)}) collective-permute-start(bf16[4,80,1280]{2,1,0:T(8,128)(2,1)} %get-tuple-element.85), channel_id=1, source_target_pairs={{64,0},{72,8},{80,16},{88,24},{96,32},{104,40},{112,48},{120,56},{... | collective-permute-start | bytes 2457608 | tf_op jit(solution)/shard_map/ppermute | solution.py:91
  419.7 35.8 %collective-permute-start.30 = (bf16[4,80,1280]{2,1,0:T(8,128)(2,1)}, bf16[4,80,1280]{2,1,0:T(8,128)(2,1)}, u32[]{:S(2)}, u32[]{:S(2)}) collective-permute-start(bf16[4,80,1280]{2,1,0:T(8,128)(2,1)} %get-tuple-element.86), channel_id=1, source_target_pairs={{32,0},{40,8},{48,16},{56,24},{64,32},{72,40},{80,48},{88,56},{96,... | collective-permute-start | bytes 2457608 | tf_op jit(solution)/shard_map/ppermute | solution.py:91
  420.8 37.2 %collective-permute-start.28 = (bf16[4,80,1280]{2,1,0:T(8,128)(2,1)}, bf16[4,80,1280]{2,1,0:T(8,128)(2,1)}, u32[]{:S(2)}, u32[]{:S(2)}) collective-permute-start(bf16[4,80,1280]{2,1,0:T(8,128)(2,1)} %get-tuple-element.83.token_ref), channel_id=1, source_target_pairs={{96,0},{104,8},{112,16},{120,24},{0,32},{8,40},{16,48},{24,56},{32... | collective-permute-start | bytes 2457608 | tf_op jit(solution)/shard_map/ppermute | solution.py:91
  421.2 16.2 %collective-permute-start.32 = (bf16[4,64,1280]{2,1,0:T(8,128)(2,1)}, bf16[4,64,1280]{2,1,0:T(8,128)(2,1)S(1)}, u32[]{:S(2)}, u32[]{:S(2)}) collective-permute-start(bf16[4,64,1280]{2,1,0:T(8,128)(2,1)} %get-tuple-element.89), channel_id=1, source_target_pairs={{16,0},{24,8},{0,16},{8,24},{48,32},{56,40},{32,48},{40,56},{80,64... | collective-permute-start | bytes 1966088 | tf_op jit(solution)/shard_map/ppermute | solution.py:91
  432.8 20.0 %collective-permute-start.33 = (bf16[4,64,1280]{2,1,0:T(8,128)(2,1)}, bf16[4,64,1280]{2,1,0:T(8,128)(2,1)S(1)}, u32[]{:S(2)}, u32[]{:S(2)}) collective-permute-start(bf16[4,64,1280]{2,1,0:T(8,128)(2,1)} %get-tuple-element.90), channel_id=1, source_target_pairs={{8,0},{16,8},{24,16},{0,24},{40,32},{48,40},{56,48},{32,56},{72,64... | collective-permute-start | bytes 1966088 | tf_op jit(solution)/shard_map/ppermute | solution.py:91
  489.0 28.7 %collective-permute-start.44 = (bf16[32,2048]{1,0:T(8,128)(2,1)S(1)}, bf16[32,2048]{1,0:T(8,128)(2,1)S(1)}, u32[]{:S(2)}, u32[]{:S(2)}) collective-permute-start(bf16[32,2048]{1,0:T(8,128)(2,1)S(1)} %pad_maximum_fusion.12), channel_id=1, source_target_pairs={{0,0},{8,1},{16,2},{24,3},{32,4},{40,5},{48,6},{56,7},{64,8},{72,9... | collective-permute-start | bytes 393224 | tf_op jit(solution)/shard_map/ppermute | solution.py:1041
  496.9 22.9 %collective-permute-start.43 = (bf16[4,144,768]{2,1,0:T(8,128)(2,1)}, bf16[4,144,768]{2,1,0:T(8,128)(2,1)}, u32[]{:S(2)}, u32[]{:S(2)}) collective-permute-start(bf16[4,144,768]{2,1,0:T(8,128)(2,1)} %pad_maximum_fusion.8.mine_ref), channel_id=1, source_target_pairs={{0,1},{1,0},{2,3},{3,2},{4,5},{5,4},{6,7},{7,6},{8,9},{9,8},{10,11... | collective-permute-start | bytes 2654216 | tf_op jit(solution)/shard_map/ppermute | solution.py:43
  (51 other events, 460.2 us)
Sparse Core Ops, SparseCore 0:
  23.4 61.4 all-gather.6
  87.0 121.7 all-gather.8
  290.8 120.3 reduce-scatter.3
  413.0 68.6 all-gather.10
